TPU v7x, 32 devices: a whole 2x2x4 slice. The times are simulated.
32 devices in a mesh: batch: 8 (over y, x, core), seq: 4 (over z).
Axes of the slice: x: 2, y: 2, z: 4, core: 2. Of those that a mesh axis runs over, the one named last changes fastest.
Arguments:
- states: bfloat16 [64, 512, 768], P('batch', 'seq'), may hold values from -6 to 6
- lengths: int32 [64], P('batch'), may hold values from 32 to 512, as said below
- labels: int32 [64], P('batch'), may hold values from 0 to 2
- cotangent: bfloat16 [64, 512, 768], P('batch', 'seq'), may hold values from -6 to 6
- query_proj: bfloat16 [768, 768], replicated, may hold values from -0.21875 to 0.21875
- key_proj: bfloat16 [768, 768], replicated, may hold values from -0.21875 to 0.21875
- value_proj: bfloat16 [768, 768], replicated, may hold values from -0.21875 to 0.21875
- output_proj: bfloat16 [768, 768], replicated, may hold values from -0.625 to 0.625
- query_bias: bfloat16 [768], replicated, may hold values from -3 to 3
- value_bias: bfloat16 [768], replicated, may hold values from -1.1953125 to 1.1953125
- output_bias: bfloat16 [768], replicated, may hold values from -1.1953125 to 1.1953125
- first_gain: bfloat16 [768], replicated, may hold values from 0.5 to 1.5
- first_bias: bfloat16 [768], replicated, may hold values from -1.796875 to 1.796875
- inner_proj: bfloat16 [768, 3072], replicated, may hold values from -0.21875 to 0.21875
- inner_bias: bfloat16 [3072], replicated, may hold values from -3 to 3
- outer_proj: bfloat16 [3072, 768], replicated, may hold values from -0.109375 to 0.109375
- outer_bias: bfloat16 [768], replicated, may hold values from -1.1953125 to 1.1953125
- second_gain: bfloat16 [768], replicated, may hold values from 0.5 to 1.5
- second_bias: bfloat16 [768], replicated, may hold values from -1.796875 to 1.796875
- pool_proj: bfloat16 [768, 768], replicated, may hold values from -0.21875 to 0.21875
- pool_bias: bfloat16 [768], replicated, may hold values from -1.796875 to 1.796875
- class_proj: bfloat16 [768, 3], replicated, may hold values from -1 to 1
- class_bias: bfloat16 [3], replicated, may hold values from -3 to 3
Outputs:
- layer_out: bfloat16 [64, 512, 768], P('batch', 'seq')
- losses: float32 [64], P('batch')
- states_grad: bfloat16 [64, 512, 768], P('batch', 'seq')
- query_proj_grad: float32 [768, 768], replicated
- key_proj_grad: float32 [768, 768], replicated
- value_proj_grad: float32 [768, 768], replicated
- output_proj_grad: float32 [768, 768], replicated
- query_bias_grad: float32 [768], replicated
- value_bias_grad: float32 [768], replicated
- output_bias_grad: float32 [768], replicated
- first_gain_grad: float32 [768], replicated
- first_bias_grad: float32 [768], replicated
- inner_proj_grad: float32 [768, 3072], replicated
- inner_bias_grad: float32 [3072], replicated
- outer_proj_grad: float32 [3072, 768], replicated
- outer_bias_grad: float32 [768], replicated
- second_gain_grad: float32 [768], replicated
- second_bias_grad: float32 [768], replicated
- pool_proj_grad: float32 [768, 768], replicated
- pool_bias_grad: float32 [768], replicated
- class_proj_grad: float32 [768, 3], replicated
- class_bias_grad: float32 [3], replicated
Inputs may be any that keep to these rules, and one draw needn't show every extreme that they name: `lengths`: in each aligned group of 8 sequences (those of one index of batch) one sequence, drawn from the seed, has exactly 512 tokens.
All inputs are finite; a program needn't handle non-finite values.
Results may differ from a plain program's by a relative error of at most 0.015.
Values may be sent and summed in bfloat16 or wider, within the bound.
A program may use at most 192 MiB of HBM per device.

v0:
```python
import jax
import jax.numpy as jnp
from jax import lax
from jax.sharding import PartitionSpec as P

HEADS = 12
HEAD_DIM = 64


highest = lax.Precision.HIGHEST
norm_eps = 1e-06
masked_fill = -1e30
inv_root_two = 0.7071067811865476
inv_root_tau = 0.3989422804014327


def passed_along(block, axis, distance):
    devices = range(lax.axis_size(axis))
    route = [((i - distance) % len(devices), i) for i in devices]
    return lax.ppermute(block, axis, route)


def spread(block, axis, owner):
    block = jnp.where(lax.axis_index(axis) == owner, block, jnp.zeros_like(block))
    return lax.psum(block, axis)


def project(left, right):
    return jnp.dot(left, right, preferred_element_type=jnp.float32)


def project_left(left, right):
    return jnp.einsum("ti,to->io", left, right, preferred_element_type=jnp.float32)


def project_right(left, right):
    return jnp.einsum("to,io->ti", left, right, preferred_element_type=jnp.float32)


def normalize(values, norm_gain, norm_bias):
    average = jnp.mean(values, axis=-1, keepdims=True)
    centered = values - average
    variance = jnp.mean(centered * centered, axis=-1, keepdims=True)
    inv_root = lax.rsqrt(variance + norm_eps)
    normed = centered * inv_root
    return (normed * norm_gain + norm_bias, normed, inv_root)


def normalize_back(upstream, normed, inv_root, norm_gain):
    gain_grad = jnp.sum(upstream * normed, axis=0)
    bias_grad = jnp.sum(upstream, axis=0)
    scaled = upstream * norm_gain
    centred_part = scaled - jnp.mean(scaled, axis=-1, keepdims=True)
    input_grad = inv_root * (
        centred_part - normed * jnp.mean(scaled * normed, axis=-1, keepdims=True)
    )
    return (input_grad, gain_grad, bias_grad)


def gelu_pair(expanded):
    cumulative = 0.5 * (1.0 + lax.erf(expanded * inv_root_two))
    density = jnp.exp(-0.5 * expanded * expanded) * inv_root_tau
    return (expanded * cumulative, cumulative + expanded * density)


def key_usable(start, key_count, seq_lengths):
    places = start + jnp.arange(key_count, dtype=jnp.int32)
    return (places[None, :] < seq_lengths[:, None])[:, None, None, :]


def initial_carry(seq_count, query_count):
    return (
        jnp.full((seq_count, HEADS, query_count), masked_fill, jnp.float32),
        jnp.zeros((seq_count, HEADS, query_count), jnp.float32),
        jnp.zeros((seq_count, HEADS, query_count, HEAD_DIM), jnp.float32),
    )


def split_heads(piece):
    key_block, value_block = piece
    seq_count, key_count = (key_block.shape[0], key_block.shape[1])
    return (
        key_block.reshape(seq_count, key_count, HEADS, HEAD_DIM),
        value_block.reshape(seq_count, key_count, HEADS, HEAD_DIM),
    )


def attend(carry, piece, start, query_heads, seq_lengths):
    run_max, run_total, accum = carry
    key_heads, value_heads = split_heads(piece)
    scores = jnp.einsum(
        "sqhd,skhd->shqk", query_heads, key_heads, preferred_element_type=jnp.float32
    ) * HEAD_DIM ** (-0.5)
    usable = key_usable(start, key_heads.shape[1], seq_lengths)
    masked = jnp.where(usable, scores, masked_fill)
    new_max = jnp.maximum(run_max, jnp.max(masked, axis=-1))
    weights_exp = jnp.where(usable, jnp.exp(masked - new_max[..., None]), 0.0)
    rescale = jnp.exp(run_max - new_max)
    new_total = run_total * rescale + jnp.sum(weights_exp, axis=-1)
    mixture = jnp.einsum(
        "shqk,skhd->shqd",
        weights_exp.astype(jnp.bfloat16),
        value_heads,
        preferred_element_type=jnp.float32,
    )
    return (new_max, new_total, accum * rescale[..., None] + mixture)


def finish(carry):
    run_max, run_total, accum = carry
    attended = jnp.transpose(accum / run_total[..., None], (0, 2, 1, 3))
    return (attended, run_max + jnp.log(run_total))


def attend_back(piece, start, query_heads, grad_heads, log_total, delta, seq_lengths):
    key_heads, value_heads = split_heads(piece)
    seq_count, key_count = (key_heads.shape[0], key_heads.shape[1])
    scaling = HEAD_DIM ** (-0.5)
    scores = (
        jnp.einsum("sqhd,skhd->shqk", query_heads, key_heads, preferred_element_type=jnp.float32)
        * scaling
    )
    usable = key_usable(start, key_count, seq_lengths)
    masked = jnp.where(usable, scores, masked_fill)
    probs = jnp.where(usable, jnp.exp(masked - log_total[..., None]), 0.0)
    prob_grad = jnp.einsum(
        "sqhd,skhd->shqk", grad_heads, value_heads, preferred_element_type=jnp.float32
    )
    score_grad = (probs * (prob_grad - delta[..., None])).astype(jnp.bfloat16)
    value_grad = jnp.einsum(
        "shqk,sqhd->skhd",
        probs.astype(jnp.bfloat16),
        grad_heads,
        preferred_element_type=jnp.float32,
    )
    query_grad = (
        jnp.einsum("shqk,skhd->sqhd", score_grad, key_heads, preferred_element_type=jnp.float32)
        * scaling
    )
    key_grad = (
        jnp.einsum("shqk,sqhd->skhd", score_grad, query_heads, preferred_element_type=jnp.float32)
        * scaling
    )
    return (
        query_grad,
        key_grad.reshape(seq_count, key_count, -1),
        value_grad.reshape(seq_count, key_count, -1),
    )


def local(
    states,
    lengths,
    labels,
    cotangent,
    query_proj,
    key_proj,
    value_proj,
    output_proj,
    query_bias,
    value_bias,
    output_bias,
    first_gain,
    first_bias,
    inner_proj,
    inner_bias,
    outer_proj,
    outer_bias,
    second_gain,
    second_bias,
    pool_proj,
    pool_bias,
    class_proj,
    class_bias,
):
    seq_count, block_len, width = states.shape
    cycle_size = lax.axis_size("seq")
    position = lax.axis_index("seq")
    token_count = seq_count * block_len
    token_rows = states.reshape(token_count, width)
    query_states = (
        (project(token_rows, query_proj) + query_bias)
        .astype(jnp.bfloat16)
        .reshape(seq_count, block_len, width)
    )
    key_states = (
        project(token_rows, key_proj).astype(jnp.bfloat16).reshape(seq_count, block_len, width)
    )
    value_states = (
        (project(token_rows, value_proj) + value_bias)
        .astype(jnp.bfloat16)
        .reshape(seq_count, block_len, width)
    )
    query_heads = query_states.reshape(seq_count, block_len, HEADS, HEAD_DIM)
    carry = initial_carry(seq_count, block_len)
    travel = (key_states, value_states)
    for turn_index in range(cycle_size):
        source = (position - turn_index) % cycle_size
        carry = attend(carry, travel, source * block_len, query_heads, lengths)
        if turn_index + 1 < cycle_size:
            travel = passed_along((travel[0], travel[1]), "seq", 1)
    attended, log_total = finish(carry)
    attended_low = attended.reshape(token_count, width).astype(jnp.bfloat16)
    attn_out = project(attended_low, output_proj) + output_bias
    first_out, first_normed, first_inv = normalize(
        token_rows.astype(jnp.float32) + attn_out,
        first_gain.astype(jnp.float32),
        first_bias.astype(jnp.float32),
    )
    first_low = first_out.astype(jnp.bfloat16)
    expanded = project(first_low, inner_proj) + inner_bias
    activated, gelu_slope = gelu_pair(expanded)
    hidden = activated.astype(jnp.bfloat16)
    projected = project(hidden, outer_proj) + outer_bias
    second_out, second_normed, second_inv = normalize(
        first_out + projected, second_gain.astype(jnp.float32), second_bias.astype(jnp.float32)
    )
    layer_out = second_out.astype(jnp.bfloat16).reshape(seq_count, block_len, width)
    cls_state = spread(layer_out[:, 0, :], "seq", 0).astype(jnp.float32)
    part_width = width // cycle_size
    column_start = position * part_width
    feature_index = jnp.arange(width, dtype=jnp.int32)
    own_columns = (feature_index >= column_start) & (feature_index < column_start + part_width)
    pool_full = pool_proj.astype(jnp.float32)
    class_full = class_proj.astype(jnp.float32)
    pooled = jnp.tanh(
        jnp.dot(cls_state, pool_full, precision=highest) + pool_bias.astype(jnp.float32)
    )
    logits = jnp.dot(pooled, class_full, precision=highest) + class_bias.astype(jnp.float32)
    logit_top = jnp.max(logits, axis=-1, keepdims=True)
    log_norm = logit_top + jnp.log(jnp.sum(jnp.exp(logits - logit_top), axis=-1, keepdims=True))
    chosen = (jnp.arange(class_proj.shape[1], dtype=jnp.int32)[None, :] == labels[:, None]).astype(
        jnp.float32
    )
    losses = log_norm[:, 0] - jnp.sum(chosen * logits, axis=-1)
    logit_grad = jnp.exp(logits - log_norm) - chosen
    is_owner = position == 0
    class_bias_grad = jnp.where(is_owner, jnp.sum(logit_grad, axis=0), 0.0)
    class_proj_grad = jnp.where(
        own_columns[:, None], jnp.dot(pooled.T, logit_grad, precision=highest), 0.0
    )
    pre_grad = jnp.dot(logit_grad, class_full.T, precision=highest) * (1.0 - pooled * pooled)
    pool_bias_grad = jnp.where(own_columns, jnp.sum(pre_grad, axis=0), 0.0)
    pool_proj_grad = jnp.where(
        own_columns[None, :], jnp.dot(cls_state.T, pre_grad, precision=highest), 0.0
    )
    cls_grad = jnp.dot(pre_grad, pool_full.T, precision=highest)
    out_grad = (
        cotangent.astype(jnp.float32)
        .at[:, 0, :]
        .add(jnp.where(is_owner, cls_grad, 0.0))
        .reshape(token_count, width)
    )
    second_z_grad, second_gain_grad, second_bias_grad = normalize_back(
        out_grad, second_normed, second_inv, second_gain.astype(jnp.float32)
    )
    projected_grad = second_z_grad.astype(jnp.bfloat16)
    outer_proj_grad = project_left(hidden, projected_grad)
    outer_bias_grad = jnp.sum(projected_grad.astype(jnp.float32), axis=0)
    expanded_grad = (project_right(projected_grad, outer_proj) * gelu_slope).astype(jnp.bfloat16)
    inner_proj_grad = project_left(first_low, expanded_grad)
    inner_bias_grad = jnp.sum(expanded_grad.astype(jnp.float32), axis=0)
    first_grad = second_z_grad + project_right(expanded_grad, inner_proj)
    first_z_grad, first_gain_grad, first_bias_grad = normalize_back(
        first_grad, first_normed, first_inv, first_gain.astype(jnp.float32)
    )
    attn_grad = first_z_grad.astype(jnp.bfloat16)
    output_proj_grad = project_left(attended_low, attn_grad)
    output_bias_grad = jnp.sum(attn_grad.astype(jnp.float32), axis=0)
    attended_grad = project_right(attn_grad, output_proj).astype(jnp.bfloat16)
    grad_heads = attended_grad.reshape(seq_count, block_len, HEADS, HEAD_DIM)
    delta = jnp.transpose(jnp.sum(grad_heads.astype(jnp.float32) * attended, axis=-1), (0, 2, 1))
    query_accum = jnp.zeros((seq_count, block_len, HEADS, HEAD_DIM), jnp.float32)
    travel = (key_states, value_states)
    moving = (
        jnp.zeros((seq_count, block_len, width), jnp.float32),
        jnp.zeros((seq_count, block_len, width), jnp.float32),
    )
    for turn_index in range(cycle_size):
        source = (position - turn_index) % cycle_size
        query_part, key_part, value_part = attend_back(
            travel, source * block_len, query_heads, grad_heads, log_total, delta, lengths
        )
        query_accum = query_accum + query_part
        moving = (
            passed_along((moving[0] + key_part).astype(jnp.bfloat16), "seq", 1).astype(jnp.float32),
            passed_along((moving[1] + value_part).astype(jnp.bfloat16), "seq", 1).astype(
                jnp.float32
            ),
        )
        if turn_index + 1 < cycle_size:
            travel = passed_along((travel[0], travel[1]), "seq", 1)
    query_grad = query_accum.reshape(seq_count, block_len, width).astype(jnp.bfloat16)
    key_grad = moving[0].astype(jnp.bfloat16)
    value_grad = moving[1].astype(jnp.bfloat16)
    query_rows = query_grad.reshape(token_count, width)
    key_rows = key_grad.reshape(token_count, width)
    value_rows = value_grad.reshape(token_count, width)
    query_proj_grad = project_left(token_rows, query_rows)
    query_bias_grad = jnp.sum(query_rows.astype(jnp.float32), axis=0)
    key_proj_grad = project_left(token_rows, key_rows)
    value_proj_grad = project_left(token_rows, value_rows)
    value_bias_grad = jnp.sum(value_rows.astype(jnp.float32), axis=0)
    states_grad = (
        (
            first_z_grad
            + project_right(query_rows, query_proj)
            + project_right(key_rows, key_proj)
            + project_right(value_rows, value_proj)
        )
        .astype(jnp.bfloat16)
        .reshape(seq_count, block_len, width)
    )
    (
        query_proj_grad,
        key_proj_grad,
        value_proj_grad,
        output_proj_grad,
        query_bias_grad,
        value_bias_grad,
        output_bias_grad,
        first_gain_grad,
        first_bias_grad,
        inner_proj_grad,
        inner_bias_grad,
        outer_proj_grad,
        outer_bias_grad,
        second_gain_grad,
        second_bias_grad,
        pool_proj_grad,
        pool_bias_grad,
        class_proj_grad,
        class_bias_grad,
    ) = lax.psum(
        (
            query_proj_grad,
            key_proj_grad,
            value_proj_grad,
            output_proj_grad,
            query_bias_grad,
            value_bias_grad,
            output_bias_grad,
            first_gain_grad,
            first_bias_grad,
            inner_proj_grad,
            inner_bias_grad,
            outer_proj_grad,
            outer_bias_grad,
            second_gain_grad,
            second_bias_grad,
            pool_proj_grad,
            pool_bias_grad,
            class_proj_grad,
            class_bias_grad,
        ),
        ("batch", "seq"),
    )
    return (
        layer_out,
        losses,
        states_grad,
        query_proj_grad,
        key_proj_grad,
        value_proj_grad,
        output_proj_grad,
        query_bias_grad,
        value_bias_grad,
        output_bias_grad,
        first_gain_grad,
        first_bias_grad,
        inner_proj_grad,
        inner_bias_grad,
        outer_proj_grad,
        outer_bias_grad,
        second_gain_grad,
        second_bias_grad,
        pool_proj_grad,
        pool_bias_grad,
        class_proj_grad,
        class_bias_grad,
    )


def solution(mesh):
    in_specs = (
        P("batch", "seq", None),
        P("batch"),
        P("batch"),
        P("batch", "seq", None),
        P(),
        P(),
        P(),
        P(),
        P(),
        P(),
        P(),
        P(),
        P(),
        P(),
        P(),
        P(),
        P(),
        P(),
        P(),
        P(),
        P(),
        P(),
        P(),
    )
    out_specs = (
        P("batch", "seq", None),
        P("batch"),
        P("batch", "seq", None),
        P(),
        P(),
        P(),
        P(),
        P(),
        P(),
        P(),
        P(),
        P(),
        P(),
        P(),
        P(),
        P(),
        P(),
        P(),
        P(),
        P(),
        P(),
        P(),
    )
    return jax.shard_map(local, mesh=mesh, in_specs=in_specs, out_specs=out_specs, check_vma=False)
```

profile of v0, /device:TPU:1, one launch (start us, length us, event | category | flops | bytes accessed | tf_op | source)
XLA Modules:
  0.0 1139.5 jit_solution(2963142738889957408)
XLA Ops:
  16.6 32.4 %collective-permute-done = bf16[8,128,768]{2,1,0:T(8,128)(2,1)} collective-permute-done((bf16[8,128,768]{2,1,0:T(8,128)(2,1)S(1)}, bf16[8,128,768]{2,1,0:T(8,128)(2,1)}, u32[]{:S(2)}, u32[]{:S(2)}) %collective-permute-start) | collective-permute-done | bytes 1572896 | tf_op jit(solution)/shard_map/ppermute | solution.py:20
  64.1 18.6 %collective-permute-done.1 = bf16[8,128,768]{2,1,0:T(8,128)(2,1)} collective-permute-done((bf16[8,128,768]{2,1,0:T(8,128)(2,1)}, bf16[8,128,768]{2,1,0:T(8,128)(2,1)}, u32[]{:S(2)}, u32[]{:S(2)}) %collective-permute-start.1) | collective-permute-done | bytes 1572896 | tf_op jit(solution)/shard_map/ppermute | solution.py:20
  86.7 29.7 %collective-permute-done.2 = bf16[8,128,768]{2,1,0:T(8,128)(2,1)} collective-permute-done((bf16[8,128,768]{2,1,0:T(8,128)(2,1)}, bf16[8,128,768]{2,1,0:T(8,128)(2,1)}, u32[]{:S(2)}, u32[]{:S(2)}) %collective-permute-start.2) | collective-permute-done | bytes 1572896 | tf_op jit(solution)/shard_map/ppermute | solution.py:20
  133.7 16.4 %collective-permute-done.3 = bf16[8,128,768]{2,1,0:T(8,128)(2,1)} collective-permute-done((bf16[8,128,768]{2,1,0:T(8,128)(2,1)}, bf16[8,128,768]{2,1,0:T(8,128)(2,1)}, u32[]{:S(2)}, u32[]{:S(2)}) %collective-permute-start.3) | collective-permute-done | bytes 1572896 | tf_op jit(solution)/shard_map/ppermute | solution.py:20
  158.7 25.1 %collective-permute-done.4 = bf16[8,128,768]{2,1,0:T(8,128)(2,1)} collective-permute-done((bf16[8,128,768]{2,1,0:T(8,128)(2,1)}, bf16[8,128,768]{2,1,0:T(8,128)(2,1)}, u32[]{:S(2)}, u32[]{:S(2)}) %collective-permute-start.4) | collective-permute-done | bytes 1572896 | tf_op jit(solution)/shard_map/ppermute | solution.py:20
  189.7 8.6 fusion.34
  220.5 10.4 fusion.180
  235.2 9.4 multiply_convert_fusion
  252.8 13.3 %psum.140 = bf16[8,768]{1,0:T(8,128)(2,1)S(1)} all-reduce(bf16[8,768]{1,0:T(8,128)(2,1)S(1)} %fusion.139), channel_id=1, replica_groups=mesh['batch'=8,'seq'=4] {'seq'}, use_global_device_ids=true, to_apply=%region_12.13 | all-reduce | flops 6144 | bytes 24576 | tf_op jit(solution)/shard_map/psum | solution.py:25
  281.8 13.0 %convert_reduce_fusion = (f32[3072]{0:T(1024)S(1)}, bf16[1024,3072]{1,0:T(8,128)(2,1)S(1)}) fusion(f32[1024,3072]{1,0:T(8,128)} %get-tuple-element.203, f32[3072]{0:T(1024)S(1)} %convert_element_type.227, bf16[3072,768]{1,0:T(8,128)(2,1)} %param.40, f32[1024,768]{1,0:T(8,128)S(1)} %get-tuple-element.174), kind=kOutput, calls=%fused_computation.7 | convolution fusion | flops 4873516032 | bytes 26763264 | tf_op jit(solution)/shard_map/to,io->ti/dot_general | solution.py:37
  318.0 7.0 fusion.26
  346.2 10.3 fusion.143
  373.1 21.0 %collective-permute-done.10 = bf16[8,128,768]{1,2,0:T(8,128)(2,1)} collective-permute-done((bf16[8,128,768]{1,2,0:T(8,128)(2,1)}, bf16[8,128,768]{1,2,0:T(8,128)(2,1)}, u32[]{:S(2)}, u32[]{:S(2)}) %collective-permute-start.10) | collective-permute-done | bytes 1572896 | tf_op jit(solution)/shard_map/ppermute | solution.py:20
  396.8 31.0 %collective-permute-done.6 = bf16[8,128,768]{1,2,0:T(8,128)(2,1)} collective-permute-done((bf16[8,128,768]{1,2,0:T(8,128)(2,1)}, bf16[8,128,768]{1,2,0:T(8,128)(2,1)}, u32[]{:S(2)}, u32[]{:S(2)}) %collective-permute-start.6) | collective-permute-done | bytes 1572896 | tf_op jit(solution)/shard_map/ppermute | solution.py:20
  438.5 22.9 %collective-permute-done.11 = bf16[8,128,768]{1,2,0:T(8,128)(2,1)S(1)} collective-permute-done((bf16[8,128,768]{1,2,0:T(8,128)(2,1)S(1)}, bf16[8,128,768]{1,2,0:T(8,128)(2,1)S(1)}, u32[]{:S(2)}, u32[]{:S(2)}) %collective-permute-start.11) | collective-permute-done | bytes 1572896 | tf_op jit(solution)/shard_map/ppermute | solution.py:20
  461.8 33.4 %collective-permute-done.7 = bf16[8,128,768]{1,2,0:T(8,128)(2,1)} collective-permute-done((bf16[8,128,768]{1,2,0:T(8,128)(2,1)}, bf16[8,128,768]{1,2,0:T(8,128)(2,1)}, u32[]{:S(2)}, u32[]{:S(2)}) %collective-permute-start.7) | collective-permute-done | bytes 1572896 | tf_op jit(solution)/shard_map/ppermute | solution.py:20
  505.1 23.7 %collective-permute-done.12 = bf16[8,128,768]{1,2,0:T(8,128)(2,1)S(1)} collective-permute-done((bf16[8,128,768]{1,2,0:T(8,128)(2,1)S(1)}, bf16[8,128,768]{1,2,0:T(8,128)(2,1)S(1)}, u32[]{:S(2)}, u32[]{:S(2)}) %collective-permute-start.12) | collective-permute-done | bytes 1572896 | tf_op jit(solution)/shard_map/ppermute | solution.py:20
  529.4 33.1 %collective-permute-done.8 = bf16[8,128,768]{1,2,0:T(8,128)(2,1)S(1)} collective-permute-done((bf16[8,128,768]{1,2,0:T(8,128)(2,1)S(1)}, bf16[8,128,768]{1,2,0:T(8,128)(2,1)S(1)}, u32[]{:S(2)}, u32[]{:S(2)}) %collective-permute-start.8) | collective-permute-done | bytes 1572896 | tf_op jit(solution)/shard_map/ppermute | solution.py:20
  563.0 8.5 fusion.172
  571.5 24.7 %collective-permute-done.13 = bf16[8,128,768]{1,2,0:T(8,128)(2,1)S(1)} collective-permute-done((bf16[8,128,768]{1,2,0:T(8,128)(2,1)S(1)}, bf16[8,128,768]{1,2,0:T(8,128)(2,1)S(1)}, u32[]{:S(2)}, u32[]{:S(2)}) %collective-permute-start.13) | collective-permute-done | bytes 1572896 | tf_op jit(solution)/shard_map/ppermute | solution.py:20
  599.0 30.9 %collective-permute-done.9 = bf16[8,128,768]{1,2,0:T(8,128)(2,1)S(1)} collective-permute-done((bf16[8,128,768]{1,2,0:T(8,128)(2,1)S(1)}, bf16[8,128,768]{1,2,0:T(8,128)(2,1)S(1)}, u32[]{:S(2)}, u32[]{:S(2)}) %collective-permute-start.9) | collective-permute-done | bytes 1572896 | tf_op jit(solution)/shard_map/ppermute | solution.py:20
  644.9 47.5 %all-reduce = (f32[768]{0:T(1024)}, f32[768]{0:T(1024)}, f32[768]{0:T(1024)}, f32[768]{0:T(1024)}, f32[768]{0:T(1024)}, /*index=5*/f32[3072]{0:T(1024)}, f32[768...) all-reduce(f32[768]{0:T(1024)S(1)} %reduce_sum.264, ...), channel_id=1, replica_groups=mesh['batch'=8,'seq'=4] {'batch','seq'}, use_global_device_ids=true, to_apply=%region_26.27 | all-reduce | flops 12291 | bytes 98328 | tf_op jit(solution)/shard_map/psum | solution.py:334
  700.7 406.6 %all-reduce.4.cloned.1.call-done = (f32[768,768]{0,1:T(8,128)}, f32[768,768]{0,1:T(8,128)}, f32[768,768]{0,1:T(8,128)}, f32[768,768]{1,0:T(8,128)}, f32[768,3072...) async-done(((f32[768,768]{0,1:T(8,128)}, f32[768,768]{0,1:T(8,128)}, f32[768,768]{0,1:T(8,128)}, f32[768,768]{1,0:T(8,128)}, f32[768,3072]{1,0:T(8,128)}, ...) | async-done | bytes 30670864 | tf_op jit(solution)/shard_map/psum | solution.py:334
  1117.0 9.3 copy.439
  (341 shorter events, 236.8 us)
Async XLA Ops:
  7.2 225.0 %copy-start = (bf16[768,768]{1,0:T(8,128)(2,1)S(1)}, bf16[768,768]{1,0:T(8,128)(2,1)}, u32[]{:S(2)}) copy-start(bf16[768,768]{1,0:T(8,128)(2,1)} %param.32) | copy-start | bytes 3538948
  7.2 1100.1 %all-reduce.4.cloned.1.call-start = ((), (), s32[]{:S(2)}) async-start(), calls=%async_computation | async-start | bytes 61341696 | tf_op jit(solution)/shard_map/psum | solution.py:334
  10.6 38.4 %collective-permute-start = (bf16[8,128,768]{2,1,0:T(8,128)(2,1)S(1)}, bf16[8,128,768]{2,1,0:T(8,128)(2,1)}, u32[]{:S(2)}, u32[]{:S(2)}) collective-permute-start(bf16[8,128,768]{2,1,0:T(8,128)(2,1)S(1)} %bitcast.336), channel_id=1, source_target_pairs={{3,0},{0,1},{1,2},{2,3},{7,4},{4,5},{5,6},{6,7},{11,8},{8,9},{9,10... | collective-permute-start | bytes 4718600 | tf_op jit(solution)/shard_map/ppermute | solution.py:20
  15.3 67.4 %collective-permute-start.1 = (bf16[8,128,768]{2,1,0:T(8,128)(2,1)}, bf16[8,128,768]{2,1,0:T(8,128)(2,1)}, u32[]{:S(2)}, u32[]{:S(2)}) collective-permute-start(bf16[8,128,768]{2,1,0:T(8,128)(2,1)} %bitcast.6), channel_id=1, source_target_pairs={{3,0},{0,1},{1,2},{2,3},{7,4},{4,5},{5,6},{6,7},{11,8},{8,9},{9,10... | collective-permute-start | bytes 4718600 | tf_op jit(solution)/shard_map/ppermute | solution.py:20
  49.0 67.4 %collective-permute-start.2 = (bf16[8,128,768]{2,1,0:T(8,128)(2,1)}, bf16[8,128,768]{2,1,0:T(8,128)(2,1)}, u32[]{:S(2)}, u32[]{:S(2)}) collective-permute-start(bf16[8,128,768]{2,1,0:T(8,128)(2,1)} %collective-permute-done), channel_id=1, source_target_pairs={{3,0},{0,1},{1,2},{2,3},{7,4},{4,5},{5,6},{6,7},{11,8},{8,9},{9,10... | collective-permute-start | bytes 4718600 | tf_op jit(solution)/shard_map/ppermute | solution.py:20
  63.3 53.1 %copy-start.62 = (s32[8]{0:T(128)S(1)}, s32[8]{0:T(128)}, u32[]{:S(2)}) copy-start(s32[8]{0:T(128)} %param.26) | copy-start | bytes 100
  63.5 53.0 %copy-start.19 = (bf16[96,8,8,128]{3,2,1,0:T(8,128)(2,1)S(1)}, bf16[96,8,8,128]{3,2,1,0:T(8,128)(2,1)}, u32[]{:S(2)}) copy-start(bf16[96,8,8,128]{3,2,1,0:T(8,128)(2,1)} %copy.356) | copy-start | bytes 4718596
  82.7 67.4 %collective-permute-start.3 = (bf16[8,128,768]{2,1,0:T(8,128)(2,1)}, bf16[8,128,768]{2,1,0:T(8,128)(2,1)}, u32[]{:S(2)}, u32[]{:S(2)}) collective-permute-start(bf16[8,128,768]{2,1,0:T(8,128)(2,1)} %collective-permute-done.1), channel_id=1, source_target_pairs={{3,0},{0,1},{1,2},{2,3},{7,4},{4,5},{5,6},{6,7},{11,8},{8,9},{9,10... | collective-permute-start | bytes 4718600 | tf_op jit(solution)/shard_map/ppermute | solution.py:20
  116.4 67.4 %collective-permute-start.4 = (bf16[8,128,768]{2,1,0:T(8,128)(2,1)}, bf16[8,128,768]{2,1,0:T(8,128)(2,1)}, u32[]{:S(2)}, u32[]{:S(2)}) collective-permute-start(bf16[8,128,768]{2,1,0:T(8,128)(2,1)} %collective-permute-done.2), channel_id=1, source_target_pairs={{3,0},{0,1},{1,2},{2,3},{7,4},{4,5},{5,6},{6,7},{11,8},{8,9},{9,10... | collective-permute-start | bytes 4718600 | tf_op jit(solution)/shard_map/ppermute | solution.py:20
  152.7 64.8 %collective-permute-start.5 = (bf16[8,128,768]{2,1,0:T(8,128)(2,1)}, bf16[8,128,768]{2,1,0:T(8,128)(2,1)}, u32[]{:S(2)}, u32[]{:S(2)}) collective-permute-start(bf16[8,128,768]{2,1,0:T(8,128)(2,1)} %collective-permute-done.3), channel_id=1, source_target_pairs={{3,0},{0,1},{1,2},{2,3},{7,4},{4,5},{5,6},{6,7},{11,8},{8,9},{9,10... | collective-permute-start | bytes 4718600 | tf_op jit(solution)/shard_map/ppermute | solution.py:20
  361.5 32.6 %collective-permute-start.10 = (bf16[8,128,768]{1,2,0:T(8,128)(2,1)}, bf16[8,128,768]{1,2,0:T(8,128)(2,1)}, u32[]{:S(2)}, u32[]{:S(2)}) collective-permute-start(bf16[8,128,768]{1,2,0:T(8,128)(2,1)} %bitcast.38), channel_id=1, source_target_pairs={{3,0},{0,1},{1,2},{2,3},{7,4},{4,5},{5,6},{6,7},{11,8},{8,9},{9,10... | collective-permute-start | bytes 4718600 | tf_op jit(solution)/shard_map/ppermute | solution.py:20
  365.8 61.9 %collective-permute-start.6 = (bf16[8,128,768]{1,2,0:T(8,128)(2,1)}, bf16[8,128,768]{1,2,0:T(8,128)(2,1)}, u32[]{:S(2)}, u32[]{:S(2)}) collective-permute-start(bf16[8,128,768]{1,2,0:T(8,128)(2,1)} %bitcast.29), channel_id=1, source_target_pairs={{3,0},{0,1},{1,2},{2,3},{7,4},{4,5},{5,6},{6,7},{11,8},{8,9},{9,10... | collective-permute-start | bytes 4718600 | tf_op jit(solution)/shard_map/ppermute | solution.py:20
  373.1 57.8 %copy-start.22 = (bf16[8,12,64,128]{3,2,1,0:T(8,128)(2,1)}, bf16[8,12,64,128]{3,2,1,0:T(8,128)(2,1)S(1)}, u32[]{:S(2)}) copy-start(bf16[8,12,64,128]{3,2,1,0:T(8,128)(2,1)S(1)} %get-tuple-element.210) | copy-start | bytes 4718596
  373.1 54.7 %copy-start.13 = (f32[8,12,64,128]{3,2,1,0:T(8,128)S(1)}, f32[8,12,64,128]{3,2,1,0:T(8,128)}, u32[]{:S(2)}) copy-start(f32[8,12,64,128]{3,2,1,0:T(8,128)} %convolution_multiply_fusion.2) | copy-start | bytes 9437188
  396.8 64.6 %collective-permute-start.11 = (bf16[8,128,768]{1,2,0:T(8,128)(2,1)S(1)}, bf16[8,128,768]{1,2,0:T(8,128)(2,1)S(1)}, u32[]{:S(2)}, u32[]{:S(2)}) collective-permute-start(bf16[8,128,768]{1,2,0:T(8,128)(2,1)S(1)} %fusion.40), channel_id=1, source_target_pairs={{3,0},{0,1},{1,2},{2,3},{7,4},{4,5},{5,6},{6,7},{11,8},{8,9},{9,10... | collective-permute-start | bytes 4718600 | tf_op jit(solution)/shard_map/ppermute | solution.py:20
  430.9 64.3 %collective-permute-start.7 = (bf16[8,128,768]{1,2,0:T(8,128)(2,1)}, bf16[8,128,768]{1,2,0:T(8,128)(2,1)}, u32[]{:S(2)}, u32[]{:S(2)}) collective-permute-start(bf16[8,128,768]{1,2,0:T(8,128)(2,1)} %fusion.43), channel_id=1, source_target_pairs={{3,0},{0,1},{1,2},{2,3},{7,4},{4,5},{5,6},{6,7},{11,8},{8,9},{9,10... | collective-permute-start | bytes 4718600 | tf_op jit(solution)/shard_map/ppermute | solution.py:20
  461.8 38.0 %copy-start.15 = (f32[1024,768]{1,0:T(8,128)S(1)}, f32[1024,768]{1,0:T(8,128)}, u32[]{:S(2)}) copy-start(f32[1024,768]{1,0:T(8,128)} %copy-done.14) | copy-start | bytes 9437188
  461.8 38.0 %copy-start.42 = (bf16[8,128,12,64]{1,0,3,2:T(8,128)(2,1)S(1)}, bf16[8,128,12,64]{1,0,3,2:T(8,128)(2,1)}, u32[]{:S(2)}) copy-start(bf16[8,128,12,64]{1,0,3,2:T(8,128)(2,1)} %copy-done.41) | copy-start | bytes 4718596
  461.8 67.0 %collective-permute-start.12 = (bf16[8,128,768]{1,2,0:T(8,128)(2,1)S(1)}, bf16[8,128,768]{1,2,0:T(8,128)(2,1)S(1)}, u32[]{:S(2)}, u32[]{:S(2)}) collective-permute-start(bf16[8,128,768]{1,2,0:T(8,128)(2,1)S(1)} %fusion.39), channel_id=1, source_target_pairs={{3,0},{0,1},{1,2},{2,3},{7,4},{4,5},{5,6},{6,7},{11,8},{8,9},{9,10... | collective-permute-start | bytes 4718600 | tf_op jit(solution)/shard_map/ppermute | solution.py:20
  497.1 65.4 %collective-permute-start.8 = (bf16[8,128,768]{1,2,0:T(8,128)(2,1)S(1)}, bf16[8,128,768]{1,2,0:T(8,128)(2,1)S(1)}, u32[]{:S(2)}, u32[]{:S(2)}) collective-permute-start(bf16[8,128,768]{1,2,0:T(8,128)(2,1)S(1)} %fusion.42), channel_id=1, source_target_pairs={{3,0},{0,1},{1,2},{2,3},{7,4},{4,5},{5,6},{6,7},{11,8},{8,9},{9,10... | collective-permute-start | bytes 4718600 | tf_op jit(solution)/shard_map/ppermute | solution.py:20
  499.7 63.2 %slice-start.13 = ((s8[6291456]{0:T(1024)(128)(4,1)}), s8[4194304]{0:T(1024)(128)(4,1)S(1)}, s32[]{:S(2)}) async-start(s8[6291456]{0:T(1024)(128)(4,1)} %bitcast.302), calls=%async_computation.14 | async-start | bytes 8388608
  502.5 60.4 %slice-start.14 = ((s8[6291456]{0:T(1024)(128)(4,1)}), s8[2097152]{0:T(1024)(128)(4,1)S(1)}, s32[]{:S(2)}) async-start(s8[6291456]{0:T(1024)(128)(4,1)} %bitcast.302), calls=%async_computation.15 | async-start | bytes 4194304
  529.2 67.0 %collective-permute-start.13 = (bf16[8,128,768]{1,2,0:T(8,128)(2,1)S(1)}, bf16[8,128,768]{1,2,0:T(8,128)(2,1)S(1)}, u32[]{:S(2)}, u32[]{:S(2)}) collective-permute-start(bf16[8,128,768]{1,2,0:T(8,128)(2,1)S(1)} %fusion.38), channel_id=1, source_target_pairs={{3,0},{0,1},{1,2},{2,3},{7,4},{4,5},{5,6},{6,7},{11,8},{8,9},{9,10... | collective-permute-start | bytes 4718600 | tf_op jit(solution)/shard_map/ppermute | solution.py:20
  562.9 67.0 %collective-permute-start.9 = (bf16[8,128,768]{1,2,0:T(8,128)(2,1)S(1)}, bf16[8,128,768]{1,2,0:T(8,128)(2,1)S(1)}, u32[]{:S(2)}, u32[]{:S(2)}) collective-permute-start(bf16[8,128,768]{1,2,0:T(8,128)(2,1)S(1)} %fusion.41), channel_id=1, source_target_pairs={{3,0},{0,1},{1,2},{2,3},{7,4},{4,5},{5,6},{6,7},{11,8},{8,9},{9,10... | collective-permute-start | bytes 4718600 | tf_op jit(solution)/shard_map/ppermute | solution.py:20
  (86 other events, 645.8 us)
Sparse Core Ops, SparseCore 0:
  634.0 473.2 all-reduce.3
where the time goes:
time: 1150 us; the launch traced here: 1140 us
  waiting for transfers between devices  751 us (65%)
  matrix products  195 us (17%)
  local copies, waits for them, and re-layouts  79.2 us (7%)
  blocking collectives  60.8 us (5%)
  other arithmetic  33.3 us (3%)
  between operations  15.9 us (1%)
    psum x1, waiting for transfers between devices, local(): lax.psum((query_proj_grad, key_proj_grad, value_proj_grad, output_proj_gr...  407 us
    ppermute x14, waiting for transfers between devices, passed_along(): return lax.ppermute(block, axis, route)  344 us
    psum x1, blocking collectives, local(): lax.psum((query_proj_grad, key_proj_grad, value_proj_grad, output_proj_gr...  47.5 us
    unnamed x201, local copies, waits for them, and re-layouts  45.2 us
    dot_general x6, matrix products, project_right(): jnp.einsum('to,io->ti', left, right, preferred_element_type=jnp.float32)  31.1 us
    dot_general x6, matrix products, project_left(): jnp.einsum('ti,to->io', left, right, preferred_element_type=jnp.float32)  30 us
    dot_general x6, matrix products, project(): return jnp.dot(left, right, preferred_element_type=jnp.float32)  25.4 us
    dot_general x4, matrix products, attend(): jnp.einsum('shqk,skhd->shqd', weights_exp.astype(jnp.bfloat16), value_hea...  25.1 us
  transfers between devices with their start and end apart: 15, of which 15 were waited for; matrix products, arithmetic and copies ran while one was open for 12% of the time, Pallas kernels for 0%

commit v1 on v0

v1 whole, which is shorter than its diff:
```python
import functools

import jax
import jax.numpy as jnp
from jax import lax
from jax.experimental import pallas as pl
from jax.experimental.pallas import tpu as pltpu
from jax.sharding import PartitionSpec as P

HEADS = 12
HEAD_DIM = 64
WIDTH = 768
HALF = 384
CHUNK = 256
MESH = pl.DeviceIdType.MESH

bf16 = jnp.bfloat16
f32 = jnp.float32
highest = lax.Precision.HIGHEST
norm_eps = 1e-06
masked_fill = -1e30
inv_root_two = 0.7071067811865476
inv_root_tau = 0.3989422804014327


def pick(code, table):
    out = table[-1]
    for i in range(len(table) - 2, -1, -1):
        out = jnp.where(code == i, table[i], out)
    return out


def flipped(index, bit):
    return index + bit * (1 - 2 * ((index // bit) % 2))


def reduce_kernel(
    chunks, pattern, lags, g_ref, small_ref, out_ref, small_out,
    acc, res, r0, r1, r2, r3, r4, sgot,
    rs_send, rs_recv, ag_send, ag_recv, loc, sm_send, sm_recv,
):
    b = lax.axis_index("batch")
    z = lax.axis_index("seq")
    core = b % 2
    got = [r0, r1, r2, r3, r4]
    near_b = [flipped(b, 2), flipped(b, 4), b, b]
    near_z = [z, z, flipped(z, 1), flipped(z, 2)]
    mine = [(b // 2) % 2, (b // 4) % 2, z % 2, (z // 2) % 2]
    orders = {"x": (0, 1, 2, 3), "y": (1, 0, 2, 3)}
    period = len(pattern)

    def direction(c, level):
        code = c % period
        dirs = [orders[p][level] for p in pattern]
        return (
            pick(code, [near_b[d] for d in dirs]),
            pick(code, [near_z[d] for d in dirs]),
            pick(code, [mine[d] for d in dirs]),
        )

    core_partner = (flipped(b, 1), z)
    barrier = pltpu.get_barrier_semaphore()
    partners = [core_partner] + [(near_b[d], near_z[d]) for d in range(4)]
    for who in partners:
        pl.semaphore_signal(barrier, inc=1, device_id=who, device_id_type=MESH)
    pl.semaphore_wait(barrier, len(partners))

    def base(c, level):
        rows = 0
        size = CHUNK
        for l in range(level):
            size = size // 2
            rows = rows + direction(c, l)[2] * size
        return pl.multiple_of(rows, 16)

    def g_rows(c):
        return pl.ds(pl.multiple_of(c * CHUNK, CHUNK), CHUNK)

    my_cols = pl.ds(pl.multiple_of(core * HALF, HALF), HALF)
    other_cols = pl.ds(pl.multiple_of((1 - core) * HALF, HALF), HALF)

    def rs_copy(c, s):
        if s == 0:
            return pltpu.make_async_remote_copy(
                g_ref.at[g_rows(c), other_cols], r0.at[c], rs_send.at[0, c], rs_recv.at[0, c],
                device_id=core_partner, device_id_type=MESH,
            )
        size = CHUNK >> s
        nb, nz, m = direction(c, s - 1)
        start = pl.multiple_of(base(c, s - 1) + (1 - m) * size, 16)
        return pltpu.make_async_remote_copy(
            acc.at[c, pl.ds(start, size)], got[s].at[c], rs_send.at[s, c], rs_recv.at[s, c],
            device_id=(nb, nz), device_id_type=MESH,
        )

    def ag_copy(c, s):
        if s == 0:
            return pltpu.make_async_remote_copy(
                res.at[c], out_ref.at[g_rows(c), my_cols], ag_send.at[0, c], ag_recv.at[0, c],
                device_id=core_partner, device_id_type=MESH,
            )
        size = CHUNK >> s
        nb, nz, _ = direction(c, s - 1)
        start = base(c, s)
        return pltpu.make_async_remote_copy(
            res.at[c, pl.ds(start, size)], res.at[c, pl.ds(start, size)],
            ag_send.at[s, c], ag_recv.at[s, c], device_id=(nb, nz), device_id_type=MESH,
        )

    def loc_in(c):
        return pltpu.make_async_copy(g_ref.at[g_rows(c), my_cols], acc.at[c], loc.at[0, c])

    def loc_out(c):
        return pltpu.make_async_copy(res.at[c], out_ref.at[g_rows(c), my_cols], loc.at[1, c])

    def stage_first(c):
        rs_copy(c, 0).start()
        loc_in(c).start()

    def stage_scatter(s, c):
        rs_copy(c, s - 1).wait_recv()
        if s == 1:
            loc_in(c).wait()
        half = CHUNK >> s
        start = base(c, s - 1)
        m = direction(c, s - 1)[2]
        for which in (0, 1):
            off = pl.multiple_of(((1 - m) if which == 0 else m) * half, 16)
            rows = pl.ds(pl.multiple_of(start + off, 16), half)
            acc[c, rows] = acc[c, rows] + got[s - 1][c, pl.ds(off, half)]
            if which == 0:
                rs_copy(c, s).start()

    def stage_turn(c):
        rs_copy(c, 4).wait_recv()
        rows = pl.ds(base(c, 4), 16)
        res[c, rows] = acc[c, rows] + r4[c]
        ag_copy(c, 4).start()

    def stage_gather(s, c):
        ag_copy(c, s + 1).wait_recv()
        ag_copy(c, s).start()
        if s == 0:
            loc_out(c).start()

    def stage_last(c):
        ag_copy(c, 0).wait_recv()
        loc_out(c).wait()
        for s in range(5):
            rs_copy(c, s).wait_send()
            ag_copy(c, s).wait_send()

    stages = (
        [stage_first]
        + [functools.partial(stage_scatter, s) for s in (1, 2, 3, 4)]
        + [stage_turn]
        + [functools.partial(stage_gather, s) for s in (3, 2, 1, 0)]
        + [stage_last]
    )

    def small_copy(i):
        return pltpu.make_async_remote_copy(
            small_out, sgot.at[i], sm_send.at[i], sm_recv.at[i],
            device_id=partners[i], device_id_type=MESH,
        )

    small_out[...] = small_ref[...]

    def tick(t, carry):
        for i in range(len(partners) + 1):

            @pl.when(t == 3 * i)
            def _():
                if i > 0:
                    small_copy(i - 1).wait()
                    small_out[...] = small_out[...] + sgot[i - 1]
                if i < len(partners):
                    small_copy(i).start()

        for stage, lag in reversed(list(zip(stages, lags))):
            c = t - lag

            @pl.when((c >= 0) & (c < chunks))
            def _():
                stage(c)

        return carry

    lax.fori_loop(0, chunks + lags[-1], tick, 0)


def reduce_all(g, small):
    rows = g.shape[0]
    if lax.axis_size("batch") != 8 or lax.axis_size("seq") != 4:
        return lax.psum(g.astype(f32), ("batch", "seq")), lax.psum(small, ("batch", "seq"))
    chunks = rows // CHUNK
    dma = pltpu.SemaphoreType.DMA
    return pl.pallas_call(
        functools.partial(reduce_kernel, chunks, "xy", tuple(3 * i for i in range(11))),
        out_shape=(
            jax.ShapeDtypeStruct(g.shape, bf16),
            jax.ShapeDtypeStruct(small.shape, f32),
        ),
        in_specs=[pl.BlockSpec(memory_space=pl.ANY), pl.BlockSpec(memory_space=pltpu.VMEM)],
        out_specs=(pl.BlockSpec(memory_space=pl.ANY), pl.BlockSpec(memory_space=pltpu.VMEM)),
        scratch_shapes=[
            pltpu.VMEM((chunks, CHUNK, HALF), bf16),
            pltpu.VMEM((chunks, CHUNK, HALF), bf16),
            pltpu.VMEM((chunks, CHUNK, HALF), bf16),
            pltpu.VMEM((chunks, CHUNK // 2, HALF), bf16),
            pltpu.VMEM((chunks, CHUNK // 4, HALF), bf16),
            pltpu.VMEM((chunks, CHUNK // 8, HALF), bf16),
            pltpu.VMEM((chunks, CHUNK // 16, HALF), bf16),
            pltpu.VMEM((5,) + small.shape, f32),
            dma((5, chunks)),
            dma((5, chunks)),
            dma((5, chunks)),
            dma((5, chunks)),
            dma((2, chunks)),
            dma((5,)),
            dma((5,)),
        ],
        compiler_params=pltpu.CompilerParams(
            collective_id=0, has_side_effects=True, vmem_limit_bytes=56 * 2**20
        ),
    )(g, small)


def shifted(block, distance):
    count = lax.axis_size("seq")
    route = [(i, (i + distance) % count) for i in range(count)]
    return lax.ppermute(block, "seq", route)


def to_sequences(block):
    count = lax.axis_size("seq")
    position = lax.axis_index("seq")
    seqs, tokens, width = block.shape
    parts = block.reshape(count, seqs // count, tokens, width)
    out = jnp.zeros((seqs // count, count, tokens, width), block.dtype)
    for distance in range(count):
        part = lax.dynamic_index_in_dim(parts, (position + distance) % count, 0, keepdims=False)
        if distance:
            part = shifted(part, distance)
        out = lax.dynamic_update_slice(
            out, part[:, None], (0, (position - distance) % count, 0, 0)
        )
    return out.reshape(seqs // count, count * tokens, width)


def to_tokens(block):
    count = lax.axis_size("seq")
    position = lax.axis_index("seq")
    seqs, tokens, width = block.shape
    parts = block.reshape(seqs, count, tokens // count, width)
    out = jnp.zeros((count, seqs, tokens // count, width), block.dtype)
    for distance in range(count):
        part = lax.dynamic_index_in_dim(parts, (position + distance) % count, 1, keepdims=False)
        if distance:
            part = shifted(part, distance)
        out = lax.dynamic_update_slice(out, part[None], ((position - distance) % count, 0, 0, 0))
    return out.reshape(count * seqs, tokens // count, width)


def project(left, right):
    return jnp.dot(left, right, preferred_element_type=f32)


def project_left(left, right):
    return jnp.einsum("ti,to->io", left, right, preferred_element_type=f32)


def project_right(left, right):
    return jnp.einsum("to,io->ti", left, right, preferred_element_type=f32)


def normalize(values, norm_gain, norm_bias):
    average = jnp.mean(values, axis=-1, keepdims=True)
    centered = values - average
    variance = jnp.mean(centered * centered, axis=-1, keepdims=True)
    inv_root = lax.rsqrt(variance + norm_eps)
    normed = centered * inv_root
    return (normed * norm_gain + norm_bias, normed, inv_root)


def normalize_back(upstream, normed, inv_root, norm_gain):
    gain_grad = jnp.sum(upstream * normed, axis=0)
    bias_grad = jnp.sum(upstream, axis=0)
    scaled = upstream * norm_gain
    centred_part = scaled - jnp.mean(scaled, axis=-1, keepdims=True)
    input_grad = inv_root * (
        centred_part - normed * jnp.mean(scaled * normed, axis=-1, keepdims=True)
    )
    return (input_grad, gain_grad, bias_grad)


def gelu_pair(expanded):
    cumulative = 0.5 * (1.0 + lax.erf(expanded * inv_root_two))
    density = jnp.exp(-0.5 * expanded * expanded) * inv_root_tau
    return (expanded * cumulative, cumulative + expanded * density)


def exit_head(cls_state, labels, pool_proj, pool_bias, class_proj, class_bias):
    pool_full = pool_proj.astype(f32)
    class_full = class_proj.astype(f32)
    pooled = jnp.tanh(jnp.dot(cls_state, pool_full, precision=highest) + pool_bias.astype(f32))
    logits = jnp.dot(pooled, class_full, precision=highest) + class_bias.astype(f32)
    logit_top = jnp.max(logits, axis=-1, keepdims=True)
    log_norm = logit_top + jnp.log(jnp.sum(jnp.exp(logits - logit_top), axis=-1, keepdims=True))
    classes = jnp.arange(class_proj.shape[1], dtype=jnp.int32)
    chosen = (classes[None, :] == labels[:, None]).astype(f32)
    losses = log_norm[:, 0] - jnp.sum(chosen * logits, axis=-1)
    logit_grad = jnp.exp(logits - log_norm) - chosen
    pre_grad = jnp.dot(logit_grad, class_full.T, precision=highest) * (1.0 - pooled * pooled)
    return pooled, losses, logit_grad, pre_grad


def local(
    states, lengths, labels, cotangent,
    query_proj, key_proj, value_proj, output_proj,
    query_bias, value_bias, output_bias, first_gain, first_bias,
    inner_proj, inner_bias, outer_proj, outer_bias, second_gain, second_bias,
    pool_proj, pool_bias, class_proj, class_bias,
):
    group, block_len, width = states.shape
    count = lax.axis_size("seq")
    position = lax.axis_index("seq")
    lane = lax.axis_index("batch")
    seqs = group // count
    length = block_len * count
    rows = seqs * length
    x = to_sequences(states).reshape(rows, width)
    upstream = to_sequences(cotangent).reshape(rows, width)
    own_lengths = lax.dynamic_slice_in_dim(lengths, position * seqs, seqs)
    own_labels = lax.dynamic_slice_in_dim(labels, position * seqs, seqs)

    queries = (project(x, query_proj) + query_bias).astype(bf16)
    keys = project(x, key_proj).astype(bf16)
    values = (project(x, value_proj) + value_bias).astype(bf16)

    def heads_of(flat):
        return flat.reshape(seqs, length, HEADS, HEAD_DIM)

    scaling = HEAD_DIM ** (-0.5)
    scores = (
        jnp.einsum("sqhd,skhd->shqk", heads_of(queries), heads_of(keys), preferred_element_type=f32)
        * scaling
    )
    usable = (jnp.arange(length, dtype=jnp.int32)[None, :] < own_lengths[:, None])[:, None, None, :]
    masked = jnp.where(usable, scores, masked_fill)
    row_top = jnp.max(masked, axis=-1, keepdims=True)
    weights_exp = jnp.where(usable, jnp.exp(masked - row_top), 0.0)
    row_total = jnp.sum(weights_exp, axis=-1, keepdims=True)
    weights_low = weights_exp.astype(bf16)
    mixture = jnp.einsum(
        "shqk,skhd->shqd", weights_low, heads_of(values), preferred_element_type=f32
    )
    attended = jnp.transpose(mixture / row_total, (0, 2, 1, 3)).reshape(rows, width)
    attended_low = attended.astype(bf16)
    attn_out = project(attended_low, output_proj) + output_bias
    first_gain_f = first_gain.astype(f32)
    second_gain_f = second_gain.astype(f32)
    first_out, first_normed, first_inv = normalize(
        x.astype(f32) + attn_out, first_gain_f, first_bias.astype(f32)
    )
    first_low = first_out.astype(bf16)
    expanded = project(first_low, inner_proj) + inner_bias
    activated, gelu_slope = gelu_pair(expanded)
    hidden = activated.astype(bf16)
    projected = project(hidden, outer_proj) + outer_bias
    second_out, second_normed, second_inv = normalize(
        first_out + projected, second_gain_f, second_bias.astype(f32)
    )
    layer_rows = second_out.astype(bf16)
    layer_full = layer_rows.reshape(seqs, length, width)
    layer_out = to_tokens(layer_full)

    cls_own = layer_full[:, 0, :]
    pre_own = exit_head(
        cls_own.astype(f32), own_labels, pool_proj, pool_bias, class_proj, class_bias
    )[3]
    cls_grad = jnp.dot(pre_own, pool_proj.astype(f32).T, precision=highest)
    cls_all = lax.all_gather(cls_own, ("batch", "seq"), axis=0, tiled=True).astype(f32)
    labels_all = lax.all_gather(labels, "batch", axis=0, tiled=True)
    pooled, losses_all, logit_grad, pre_grad = exit_head(
        cls_all, labels_all, pool_proj, pool_bias, class_proj, class_bias
    )
    losses = lax.dynamic_slice_in_dim(losses_all, lane * group, group)
    class_bias_grad = jnp.sum(logit_grad, axis=0)
    class_proj_grad = jnp.dot(pooled.T, logit_grad, precision=highest)
    pool_bias_grad = jnp.sum(pre_grad, axis=0)
    pool_proj_grad = jnp.dot(cls_all.T, pre_grad, precision=highest)

    out_grad = (
        upstream.astype(f32).reshape(seqs, length, width).at[:, 0, :].add(cls_grad)
    ).reshape(rows, width)
    second_z_grad, second_gain_grad, second_bias_grad = normalize_back(
        out_grad, second_normed, second_inv, second_gain_f
    )
    projected_grad = second_z_grad.astype(bf16)
    outer_proj_grad = project_left(hidden, projected_grad)
    outer_bias_grad = jnp.sum(projected_grad.astype(f32), axis=0)
    expanded_grad = (project_right(projected_grad, outer_proj) * gelu_slope).astype(bf16)
    inner_proj_grad = project_left(first_low, expanded_grad)
    inner_bias_grad = jnp.sum(expanded_grad.astype(f32), axis=0)
    first_grad = second_z_grad + project_right(expanded_grad, inner_proj)
    first_z_grad, first_gain_grad, first_bias_grad = normalize_back(
        first_grad, first_normed, first_inv, first_gain_f
    )
    attn_grad = first_z_grad.astype(bf16)
    output_proj_grad = project_left(attended_low, attn_grad)
    output_bias_grad = jnp.sum(attn_grad.astype(f32), axis=0)
    attended_grad = project_right(attn_grad, output_proj).astype(bf16)
    delta = jnp.sum(
        heads_of(attended_grad).astype(f32) * heads_of(attended), axis=-1
    )
    delta = jnp.transpose(delta, (0, 2, 1))[..., None]
    probs = weights_exp / row_total
    prob_grad = jnp.einsum(
        "sqhd,skhd->shqk", heads_of(attended_grad), heads_of(values), preferred_element_type=f32
    )
    score_grad = (probs * (prob_grad - delta)).astype(bf16)
    value_rows = (
        jnp.einsum(
            "shqk,sqhd->skhd", probs.astype(bf16), heads_of(attended_grad),
            preferred_element_type=f32,
        )
        .astype(bf16)
        .reshape(rows, width)
    )
    query_rows = (
        (
            jnp.einsum("shqk,skhd->sqhd", score_grad, heads_of(keys), preferred_element_type=f32)
            * scaling
        )
        .astype(bf16)
        .reshape(rows, width)
    )
    key_rows = (
        (
            jnp.einsum("shqk,sqhd->skhd", score_grad, heads_of(queries), preferred_element_type=f32)
            * scaling
        )
        .astype(bf16)
        .reshape(rows, width)
    )
    query_bias_grad = jnp.sum(query_rows.astype(f32), axis=0)
    value_bias_grad = jnp.sum(value_rows.astype(f32), axis=0)
    states_grad = to_tokens(
        (
            first_z_grad
            + project_right(query_rows, query_proj)
            + project_right(key_rows, key_proj)
            + project_right(value_rows, value_proj)
        )
        .astype(bf16)
        .reshape(seqs, length, width)
    )
    outer_block = outer_proj_grad.astype(bf16)
    inner_block = (
        inner_proj_grad.astype(bf16).reshape(width, 4, width).transpose(1, 0, 2).reshape(-1, width)
    )
    g = jnp.concatenate(
        [outer_block, inner_block, output_proj_grad.astype(bf16)]
        + [project_left(x, r).astype(bf16) for r in (query_rows, key_rows, value_rows)]
    )
    small = jnp.concatenate(
        [
            query_bias_grad[None], value_bias_grad[None], output_bias_grad[None],
            first_gain_grad[None], first_bias_grad[None], outer_bias_grad[None],
            second_gain_grad[None], second_bias_grad[None],
            inner_bias_grad.reshape(4, width), jnp.zeros((4, width), f32),
        ]
    )
    total, small = reduce_all(g, small)
    total = total.astype(f32).reshape(12, width, width)
    outer_total = total[0:4].reshape(4 * width, width)
    inner_total = total[4:8].transpose(1, 0, 2).reshape(width, 4 * width)
    return (
        layer_out, losses, states_grad,
        total[9], total[10], total[11], total[8],
        small[0], small[1], small[2], small[3], small[4],
        inner_total, small[8:12].reshape(-1), outer_total, small[5], small[6], small[7],
        pool_proj_grad, pool_bias_grad, class_proj_grad, class_bias_grad,
    )


def solution(mesh):
    split = P("batch", "seq", None)
    in_specs = (split, P("batch"), P("batch"), split) + (P(),) * 19
    out_specs = (split, P("batch"), split) + (P(),) * 19
    return jax.shard_map(local, mesh=mesh, in_specs=in_specs, out_specs=out_specs, check_vma=False)
```

time: 1150 us -> 608 us (0.53)
  waiting for transfers between devices: 751 us -> 43 us
  Pallas kernels: 0 us -> 141 us
  starting transfers between devices: 4.38 us -> 49.4 us
  matrix products: 195 us -> 169 us
  local copies, waits for them, and re-layouts: 79.2 us -> 98.1 us
  between operations: 15.9 us -> 2.99 us
    psum x1 -> x0, waiting for transfers between devices: 407 us -> none  [local(): lax.psum((query_proj_grad, key_proj_grad, value_proj_grad, output_proj_gr...]
    ppermute x14 -> x12, waiting for transfers between devices: 344 us -> 43 us  [shifted(): return lax.ppermute(block, 'seq', route)]
    pallas_call x0 -> x1, Pallas kernels: none -> 141 us  [reduce_all(): pl.pallas_call(functools.partial(reduce_kernel, chunks, 'xy', tuple((3 *...]
    all_gather x0 -> x1, blocking collectives: none -> 60.9 us  [local(): lax.all_gather(cls_own, ('batch', 'seq'), axis=0, tiled=True).astype(f32)]
    psum x2 -> x0, blocking collectives: 60.8 us -> none  [the longest x1 47.5 us: local(): lax.psum((query_proj_grad, key_proj_grad, value_proj_grad, output_proj_gr...]
    ppermute x14 -> x12, starting transfers between devices: 4.35 us -> 49.4 us  [shifted(): return lax.ppermute(block, 'seq', route)]
    dot_general x48 -> x32, matrix products: 195 us -> 152 us  [the longest x6 32.5 us: project_right(): return jnp.einsum('to,io->ti', left, right, preferred_element_type=f32)]
    unnamed x201 -> x152, local copies, waits for them, and re-layouts: 45.2 us -> 17.6 us
  transfers between devices with their start and end apart: 15 -> 12, of which waited for: 15 -> 4; matrix products, arithmetic and copies ran while one was open for 12% -> 8% of each run, Pallas kernels for 0% -> 0%
where the time goes in v1:
time: 608 us; the launch traced here: 597 us
  matrix products  169 us (28%)
  Pallas kernels  141 us (23%)
  local copies, waits for them, and re-layouts  98.1 us (16%)
  blocking collectives  69.6 us (11%)
  starting transfers between devices  49.4 us (8%)
  waiting for transfers between devices  43 us (7%)
  other arithmetic  24.2 us (4%)
    pallas_call x1, Pallas kernels, reduce_all(): pl.pallas_call(functools.partial(reduce_kernel, chunks, 'xy', tuple((3 *...  141 us
    all_gather x1, blocking collectives, local(): lax.all_gather(cls_own, ('batch', 'seq'), axis=0, tiled=True).astype(f32)  60.9 us
    ppermute x12, starting transfers between devices, shifted(): return lax.ppermute(block, 'seq', route)  49.4 us
    ppermute x12, waiting for transfers between devices, shifted(): return lax.ppermute(block, 'seq', route)  43 us
    dot_general x6, matrix products, project_right(): return jnp.einsum('to,io->ti', left, right, preferred_element_type=f32)  32.5 us
    dot_general x6, matrix products, project(): return jnp.dot(left, right, preferred_element_type=f32)  26.9 us
    dot_general x6, matrix products, project_left(): return jnp.einsum('ti,to->io', left, right, preferred_element_type=f32)  25.2 us
    unnamed x152, local copies, waits for them, and re-layouts  17.6 us
  transfers between devices with their start and end apart: 12, of which 4 were waited for; matrix products, arithmetic and copies ran while one was open for 8% of the time, Pallas kernels for 0%

profile of v1, /device:TPU:1, one launch (start us, length us, event | category | flops | bytes accessed | tf_op | source)
XLA Modules:
  0.0 597.0 jit_solution(12147679035623163888)
XLA Ops:
  28.5 8.7 %all-reduce = s32[64]{0:T(128)} all-reduce(s32[64]{0:T(128)} %dynamic-update-slice.3), channel_id=1, replica_groups=mesh['batch'=8,'seq'=4] {'batch'}, use_global_device_ids=true, to_apply=%add | all-reduce | flops 64 | bytes 512
  38.5 11.2 %collective-permute-done.6 = bf16[2,128,768]{2,1,0:T(8,128)(2,1)} collective-permute-done((bf16[2,128,768]{2,1,0:T(8,128)(2,1)}, bf16[2,128,768]{2,1,0:T(8,128)(2,1)}, u32[]{:S(2)}, u32[]{:S(2)}) %collective-permute-start.6) | collective-permute-done | bytes 393248 | tf_op jit(solution)/shard_map/ppermute | solution.py:232
  49.7 10.2 %collective-permute-start.7 = (bf16[2,128,768]{2,1,0:T(8,128)(2,1)}, bf16[2,128,768]{2,1,0:T(8,128)(2,1)S(1)}, u32[]{:S(2)}, u32[]{:S(2)}) collective-permute-start(bf16[2,128,768]{2,1,0:T(8,128)(2,1)} %get-tuple-element.70), channel_id=1, source_target_pairs={{0,2},{1,3},{2,0},{3,1},{4,6},{5,7},{6,4},{7,5},{8,10},{9,11},{10,... | collective-permute-start | bytes 1179656 | tf_op jit(solution)/shard_map/ppermute | solution.py:232
  61.9 16.0 %collective-permute-done.7 = bf16[2,128,768]{2,1,0:T(8,128)(2,1)S(1)} collective-permute-done((bf16[2,128,768]{2,1,0:T(8,128)(2,1)}, bf16[2,128,768]{2,1,0:T(8,128)(2,1)S(1)}, u32[]{:S(2)}, u32[]{:S(2)}) %collective-permute-start.7) | collective-permute-done | bytes 393248 | tf_op jit(solution)/shard_map/ppermute | solution.py:232
  104.5 17.1 %fusion.83 = (f32[2,12,512]{2,1,0:T(8,128)S(1)}, f32[2,12,512,512]{2,3,1,0:T(8,128)}) fusion(pred[2,512]{1,0:T(4,128)(4,1)S(1)} %copy-done.55, bf16[2,512,12,64]{1,0,3,2:T(2,128)(2,1)S(1)} %reshape.266, bf16[2,512,12,64]{1,0,3,2:T(2,128)(2,1)} %reshape.265), kind=kOutput, calls=%fused_computation.174 | convolution fusion | flops 836764160 | bytes 28361728 | tf_op jit(solution)/shard_map/sub | solution.py:352
  121.6 12.6 %fusion.92 = (bf16[2,512,12,64]{1,3,2,0:T(8,128)(2,1)S(1)}, f32[2,512,12,64]{1,3,2,0:T(8,128)}) fusion(f32[2,512,12]{1,2,0:T(8,128)S(1)} %bitcast.223, f32[2,12,512,512]{2,3,1,0:T(8,128)} %get-tuple-element.79, bf16[2,512,12,64]{1,0,3,2:T(2,128)(2,1)} %reshape.267), kind=kOutput, calls=%fused_computation.175 | convolution fusion | flops 813170688 | bytes 31506432 | tf_op jit(solution)/shard_map/shqk,skhd->shqd/dot_general | solution.py:355
  139.8 9.8 %multiply_convert_fusion.1 = (bf16[1024,3072]{1,0:T(8,128)(2,1)S(1)}, f32[1024,3072]{1,0:T(8,128)}) fusion(f32[3072]{0:T(1024)S(1)} %copy-done.42, bf16[768,3072]{1,0:T(8,128)(2,1)S(1)} %bitcast.230, f32[1024,768]{1,0:T(8,128)S(1)} %get-tuple-element.83, f32[768]{0:T(1024)S(1)} %copy-done.47, f32[768]{0:T(1024)S(1)} %convert_element_type.175, ...), kind=kOutput, calls=%fused_computation.16 | convolution fusion | flops 4854644736 | bytes 26765312 | tf_op jit(solution)/shard_map/dot_general | solution.py:266
  149.7 5.5 fusion.94
  156.3 60.9 %all-gather = bf16[64,1,768]{2,1,0:T(2,128)(2,1)S(1)} all-gather(bf16[2,1,768]{2,1,0:T(2,128)(2,1)S(1)} %slice.96), channel_id=2, replica_groups=mesh['batch'=8,'seq'=4] {'batch','seq'}, dimensions={0}, use_global_device_ids=true | all-gather | bytes 101376 | tf_op jit(solution)/shard_map/all_gather | solution.py:383
  232.0 13.0 %convert_reduce_fusion = (f32[3072]{0:T(1024)S(1)}, bf16[1024,3072]{1,0:T(8,128)(2,1)S(1)}) fusion(f32[1024,3072]{1,0:T(8,128)} %get-tuple-element.85, f32[3072]{0:T(1024)S(1)} %copy-done.42, bf16[3072,768]{1,0:T(8,128)(2,1)} %param.40, f32[1024,768]{1,0:T(8,128)S(1)} %get-tuple-element.57), kind=kOutput, calls=%fused_computation.12 | convolution fusion | flops 4873516032 | bytes 26763264 | tf_op jit(solution)/shard_map/to,io->ti/dot_general | solution.py:274
  245.0 6.1 %multiply_reduce_fusion = (f32[768]{0:T(1024)S(1)}, f32[1024]{0:T(1024)S(1)}, f32[1024]{0:T(1024)S(1)}, f32[768]{0:T(1024)S(1)}, f32[1024,768]{1,0:T(8,128)S(1)}) fusion(f32[1024,768]{1,0:T(8,128)S(1)} %copy-done.5, f32[1024]{0:T(1024)S(1)} %add_rsqrt_fusion.1, f32[1024]{0:T(1024)S(1)} %broadcast_multiply_fusion.5, f32[768]{0:T(1024)S(1)} %convert_element_type.175, ...), kind=kOutput, calls=%fused_computation.32 | convolution fusion | flops 4839698432 | bytes 20472832 | tf_op jit(solution)/shard_map/to,io->ti/dot_general | solution.py:274
  251.1 7.9 %convolution_convert_fusion = bf16[768,3072]{1,0:T(8,128)(2,1)} fusion(bf16[1024,3072]{1,0:T(8,128)(2,1)S(1)} %get-tuple-element.98, f32[1024,768]{1,0:T(8,128)S(1)} %copy-done.5, f32[768]{0:T(1024)S(1)} %copy-done.47, f32[768]{0:T(1024)S(1)} %convert_element_type.175, f32[1024]{0:T(1024)S(1)} %add_rsqrt_fusion.1, f32[1024]{0:T(1024)S(1)} %broadcast_multiply_fusion.5), kind=kOutput, calls=%fused_computation.23 | convolution fusion | flops 4838129664 | bytes 14170112 | tf_op jit(solution)/shard_map/ti,to->io/dot_general | solution.py:270
  271.2 13.7 %convert_reduce_fusion.3 = (f32[12,64]{1,0:T(8,128)S(1)}, bf16[2,512,12,64]{1,3,2,0:T(8,128)(2,1)}) fusion(f32[2,12,512,512]{2,3,1,0:T(8,128)} %get-tuple-element.79, f32[2,12,512]{2,1,0:T(8,128)S(1)} %get-tuple-element.78, bf16[2,512,12,64]{1,0,3,2:T(2,128)(2,1)} %reshape.273), kind=kOutput, calls=%fused_computation.34 | convolution fusion | flops 820247808 | bytes 28363776 | tf_op jit(solution)/shard_map/shqk,sqhd->skhd/dot_general | solution.py:424
  287.9 15.5 %multiply_convert_fusion = bf16[2,12,512,512]{2,3,1,0:T(8,128)(2,1)} fusion(f32[2,12,512]{2,1,0:T(8,128)S(1)} %bitcast.224, f32[2,12,512,512]{2,3,1,0:T(8,128)} %get-tuple-element.79, f32[2,12,512]{2,1,0:T(8,128)S(1)} %get-tuple-element.78, bf16[2,512,12,64]{1,0,3,2:T(2,128)(2,1)} %reshape.267, bf16[2,512,12,64]{1,0,3,2:T(2,128)(2,1)} %reshape.273), kind=kOutput, calls=%fused_computation.1 | convolution fusion | flops 830472192 | bytes 40992768 | tf_op jit(solution)/shard_map/sqhd,skhd->shqk/dot_general | solution.py:419
  303.5 10.2 %fusion.33 = bf16[2,512,12,64]{1,3,2,0:T(8,128)(2,1)} fusion(bf16[2,12,512,512]{2,3,1,0:T(8,128)(2,1)} %multiply_convert_fusion, bf16[2,512,12,64]{1,0,3,2:T(2,128)(2,1)} %reshape.265), kind=kOutput, calls=%fused_computation.72 | convolution fusion | flops 806879232 | bytes 15728640 | tf_op jit(solution)/shard_map/shqk,sqhd->skhd/dot_general | solution.py:441
  313.7 8.0 %convert_reduce_fusion.4 = (f32[12,64]{1,0:T(8,128)S(1)}, bf16[2,512,12,64]{1,3,2,0:T(8,128)(2,1)}) fusion(bf16[2,12,512,512]{2,3,1,0:T(8,128)(2,1)} %multiply_convert_fusion, bf16[2,512,12,64]{1,0,3,2:T(2,128)(2,1)S(1)} %reshape.266), kind=kOutput, calls=%fused_computation.35 | convolution fusion | flops 808451328 | bytes 15731712 | tf_op jit(solution)/shard_map/shqk,skhd->sqhd/dot_general | solution.py:433
  321.7 7.2 %fusion.15 = bf16[9216,768]{1,0:T(8,128)(2,1)} fusion(bf16[1024,3072]{1,0:T(8,128)(2,1)S(1)} %bitcast.234, f32[1024,768]{1,0:T(8,128)S(1)} %copy-done.20), kind=kOutput, calls=%fused_computation.25 | convolution fusion | flops 4834983936 | bytes 14155776 | tf_op jit(solution)/shard_map/ti,to->io/dot_general | solution.py:270
  363.3 140.7 %shard_map.390 = (bf16[9216,768]{1,0:T(8,128)(2,1)}, f32[16,768]{1,0:T(8,128)}) custom-call(bf16[9216,768]{1,0:T(8,128)(2,1)} %fusion.25.g_ref, f32[16,768]{1,0:T(8,128)} %concatenate.9.small_ref), custom_call_target="tpu_custom_call" | custom-call | tf_op jit(solution)/shard_map/pallas_call | solution.py:198
  503.9 6.2 %fusion.82 = (f32[768,768]{1,0:T(8,128)}, f32[768,768]{1,0:T(8,128)}, f32[768,768]{1,0:T(8,128)}, f32[768,768]{1,0:T(8,128)}) fusion(bf16[9216,768]{1,0:T(8,128)(2,1)} %get-tuple-element.36), kind=kLoop, calls=%fused_computation.173 | loop fusion | bytes 18874368 | tf_op jit(solution)/shard_map/slice | solution.py:481
  510.1 12.2 %fusion.81 = (f32[3072,768]{1,0:T(8,128)}, f32[3072,768]{1,0:T(8,128)}) fusion(bf16[9216,768]{1,0:T(8,128)(2,1)} %get-tuple-element.36), kind=kLoop, calls=%fused_computation.172 | loop fusion | bytes 37748736 | tf_op jit(solution)/shard_map/slice | solution.py:477
  538.6 9.0 %copy.175 = f32[4,96,8,768]{3,2,0,1:T(8,128)} copy(f32[4,96,8,768]{3,2,1,0:T(8,128)} %bitcast.186) | data formatting | bytes 18874368 | tf_op jit(solution)/shard_map/reshape | solution.py:478
  549.4 27.1 %collective-permute-start.9 = (bf16[2,128,768]{2,1,0:T(8,128)(2,1)S(1)}, bf16[2,128,768]{2,1,0:T(8,128)(2,1)S(1)}, u32[]{:S(2)}, u32[]{:S(2)}) collective-permute-start(bf16[2,128,768]{2,1,0:T(8,128)(2,1)S(1)} %get-tuple-element.68), channel_id=1, source_target_pairs={{0,1},{1,2},{2,3},{3,0},{4,5},{5,6},{6,7},{7,4},{8,9},{9,10},{10,1... | collective-permute-start | bytes 1179656 | tf_op jit(solution)/shard_map/ppermute | solution.py:232
  578.6 5.2 collective-permute-done.9
  583.8 10.6 %collective-permute-done.10 = bf16[2,128,768]{2,1,0:T(8,128)(2,1)} collective-permute-done((bf16[2,128,768]{2,1,0:T(8,128)(2,1)S(1)}, bf16[2,128,768]{2,1,0:T(8,128)(2,1)}, u32[]{:S(2)}, u32[]{:S(2)}) %collective-permute-start.10) | collective-permute-done | bytes 393248 | tf_op jit(solution)/shard_map/ppermute | solution.py:232
  (286 shorter events, 149.6 us)
Async XLA Ops:
  0.7 135.7 %copy-start = (bf16[768,768]{1,0:T(8,128)(2,1)S(1)}, bf16[768,768]{1,0:T(8,128)(2,1)}, u32[]{:S(2)}) copy-start(bf16[768,768]{1,0:T(8,128)(2,1)} %param.32) | copy-start | bytes 3538948
  3.0 76.0 %collective-permute-start.2 = (bf16[2,128,768]{2,1,0:T(8,128)(2,1)S(1)}, bf16[2,128,768]{2,1,0:T(8,128)(2,1)}, u32[]{:S(2)}, u32[]{:S(2)}) collective-permute-start(bf16[2,128,768]{2,1,0:T(8,128)(2,1)S(1)} %get-tuple-element.75), channel_id=1, source_target_pairs={{0,3},{1,0},{2,1},{3,2},{4,7},{5,4},{6,5},{7,6},{8,11},{9,8},{10,9... | collective-permute-start | bytes 1179656 | tf_op jit(solution)/shard_map/ppermute | solution.py:232
  7.1 70.8 %collective-permute-start.1 = (bf16[2,128,768]{2,1,0:T(8,128)(2,1)S(1)}, bf16[2,128,768]{2,1,0:T(8,128)(2,1)}, u32[]{:S(2)}, u32[]{:S(2)}) collective-permute-start(bf16[2,128,768]{2,1,0:T(8,128)(2,1)S(1)} %get-tuple-element.76), channel_id=1, source_target_pairs={{0,2},{1,3},{2,0},{3,1},{4,6},{5,7},{6,4},{7,5},{8,10},{9,11},{10,... | collective-permute-start | bytes 1179656 | tf_op jit(solution)/shard_map/ppermute | solution.py:232
  7.1 53.8 %collective-permute-start = (bf16[2,128,768]{2,1,0:T(8,128)(2,1)}, bf16[2,128,768]{2,1,0:T(8,128)(2,1)}, u32[]{:S(2)}, u32[]{:S(2)}) collective-permute-start(bf16[2,128,768]{2,1,0:T(8,128)(2,1)} %get-tuple-element.77), channel_id=1, source_target_pairs={{0,1},{1,2},{2,3},{3,0},{4,5},{5,6},{6,7},{7,4},{8,9},{9,10},{10,1... | collective-permute-start | bytes 1179656 | tf_op jit(solution)/shard_map/ppermute | solution.py:232
  8.6 70.4 %collective-permute-start.8 = (bf16[2,128,768]{2,1,0:T(8,128)(2,1)}, bf16[2,128,768]{2,1,0:T(8,128)(2,1)}, u32[]{:S(2)}, u32[]{:S(2)}) collective-permute-start(bf16[2,128,768]{2,1,0:T(8,128)(2,1)} %get-tuple-element.69), channel_id=1, source_target_pairs={{0,3},{1,0},{2,1},{3,2},{4,7},{5,4},{6,5},{7,6},{8,11},{9,8},{10,9... | collective-permute-start | bytes 1179656 | tf_op jit(solution)/shard_map/ppermute | solution.py:232
  11.4 38.3 %collective-permute-start.6 = (bf16[2,128,768]{2,1,0:T(8,128)(2,1)}, bf16[2,128,768]{2,1,0:T(8,128)(2,1)}, u32[]{:S(2)}, u32[]{:S(2)}) collective-permute-start(bf16[2,128,768]{2,1,0:T(8,128)(2,1)} %get-tuple-element.71), channel_id=1, source_target_pairs={{0,1},{1,2},{2,3},{3,0},{4,5},{5,6},{6,7},{7,4},{8,9},{9,10},{10,1... | collective-permute-start | bytes 1179656 | tf_op jit(solution)/shard_map/ppermute | solution.py:232
  37.4 44.5 %copy-start.33 = (bf16[768,768]{1,0:T(8,128)(2,1)S(1)}, bf16[768,768]{1,0:T(8,128)(2,1)}, u32[]{:S(2)}) copy-start(bf16[768,768]{1,0:T(8,128)(2,1)} %param.31) | copy-start | bytes 3538948
  37.4 44.5 %copy-start.51 = (f32[768]{0:T(1024)S(1)}, f32[768]{0:T(1024)}, u32[]{:S(2)}) copy-start(f32[768]{0:T(1024)} %convert_element_type.170) | copy-start | bytes 9220
  49.7 28.2 %collective-permute-start.7 = (bf16[2,128,768]{2,1,0:T(8,128)(2,1)}, bf16[2,128,768]{2,1,0:T(8,128)(2,1)S(1)}, u32[]{:S(2)}, u32[]{:S(2)}) collective-permute-start(bf16[2,128,768]{2,1,0:T(8,128)(2,1)} %get-tuple-element.70), channel_id=1, source_target_pairs={{0,2},{1,3},{2,0},{3,1},{4,6},{5,7},{6,4},{7,5},{8,10},{9,11},{10,... | collective-permute-start | bytes 1179656 | tf_op jit(solution)/shard_map/ppermute | solution.py:232
  155.1 71.2 %copy-start.2 = (f32[1024,768]{1,0:T(8,128)}, f32[1024,768]{1,0:T(8,128)S(1)}, u32[]{:S(2)}) copy-start(f32[1024,768]{1,0:T(8,128)S(1)} %get-tuple-element.87) | copy-start | bytes 9437188
  155.7 61.6 %copy-start.10 = (bf16[768,768]{1,0:T(8,128)(2,1)S(1)}, bf16[768,768]{1,0:T(8,128)(2,1)}, u32[]{:S(2)}) copy-start(bf16[768,768]{1,0:T(8,128)(2,1)} %param.44) | copy-start | bytes 3538948
  155.7 62.2 %copy-start.41 = (bf16[768,3]{0,1:T(4,128)(2,1)S(1)}, bf16[768,3]{0,1:T(4,128)(2,1)}, u32[]{:S(2)}) copy-start(bf16[768,3]{0,1:T(4,128)(2,1)} %param.46) | copy-start | bytes 13828
  155.7 62.2 %copy-start.56 = (f32[3]{0:T(128)S(1)}, f32[3]{0:T(128)}, u32[]{:S(2)}) copy-start(f32[3]{0:T(128)} %convert_element_type.185) | copy-start | bytes 40
  155.7 62.5 %copy-start.43 = (s32[64]{0:T(128)S(1)}, s32[64]{0:T(128)}, u32[]{:S(2)}) copy-start(s32[64]{0:T(128)} %all-reduce) | copy-start | bytes 772
  155.8 64.9 %copy-start.14 = (bf16[2,4,128,768]{3,2,1,0:T(8,128)(2,1)S(1)}, bf16[2,4,128,768]{3,2,1,0:T(8,128)(2,1)}, u32[]{:S(2)}) copy-start(bf16[2,4,128,768]{3,2,1,0:T(8,128)(2,1)} %copy-done.13) | copy-start | bytes 4718596
  156.3 64.3 %copy-start.11 = (bf16[1024,768]{1,0:T(8,128)(2,1)}, bf16[1024,768]{1,0:T(8,128)(2,1)S(1)}, u32[]{:S(2)}) copy-start(bf16[1024,768]{1,0:T(8,128)(2,1)S(1)} %add_convert_fusion.1) | copy-start | bytes 4718596
  523.3 54.2 %collective-permute-start.4 = (bf16[2,128,768]{2,1,0:T(8,128)(2,1)}, bf16[2,128,768]{2,1,0:T(8,128)(2,1)}, u32[]{:S(2)}, u32[]{:S(2)}) collective-permute-start(bf16[2,128,768]{2,1,0:T(8,128)(2,1)} %get-tuple-element.73), channel_id=1, source_target_pairs={{0,2},{1,3},{2,0},{3,1},{4,6},{5,7},{6,4},{7,5},{8,10},{9,11},{10,... | collective-permute-start | bytes 1179656 | tf_op jit(solution)/shard_map/ppermute | solution.py:232
  524.4 24.9 %collective-permute-start.3 = (bf16[2,128,768]{2,1,0:T(8,128)(2,1)}, bf16[2,128,768]{2,1,0:T(8,128)(2,1)}, u32[]{:S(2)}, u32[]{:S(2)}) collective-permute-start(bf16[2,128,768]{2,1,0:T(8,128)(2,1)} %get-tuple-element.74), channel_id=1, source_target_pairs={{0,1},{1,2},{2,3},{3,0},{4,5},{5,6},{6,7},{7,4},{8,9},{9,10},{10,1... | collective-permute-start | bytes 1179656 | tf_op jit(solution)/shard_map/ppermute | solution.py:232
  534.0 44.5 %collective-permute-start.5 = (bf16[2,128,768]{2,1,0:T(8,128)(2,1)S(1)}, bf16[2,128,768]{2,1,0:T(8,128)(2,1)S(1)}, u32[]{:S(2)}, u32[]{:S(2)}) collective-permute-start(bf16[2,128,768]{2,1,0:T(8,128)(2,1)S(1)} %get-tuple-element.72), channel_id=1, source_target_pairs={{0,3},{1,0},{2,1},{3,2},{4,7},{5,4},{6,5},{7,6},{8,11},{9,8},{10,9... | collective-permute-start | bytes 1179656 | tf_op jit(solution)/shard_map/ppermute | solution.py:232
  537.6 57.8 %collective-permute-start.11 = (bf16[2,128,768]{2,1,0:T(8,128)(2,1)S(1)}, bf16[2,128,768]{2,1,0:T(8,128)(2,1)S(1)}, u32[]{:S(2)}, u32[]{:S(2)}) collective-permute-start(bf16[2,128,768]{2,1,0:T(8,128)(2,1)S(1)} %get-tuple-element.66), channel_id=1, source_target_pairs={{0,3},{1,0},{2,1},{3,2},{4,7},{5,4},{6,5},{7,6},{8,11},{9,8},{10,9... | collective-permute-start | bytes 1179656 | tf_op jit(solution)/shard_map/ppermute | solution.py:232
  537.6 56.7 %collective-permute-start.10 = (bf16[2,128,768]{2,1,0:T(8,128)(2,1)S(1)}, bf16[2,128,768]{2,1,0:T(8,128)(2,1)}, u32[]{:S(2)}, u32[]{:S(2)}) collective-permute-start(bf16[2,128,768]{2,1,0:T(8,128)(2,1)S(1)} %get-tuple-element.67), channel_id=1, source_target_pairs={{0,2},{1,3},{2,0},{3,1},{4,6},{5,7},{6,4},{7,5},{8,10},{9,11},{10,... | collective-permute-start | bytes 1179656 | tf_op jit(solution)/shard_map/ppermute | solution.py:232
  538.6 37.9 %copy-start.27 = (bf16[4,2,128,768]{3,2,1,0:T(8,128)(2,1)S(1)}, bf16[4,2,128,768]{3,2,1,0:T(8,128)(2,1)}, u32[]{:S(2)}) copy-start(bf16[4,2,128,768]{3,2,1,0:T(8,128)(2,1)} %copy-done.26) | copy-start | bytes 4718596
  548.1 48.5 %copy-start.1 = (bf16[768,768]{1,0:T(8,128)(2,1)S(1)}, bf16[768,768]{1,0:T(8,128)(2,1)}, u32[]{:S(2)}) copy-start(bf16[768,768]{1,0:T(8,128)(2,1)} %param.32) | copy-start | bytes 3538948
  549.4 34.4 %collective-permute-start.9 = (bf16[2,128,768]{2,1,0:T(8,128)(2,1)S(1)}, bf16[2,128,768]{2,1,0:T(8,128)(2,1)S(1)}, u32[]{:S(2)}, u32[]{:S(2)}) collective-permute-start(bf16[2,128,768]{2,1,0:T(8,128)(2,1)S(1)} %get-tuple-element.68), channel_id=1, source_target_pairs={{0,1},{1,2},{2,3},{3,0},{4,5},{5,6},{6,7},{7,4},{8,9},{9,10},{10,1... | collective-permute-start | bytes 1179656 | tf_op jit(solution)/shard_map/ppermute | solution.py:232
  (59 other events, 411.9 us)

commit v2 on v1

v2 whole, which is shorter than its diff:
```python
import functools

import jax
import jax.numpy as jnp
from jax import lax
from jax.experimental import pallas as pl
from jax.experimental.pallas import tpu as pltpu
from jax.sharding import PartitionSpec as P

HEADS = 12
HEAD_DIM = 64
WIDTH = 768
HALF = 384
CHUNK = 256
MESH = pl.DeviceIdType.MESH

bf16 = jnp.bfloat16
f32 = jnp.float32
highest = lax.Precision.HIGHEST
norm_eps = 1e-06
masked_fill = -1e30
inv_root_two = 0.7071067811865476
inv_root_tau = 0.3989422804014327


def pick(code, table):
    out = table[-1]
    for i in range(len(table) - 2, -1, -1):
        out = jnp.where(code == i, table[i], out)
    return out


def flipped(index, bit):
    return index + bit * (1 - 2 * ((index // bit) % 2))


NT = (((1,), (1,)), ((), ()))
NN = (((1,), (0,)), ((), ()))
TN = (((0,), (0,)), ((), ()))
VECS = 24
QB, VB, OB, G1, B1, IB, UB, G2, B2, PB, CP, CB = 0, 1, 2, 3, 4, 5, 9, 10, 11, 12, 13, 16


def dot(left, right, dims=NN):
    return lax.dot_general(left, right, dims, preferred_element_type=f32)


def gelu_parts(u):
    t = 1.0 / (1.0 + (0.3275911 * inv_root_two) * jnp.abs(u))
    bell = jnp.exp(-0.5 * u * u)
    poly = 1.061405429
    for coefficient in (-1.453152027, 1.421413741, -0.284496736, 0.254829592):
        poly = poly * t + coefficient
    tail = (0.5 * t) * poly * bell
    cumulative = jnp.where(u >= 0.0, 1.0 - tail, tail)
    return u * cumulative, cumulative + u * (bell * inv_root_tau)


def norm_rows(z):
    average = jnp.mean(z, axis=-1, keepdims=True)
    centered = z - average
    inv_root = lax.rsqrt(jnp.mean(centered * centered, axis=-1, keepdims=True) + norm_eps)
    return centered * inv_root, inv_root


def norm_rows_back(upstream, normed, inv_root, gain):
    scaled = upstream * gain
    return inv_root * (
        scaled
        - jnp.mean(scaled, axis=-1, keepdims=True)
        - normed * jnp.mean(scaled * normed, axis=-1, keepdims=True)
    )


def tile(i, size):
    return pl.ds(pl.multiple_of(i * size, size), size)


def copies(pairs, sems):
    out = []
    for i, (src, dst) in enumerate(pairs):
        out.append(pltpu.make_async_copy(src, dst, sems.at[i]))
    return out


def head_lanes(which):
    lane = lax.broadcasted_iota(jnp.int32, (1, 128), 1)
    return (lane >= 64) if which else (lane < 64)


def only(mask, block):
    return jnp.where(mask, block, jnp.zeros_like(block))


def attend_pair(q2, k2, v2, length, keys):
    k2 = k2[:keys]
    v2 = v2[:keys]
    place = lax.broadcasted_iota(jnp.int32, (1, keys), 1)
    out = None
    logs = []
    for which in (0, 1):
        lanes = head_lanes(which)
        scores = dot(only(lanes, q2) * bf16(0.125), k2, NT)
        scores = jnp.where(place < length, scores, masked_fill)
        top = jnp.max(scores, axis=-1, keepdims=True)
        weights = jnp.exp(scores - top)
        total = jnp.sum(weights, axis=-1, keepdims=True)
        part = dot(weights.astype(bf16), only(lanes, v2)) * (1.0 / total)
        out = part if out is None else out + part
        logs.append(top + jnp.log(total))
    return out, logs


def spread(src, dst, seqs, tokens, to_rows, sends, recvs, base, s):
    count = lax.axis_size("seq")
    b = lax.axis_index("batch")
    z = lax.axis_index("seq")
    out = []
    for d in range(1, count):
        other = lax.rem(z + d, count)
        if to_rows:
            source = src.at[other * seqs + s]
            target = dst.at[pl.ds(pl.multiple_of((s * count + z) * tokens, tokens), tokens)]
        else:
            source = src.at[pl.ds(pl.multiple_of((s * count + other) * tokens, tokens), tokens)]
            target = dst.at[z * seqs + s]
        i = base + s * (count - 1) + d - 1
        out.append(
            pltpu.make_async_remote_copy(
                source, target, sends.at[i], recvs.at[i],
                device_id=(b, other), device_id_type=MESH,
            )
        )
    return out


def own_part(src, dst, seqs, tokens, to_rows, sem, s):
    count = lax.axis_size("seq")
    z = lax.axis_index("seq")
    block = z * seqs + s
    rows = pl.ds(pl.multiple_of((s * count + z) * tokens, tokens), tokens)
    if to_rows:
        return pltpu.make_async_copy(src.at[block], dst.at[rows], sem)
    return pltpu.make_async_copy(src.at[rows], dst.at[block], sem)


def greet_line():
    count = lax.axis_size("seq")
    z = lax.axis_index("seq")
    return [(lax.axis_index("batch"), lax.rem(z + d, count)) for d in range(1, count)]


def forward_kernel(
    seqs, len_ref, states, cot, wq, wk, wv, wo, w1, w2,
    query_bias, value_bias, output_bias, first_gain, first_bias, inner_bias, outer_bias,
    second_gain, second_bias, pool_bias, class_proj, class_bias,
    vec_ref, x_out, cot_out, q_out, k_out, v_out, att_out, n1_out, low_out, hid_out, slope_out,
    n2_out, stat_out, y_out,
    x_s, wq_s, wk_s, wv_s, wo_s, w1_s, w2_s,
    q_s, k_s, v_s, att_s, n1_s, low_s, hid_s, slope_s, n2_s, stat_s, y_s, z_s,
    in_sem, out_sem, own_sem, sends, recvs,
):
    rows = z_s.shape[0]
    tokens = states.shape[1]
    line = greet_line()
    barrier = pltpu.get_barrier_semaphore()
    for who in line:
        pl.semaphore_signal(barrier, inc=1, device_id=who, device_id_type=MESH)
    weights_in = copies(
        [(wq, wq_s), (wk, wk_s), (wv, wv_s), (wo, wo_s), (w1, w1_s), (w2, w2_s)], in_sem
    )
    own = []
    for s in range(seqs):
        own.append(own_part(states, x_s, seqs, tokens, True, own_sem.at[s], s))
        own.append(own_part(cot, cot_out, seqs, tokens, True, own_sem.at[seqs + s], s))
    for copy in own + weights_in:
        copy.start()
    pl.semaphore_wait(barrier, len(line))
    moves = [spread(states, x_s, seqs, tokens, True, sends, recvs, 0, s) for s in range(seqs)]
    late = [
        spread(cot, cot_out, seqs, tokens, True, sends, recvs, seqs * len(line), s)
        for s in range(seqs)
    ]
    for group in moves + late:
        for copy in group:
            copy.start()
    vec_ref[...] = jnp.zeros_like(vec_ref)
    for i, ref in (
        (QB, query_bias), (VB, value_bias), (OB, output_bias), (G1, first_gain), (B1, first_bias),
        (UB, outer_bias), (G2, second_gain), (B2, second_bias), (PB, pool_bias),
    ):
        vec_ref[i : i + 1, :] = ref[...].astype(f32).reshape(1, WIDTH)
    for i in range(4):
        vec_ref[IB + i : IB + i + 1, :] = (
            inner_bias[i * WIDTH : (i + 1) * WIDTH].astype(f32).reshape(1, WIDTH)
        )
    eye = (
        lax.broadcasted_iota(jnp.int32, (8, 3), 0) == lax.broadcasted_iota(jnp.int32, (8, 3), 1)
    ).astype(bf16)
    vec_ref[CP : CP + 3, :] = dot(eye, class_proj[...], NT)[0:3, :]
    vec_ref[CB : CB + 1, 0:3] = class_bias[...].astype(f32).reshape(1, 3)

    z = lax.axis_index("seq")
    waiting = []
    for s in range(seqs):
        for copy in moves[s]:
            copy.wait_recv()
        own[2 * s].wait()
        part = pl.ds(s * rows, rows)
        waiting += forward_rows(
            s, part, len_ref[z * seqs + s], rows, s == 0, vec_ref, weights_in,
            (x_s, wq_s, wk_s, wv_s, wo_s, w1_s, w2_s, q_s, k_s, v_s, att_s, n1_s, low_s, hid_s,
             slope_s, n2_s, stat_s, y_s, z_s),
            (x_out, q_out, k_out, v_out, att_out, n1_out, low_out, hid_out, slope_out, n2_out,
             stat_out, y_out),
            out_sem,
        )
    for group in moves:
        for copy in group:
            copy.wait_send()
    for group in late:
        for copy in group:
            copy.wait()
    for s in range(seqs):
        own[2 * s + 1].wait()
    for copy in waiting:
        copy.wait()


def forward_rows(s, part, length, rows, first_time, vec_ref, weights_in, scratch, outs, out_sem):
    (x_s, wq_s, wk_s, wv_s, wo_s, w1_s, w2_s, q_s, k_s, v_s, att_s, n1_s, low_s, hid_s,
     slope_s, n2_s, stat_s, y_s, z_s) = scratch
    start = s * rows
    out = [
        pltpu.make_async_copy(src.at[part], dst.at[part], out_sem.at[s, i])
        for i, (src, dst) in enumerate(
            zip((x_s, q_s, k_s, v_s, att_s, n1_s, low_s, hid_s, slope_s, n2_s, stat_s, y_s), outs)
        )
    ]
    out[0].start()
    for i, (w, dst, bias) in enumerate(((wq_s, q_s, QB), (wk_s, k_s, None), (wv_s, v_s, VB))):
        if first_time:
            weights_in[i].wait()

        @pl.loop(0, WIDTH // 256)
        def _(j):
            cols = tile(j, 256)
            grid = dot(x_s[part, :], w[:, cols])
            if bias is not None:
                grid = grid + vec_ref[bias : bias + 1, cols]
            dst[part, cols] = grid.astype(bf16)

        out[1 + i].start()

    stat_s[part, :] = jnp.zeros((rows, 128), f32)
    lane = lax.broadcasted_iota(jnp.int32, (1, 128), 1)

    @pl.loop(0, HEADS // 2)
    def _(p):
        cols = tile(p, 128)
        mix, logs = attend_pair(q_s[part, cols], k_s[part, cols], v_s[part, cols], length, rows)
        att_s[part, cols] = mix.astype(bf16)
        stat_s[part, :] = jnp.where(
            lane == 2 * p, logs[0], jnp.where(lane == 2 * p + 1, logs[1], stat_s[part, :])
        )

    out[4].start()
    if first_time:
        weights_in[3].wait()

    @pl.loop(0, WIDTH // 256)
    def _(j):
        cols = tile(j, 256)
        z_s[:, cols] = (
            x_s[part, cols].astype(f32)
            + dot(att_s[part, :], wo_s[:, cols])
            + vec_ref[OB : OB + 1, cols]
        )

    @pl.loop(0, rows // 128)
    def _(i):
        r = tile(i, 128)
        q = pl.ds(pl.multiple_of(start + i * 128, 128), 128)
        normed, inv_root = norm_rows(z_s[r, :])
        n1_s[q, :] = normed.astype(bf16)
        first = normed * vec_ref[G1 : G1 + 1, :] + vec_ref[B1 : B1 + 1, :]
        low_s[q, :] = first.astype(bf16)
        z_s[r, :] = first + vec_ref[UB : UB + 1, :]
        stat_s[q, :] = jnp.where(lane == 12, inv_root, stat_s[q, :])

    out[5].start()
    out[6].start()
    if first_time:
        weights_in[4].wait()
        weights_in[5].wait()
    ft = 256

    @pl.loop(0, 4 * WIDTH // ft)
    def _(j):
        cols = tile(j, ft)
        u = dot(low_s[part, :], w1_s[:, cols]) + vec_ref[pl.ds(IB + j // 3, 1), tile(j % 3, ft)]
        h, slope = gelu_parts(u)
        hid_s[part, cols] = h.astype(bf16)
        slope_s[part, cols] = slope.astype(bf16)

    out[7].start()
    out[8].start()

    @pl.loop(0, WIDTH // 256)
    def _(j):
        cols = tile(j, 256)
        z_s[:, cols] += dot(hid_s[part, :], w2_s[:, cols])

    @pl.loop(0, rows // 128)
    def _(i):
        r = tile(i, 128)
        q = pl.ds(pl.multiple_of(start + i * 128, 128), 128)
        normed, inv_root = norm_rows(z_s[r, :])
        n2_s[q, :] = normed.astype(bf16)
        y_s[q, :] = (normed * vec_ref[G2 : G2 + 1, :] + vec_ref[B2 : B2 + 1, :]).astype(bf16)
        stat_s[q, :] = jnp.where(lane == 13, inv_root, stat_s[q, :])

    for i in (9, 10, 11):
        out[i].start()
    return out


def forward(lengths, states, cotangent, weights, small):
    count = lax.axis_size("seq")
    group, tokens, width = states.shape
    seqs = group // count
    one = count * tokens
    rows = seqs * one
    ff = 4 * width
    anywhere = pl.BlockSpec(memory_space=pl.ANY)
    in_vmem = pl.BlockSpec(memory_space=pltpu.VMEM)
    saved = [((rows, width), bf16)] * 6 + [((rows, ff), bf16)] * 2 + [
        ((rows, width), bf16), ((rows, 128), f32), ((rows, width), bf16),
    ]
    outs = [((VECS, width), f32), ((rows, width), bf16), ((rows, width), bf16)] + saved
    moves = 2 * seqs * (count - 1)
    flops = 2 * rows * width * (4 * width + 2 * ff) + 4 * rows * one * width
    dma = pltpu.SemaphoreType.DMA
    return pl.pallas_call(
        functools.partial(forward_kernel, seqs),
        out_shape=tuple(jax.ShapeDtypeStruct(s, t) for s, t in outs),
        in_specs=[pl.BlockSpec(memory_space=pltpu.SMEM)] + [anywhere] * 8 + [in_vmem] * len(small),
        out_specs=(in_vmem,) + (anywhere,) * (len(outs) - 1),
        scratch_shapes=[pltpu.VMEM((rows, width), bf16)]
        + [pltpu.VMEM(w.shape, bf16) for w in weights]
        + [pltpu.VMEM(s, t) for s, t in saved]
        + [
            pltpu.VMEM((one, width), f32), dma((6,)), dma((seqs, 12)), dma((2 * seqs,)),
            dma((moves,)), dma((moves,)),
        ],
        compiler_params=pltpu.CompilerParams(
            collective_id=1, has_side_effects=True, vmem_limit_bytes=60 * 2**20
        ),
        cost_estimate=pl.CostEstimate(
            flops=flops, bytes_accessed=50 * 2**20, transcendentals=rows * (ff + 12 * one)
        ),
        name="forward",
    )(lengths, states, cotangent, *weights, *small)


def exit_back(cls_rows, labels, vec_ref, pool_s):
    pooled = jnp.tanh(dot(cls_rows, pool_s[...]) + vec_ref[PB : PB + 1, :])
    class_rows = vec_ref[CP : CP + 3, :]
    logits = [
        jnp.sum(pooled * class_rows[i : i + 1, :], axis=-1, keepdims=True)
        + vec_ref[CB : CB + 1, i : i + 1]
        for i in range(3)
    ]
    top = jnp.maximum(jnp.maximum(logits[0], logits[1]), logits[2])
    raised = [jnp.exp(l - top) for l in logits]
    total = raised[0] + raised[1] + raised[2]
    back = jnp.zeros_like(pooled)
    for i in range(3):
        back = back + (raised[i] / total - (labels == i).astype(f32)) * class_rows[i : i + 1, :]
    pre = back * (1.0 - pooled * pooled)
    high = pre.astype(bf16)
    rest = pre - high.astype(f32)
    mid = rest.astype(bf16)
    low = (rest - mid.astype(f32)).astype(bf16)
    return dot(high, pool_s[...], NT) + dot(mid, pool_s[...], NT) + dot(low, pool_s[...], NT)


def ffn_back_kernel(
    seqs, label_ref, vec_ref, cot, n2, hid, slope, low, n1, stat, y, w1, w2, pool,
    g_out, ag_out, sums_out, head_out,
    cot_s, n2_s, hid_s, slope_s, low_s, n1_s, stat_s, cls_s, w1_s, w2_s, pool_s,
    pg_s, fg_s, eg_s, gst, ag_s, row_s, in_sem, out_sem,
):
    rows = cot_s.shape[0]
    one = rows // seqs
    cls_in = [
        pltpu.make_async_copy(
            y.at[pl.ds(s * one, 16)], cls_s.at[pl.ds(s * 16, 16)], in_sem.at[10 + s]
        )
        for s in range(seqs)
    ]
    loads = copies(
        [
            (pool, pool_s), (cot, cot_s), (n2, n2_s), (stat, stat_s), (w2, w2_s), (hid, hid_s),
            (slope, slope_s), (low, low_s), (w1, w1_s), (n1, n1_s),
        ],
        in_sem,
    )
    for copy in cls_in + loads:
        copy.start()
    for copy in cls_in:
        copy.wait()
    loads[0].wait()
    z = lax.axis_index("seq")
    place = lax.broadcasted_iota(jnp.int32, (16 * seqs, 1), 0)
    labels = jnp.zeros((16 * seqs, 1), jnp.int32)
    label_row = jnp.zeros((1, 128), f32)
    lane = lax.broadcasted_iota(jnp.int32, (1, 128), 1)
    for s in range(seqs):
        label = label_ref[z * seqs + s]
        labels = jnp.where(place == 16 * s, label, labels)
        label_row = jnp.where(lane == s, label.astype(f32), label_row)
    cls_grad = exit_back(cls_s[...], labels, vec_ref, pool_s)
    row_s[...] = jnp.zeros_like(row_s)
    for s in range(seqs):
        first = cls_s[16 * s : 16 * (s + 1), :].astype(f32)
        for j in range(6):
            row_s[s * 6 + j : s * 6 + j + 1, :] = first[0:1, j * 128 : (j + 1) * 128]
    row_s[12:13, :] = label_row
    head_out[...] = row_s[...].astype(bf16)
    for copy in loads[1:4]:
        copy.wait()
    sums_out[...] = jnp.zeros_like(sums_out)
    ROW = 128

    def add_sum(index, block):
        sums_out[index : index + 1, :] += jnp.sum(block, axis=0, keepdims=True)

    @pl.loop(0, rows // ROW)
    def _(i):
        r = tile(i, ROW)
        upstream = cot_s[r, :].astype(f32)
        place = lax.broadcasted_iota(jnp.int32, (ROW, 1), 0) + i * ROW
        for s in range(seqs):
            upstream = upstream + jnp.where(place == s * one, cls_grad[16 * s : 16 * s + 1, :], 0.0)
        normed = n2_s[r, :].astype(f32)
        add_sum(G2, upstream * normed)
        add_sum(B2, upstream)
        zg = norm_rows_back(upstream, normed, stat_s[r, 13:14], vec_ref[G2 : G2 + 1, :])
        low = zg.astype(bf16)
        pg_s[r, :] = low
        add_sum(UB, low.astype(f32))
        fg_s[r, :] = zg

    for copy in loads[4:9]:
        copy.wait()

    def g_copy(slot, unit):
        return pltpu.make_async_copy(gst.at[slot], g_out.at[unit], out_sem.at[slot])

    for j in range(4):

        @pl.loop(0, WIDTH // 256)
        def _(t):
            cols = tile(t, 256)
            ff = pl.ds(pl.multiple_of(j * WIDTH + t * 256, 256), 256)
            grad = dot(pg_s[...], w2_s[ff, :], NT) * slope_s[:, ff].astype(f32)
            low = grad.astype(bf16)
            eg_s[:, cols] = low
            sums_out[IB + j : IB + j + 1, cols] = jnp.sum(low.astype(f32), axis=0, keepdims=True)

        if j > 0:
            g_copy(0, j - 1).wait()

        @pl.loop(0, WIDTH // 256)
        def _(t):
            ff = pl.ds(pl.multiple_of(j * WIDTH + t * 256, 256), 256)
            gst[0, tile(t, 256), :] = dot(hid_s[:, ff], pg_s[...], TN).astype(bf16)

        g_copy(0, j).start()
        if j > 0:
            g_copy(1, 4 + j - 1).wait()

        @pl.loop(0, WIDTH // 256)
        def _(t):
            gst[1, tile(t, 256), :] = dot(low_s[:, tile(t, 256)], eg_s[...], TN).astype(bf16)

        g_copy(1, 4 + j).start()

        @pl.loop(0, WIDTH // 256)
        def _(t):
            cols = tile(t, 256)
            fg_s[:, cols] += dot(eg_s[...], w1_s[cols, j * WIDTH : (j + 1) * WIDTH], NT)

    loads[9].wait()

    @pl.loop(0, rows // ROW)
    def _(i):
        r = tile(i, ROW)
        upstream = fg_s[r, :]
        normed = n1_s[r, :].astype(f32)
        add_sum(G1, upstream * normed)
        add_sum(B1, upstream)
        zg = norm_rows_back(upstream, normed, stat_s[r, 12:13], vec_ref[G1 : G1 + 1, :])
        low = zg.astype(bf16)
        ag_s[r, :] = low
        add_sum(OB, low.astype(f32))

    ag_copy = pltpu.make_async_copy(ag_s, ag_out, out_sem.at[2])
    ag_copy.start()
    g_copy(0, 3).wait()
    g_copy(1, 7).wait()
    ag_copy.wait()


def ffn_back(seqs, labels, vecs, saved, w1, w2, pool):
    rows, width = saved[0].shape
    ff = 4 * width
    anywhere = pl.BlockSpec(memory_space=pl.ANY)
    in_vmem = pl.BlockSpec(memory_space=pltpu.VMEM)
    wide = pltpu.VMEM((rows, width), bf16)
    return pl.pallas_call(
        functools.partial(ffn_back_kernel, seqs),
        out_shape=(
            jax.ShapeDtypeStruct((12, width, width), bf16),
            jax.ShapeDtypeStruct((rows, width), bf16),
            jax.ShapeDtypeStruct((16, width), f32),
            jax.ShapeDtypeStruct((16, 128), bf16),
        ),
        in_specs=[pl.BlockSpec(memory_space=pltpu.SMEM), in_vmem] + [anywhere] * (len(saved) + 3),
        out_specs=(anywhere, anywhere, in_vmem, in_vmem),
        scratch_shapes=[
            wide, wide, pltpu.VMEM((rows, ff), bf16), pltpu.VMEM((rows, ff), bf16), wide, wide,
            pltpu.VMEM((rows, 128), f32), pltpu.VMEM((16 * seqs, width), bf16),
            pltpu.VMEM(w1.shape, bf16), pltpu.VMEM(w2.shape, bf16), pltpu.VMEM(pool.shape, bf16),
            wide, pltpu.VMEM((rows, width), f32), wide, pltpu.VMEM((2, width, width), bf16), wide,
            pltpu.VMEM((16, 128), f32),
            pltpu.SemaphoreType.DMA((10 + seqs,)), pltpu.SemaphoreType.DMA((3,)),
        ],
        compiler_params=pltpu.CompilerParams(vmem_limit_bytes=58 * 2**20),
        cost_estimate=pl.CostEstimate(
            flops=8 * rows * width * ff, bytes_accessed=45 * 2**20, transcendentals=0
        ),
        name="ffn_back",
    )(labels, vecs, *saved, w1, w2, pool)


def attend_back_pair(q2, k2, v2, d2, logs, delta, length, keys):
    k2 = k2[:keys]
    v2 = v2[:keys]
    usable = lax.broadcasted_iota(jnp.int32, (keys, 1), 0) < length
    dq = dk = dv = None
    for which in (0, 1):
        lanes = head_lanes(which)
        qh = only(lanes, q2) * bf16(0.125)
        dh = only(lanes, d2)
        kh = only(lanes, k2) * bf16(0.125)
        scores = dot(k2, qh, NT)
        probs = jnp.where(usable, jnp.exp(scores - logs[which]), 0.0)
        prob_grad = dot(v2, dh, NT)
        score_grad = (probs * (prob_grad - delta[which])).astype(bf16)
        parts = (
            dot(score_grad, kh, TN),
            dot(score_grad, qh),
            dot(probs.astype(bf16), dh),
        )
        if dq is None:
            dq, dk, dv = parts
        else:
            dq, dk, dv = dq + parts[0], dk + parts[1], dv + parts[2]
    return dq, dk, dv


def attn_back_kernel(
    seqs, len_ref, ag_ref, g_in, q, k, v, att, x, stat, wq, wk, wv, wo,
    g_out, sg_out, sums_out,
    q_s, k_s, v_s, att_s, x_s, stat_s, wq_s, wk_s, wv_s, wo_s,
    dat_s, dq_s, dk_s, dv_s, rowt_s, gst, sg_s, in_sem, out_sem,
):
    rows = ag_ref.shape[0]
    one = rows // seqs
    z = lax.axis_index("seq")
    loads = copies(
        [
            (wo, wo_s), (att, att_s), (q, q_s), (k, k_s), (v, v_s), (stat, stat_s),
            (x, x_s), (wq, wq_s), (wk, wk_s), (wv, wv_s),
        ],
        in_sem,
    )
    for copy in loads:
        copy.start()
    loads[0].wait()

    @pl.loop(0, WIDTH // 256)
    def _(t):
        cols = tile(t, 256)
        dat_s[:, cols] = dot(ag_ref[...], wo_s[cols, :], NT).astype(bf16)

    def g_copy(unit):
        return pltpu.make_async_copy(gst.at[unit], g_out.at[8 + unit], out_sem.at[unit])

    loads[1].wait()

    @pl.loop(0, WIDTH // 256)
    def _(t):
        gst[0, tile(t, 256), :] = dot(att_s[:, tile(t, 256)], ag_ref[...], TN).astype(bf16)

    g_copy(0).start()
    for copy in loads[2:6]:
        copy.wait()
    head_of = lax.broadcasted_iota(jnp.int32, (16, WIDTH), 1) // HEAD_DIM
    picker = (head_of == lax.broadcasted_iota(jnp.int32, (16, WIDTH), 0)).astype(bf16)
    for s in range(seqs):
        part = pl.ds(s * one, one)
        product = dat_s[part, :].astype(f32) * att_s[part, :].astype(f32)
        high = product.astype(bf16)
        low = (product - high.astype(f32)).astype(bf16)
        rowt_s[s, 128:144, :] = dot(picker, high, NT) + dot(picker, low, NT)
        rowt_s[s, 0:128, :] = jnp.transpose(stat_s[part, :])
        length = len_ref[z * seqs + s]
        step = one // 4
        for n in range(4):
            keys = (n + 1) * step

            @pl.when((length > n * step) & (length <= (n + 1) * step))
            def _():
                @pl.loop(0, HEADS // 2)
                def _(p):
                    cols = tile(p, 128)
                    logs = [rowt_s[s, pl.ds(2 * p + w, 1), :] for w in (0, 1)]
                    delta = [rowt_s[s, pl.ds(128 + 2 * p + w, 1), :] for w in (0, 1)]
                    dq, dk, dv = attend_back_pair(
                        q_s[part, cols], k_s[part, cols], v_s[part, cols], dat_s[part, cols],
                        logs, delta, length, keys,
                    )
                    dq_s[part, cols] = dq.astype(bf16)
                    dk_s[pl.ds(s * one, keys), cols] = dk.astype(bf16)
                    dv_s[pl.ds(s * one, keys), cols] = dv.astype(bf16)
                    if keys < one:
                        rest = pl.ds(s * one + keys, one - keys)
                        dk_s[rest, cols] = jnp.zeros((one - keys, 128), bf16)
                        dv_s[rest, cols] = jnp.zeros((one - keys, 128), bf16)

    for copy in loads[6:]:
        copy.wait()

    @pl.loop(0, WIDTH // 256)
    def _(t):
        cols = tile(t, 256)
        total = ag_ref[:, cols].astype(f32)
        for d, w in ((dq_s, wq_s), (dk_s, wk_s), (dv_s, wv_s)):
            total = total + dot(d[...], w[cols, :], NT)
        sg_s[:, cols] = total.astype(bf16)
        sums_out[0:1, cols] = jnp.sum(dq_s[:, cols].astype(f32), axis=0, keepdims=True)
        sums_out[1:2, cols] = jnp.sum(dv_s[:, cols].astype(f32), axis=0, keepdims=True)
        sums_out[2:8, cols] = jnp.zeros((6, 256), f32)

    sg_copy = pltpu.make_async_copy(sg_s, sg_out, out_sem.at[4])
    sg_copy.start()
    for i, d in enumerate((dq_s, dk_s, dv_s)):

        @pl.loop(0, WIDTH // 256)
        def _(t):
            gst[1 + i, tile(t, 256), :] = dot(x_s[:, tile(t, 256)], d[...], TN).astype(bf16)

        g_copy(1 + i).start()
    for unit in range(4):
        g_copy(unit).wait()
    sg_copy.wait()


def attn_back(seqs, lengths, ag, g, saved, weights):
    rows, width = ag.shape
    one = rows // seqs
    anywhere = pl.BlockSpec(memory_space=pl.ANY)
    in_vmem = pl.BlockSpec(memory_space=pltpu.VMEM)
    wide = pltpu.VMEM((rows, width), bf16)
    square = pltpu.VMEM((width, width), bf16)
    return pl.pallas_call(
        functools.partial(attn_back_kernel, seqs),
        out_shape=(
            jax.ShapeDtypeStruct(g.shape, bf16),
            jax.ShapeDtypeStruct((rows, width), bf16),
            jax.ShapeDtypeStruct((8, width), f32),
        ),
        in_specs=[pl.BlockSpec(memory_space=pltpu.SMEM), in_vmem] + [anywhere] * (len(saved) + 5),
        out_specs=(anywhere, anywhere, in_vmem),
        input_output_aliases={2: 0},
        scratch_shapes=[wide] * 5
        + [pltpu.VMEM((rows, 128), f32)]
        + [square] * 4
        + [wide] * 4
        + [
            pltpu.VMEM((seqs, 144, one), f32), pltpu.VMEM((4, width, width), bf16), wide,
            pltpu.SemaphoreType.DMA((10,)), pltpu.SemaphoreType.DMA((5,)),
        ],
        compiler_params=pltpu.CompilerParams(vmem_limit_bytes=56 * 2**20),
        cost_estimate=pl.CostEstimate(
            flops=16 * rows * width * width + 10 * rows * one * width,
            bytes_accessed=25 * 2**20, transcendentals=12 * rows * one,
        ),
        name="attn_back",
    )(lengths, ag, g, *saved, *weights)


def place_of_block():
    return (lax.axis_index("batch") % 8) * 4 + lax.axis_index("seq")


def sum_kernel(
    seqs, chunks, pattern, lags, g_ref, small_ref, head_ref, y_ref, sg_ref,
    out_ref, small_out, head_out, lay_out, grad_out,
    acc, res, r0, r1, r2, r3, r4, sgot,
    rs_send, rs_recv, ag_send, ag_recv, loc, sm_send, sm_recv, hd_send, hd_recv,
    tok_send, tok_recv, tok_own,
):
    b = lax.axis_index("batch")
    z = lax.axis_index("seq")
    core = b % 2
    got = [r0, r1, r2, r3, r4]
    near_b = [flipped(b, 2), flipped(b, 4), b, b]
    near_z = [z, z, flipped(z, 1), flipped(z, 2)]
    mine = [(b // 2) % 2, (b // 4) % 2, z % 2, (z // 2) % 2]
    orders = {"x": (0, 1, 2, 3), "y": (1, 0, 2, 3)}
    period = len(pattern)

    def direction(c, level):
        code = c % period
        dirs = [orders[p][level] for p in pattern]
        return (
            pick(code, [near_b[d] for d in dirs]),
            pick(code, [near_z[d] for d in dirs]),
            pick(code, [mine[d] for d in dirs]),
        )

    core_partner = (flipped(b, 1), z)
    barrier = pltpu.get_barrier_semaphore()
    partners = [(near_b[2], near_z[2]), (near_b[3], near_z[3]), core_partner]
    partners += [(near_b[0], near_z[0]), (near_b[1], near_z[1])]
    greeted = [core_partner, (near_b[0], near_z[0]), (near_b[1], near_z[1])] + greet_line()
    for who in greeted:
        pl.semaphore_signal(barrier, inc=1, device_id=who, device_id_type=MESH)
    pl.semaphore_wait(barrier, len(greeted))

    tokens = lay_out.shape[1]
    count = lax.axis_size("seq")
    moves = []
    own = []
    for i, (src, dst) in enumerate(((y_ref, lay_out), (sg_ref, grad_out))):
        for s in range(seqs):
            base_sem = i * seqs * (count - 1)
            moves += spread(src, dst, seqs, tokens, False, tok_send, tok_recv, base_sem, s)
            own.append(own_part(src, dst, seqs, tokens, False, tok_own.at[i * seqs + s], s))
    for copy in own:
        copy.start()
    half_moves = len(moves) // 2
    move_ticks = [i for i in range(half_moves)] + [12 + 4 * i for i in range(half_moves)]

    def base(c, level):
        rows = 0
        size = CHUNK
        for l in range(level):
            size = size // 2
            rows = rows + direction(c, l)[2] * size
        return pl.multiple_of(rows, 16)

    def g_rows(c):
        return pl.ds(pl.multiple_of(c * CHUNK, CHUNK), CHUNK)

    my_cols = pl.ds(pl.multiple_of(core * HALF, HALF), HALF)
    other_cols = pl.ds(pl.multiple_of((1 - core) * HALF, HALF), HALF)

    def rs_copy(c, s):
        if s == 0:
            return pltpu.make_async_remote_copy(
                g_ref.at[g_rows(c), other_cols], r0.at[c], rs_send.at[0, c], rs_recv.at[0, c],
                device_id=core_partner, device_id_type=MESH,
            )
        size = CHUNK >> s
        nb, nz, m = direction(c, s - 1)
        start = pl.multiple_of(base(c, s - 1) + (1 - m) * size, 16)
        return pltpu.make_async_remote_copy(
            acc.at[c, pl.ds(start, size)], got[s].at[c], rs_send.at[s, c], rs_recv.at[s, c],
            device_id=(nb, nz), device_id_type=MESH,
        )

    def ag_copy(c, s):
        if s == 0:
            return pltpu.make_async_remote_copy(
                res.at[c], out_ref.at[g_rows(c), my_cols], ag_send.at[0, c], ag_recv.at[0, c],
                device_id=core_partner, device_id_type=MESH,
            )
        size = CHUNK >> s
        nb, nz, _ = direction(c, s - 1)
        start = base(c, s)
        return pltpu.make_async_remote_copy(
            res.at[c, pl.ds(start, size)], res.at[c, pl.ds(start, size)],
            ag_send.at[s, c], ag_recv.at[s, c], device_id=(nb, nz), device_id_type=MESH,
        )

    def loc_in(c):
        return pltpu.make_async_copy(g_ref.at[g_rows(c), my_cols], acc.at[c], loc.at[0, c])

    def loc_out(c):
        return pltpu.make_async_copy(res.at[c], out_ref.at[g_rows(c), my_cols], loc.at[1, c])

    def stage_first(c):
        rs_copy(c, 0).start()
        loc_in(c).start()

    def stage_scatter(s, c):
        rs_copy(c, s - 1).wait_recv()
        if s == 1:
            loc_in(c).wait()
        half = CHUNK >> s
        start = base(c, s - 1)
        m = direction(c, s - 1)[2]
        for which in (0, 1):
            off = pl.multiple_of(((1 - m) if which == 0 else m) * half, 16)
            rows = pl.ds(pl.multiple_of(start + off, 16), half)
            acc[c, rows] = acc[c, rows] + got[s - 1][c, pl.ds(off, half)]
            if which == 0:
                rs_copy(c, s).start()

    def stage_turn(c):
        rs_copy(c, 4).wait_recv()
        rows = pl.ds(base(c, 4), 16)
        res[c, rows] = acc[c, rows] + r4[c]
        ag_copy(c, 4).start()

    def stage_gather(s, c):
        ag_copy(c, s + 1).wait_recv()
        ag_copy(c, s).start()
        if s == 0:
            loc_out(c).start()

    def stage_last(c):
        ag_copy(c, 0).wait_recv()
        loc_out(c).wait()
        for s in range(5):
            rs_copy(c, s).wait_send()
            ag_copy(c, s).wait_send()

    stages = (
        [stage_first]
        + [functools.partial(stage_scatter, s) for s in (1, 2, 3, 4)]
        + [stage_turn]
        + [functools.partial(stage_gather, s) for s in (3, 2, 1, 0)]
        + [stage_last]
    )

    place = place_of_block()

    def small_copies(i):
        first = place - place % (1 << i)
        part = pl.ds(first, 1 << i)
        return (
            pltpu.make_async_remote_copy(
                small_out, sgot.at[i], sm_send.at[i], sm_recv.at[i],
                device_id=partners[i], device_id_type=MESH,
            ),
            pltpu.make_async_remote_copy(
                head_out.at[part], head_out.at[part], hd_send.at[i], hd_recv.at[i],
                device_id=partners[i], device_id_type=MESH,
            ),
        )

    small_out[...] = small_ref[...]
    head_out[place] = head_ref[...]

    def tick(t, carry):
        for when, copy in zip(move_ticks, moves):

            @pl.when(t == when)
            def _():
                copy.start()

        for i in range(len(partners) + 1):

            @pl.when(t == 3 * i)
            def _():
                if i > 0:
                    for copy in small_copies(i - 1):
                        copy.wait()
                    small_out[...] = small_out[...] + sgot[i - 1]
                if i < len(partners):
                    for copy in small_copies(i):
                        copy.start()

        for stage, lag in reversed(list(zip(stages, lags))):
            c = t - lag

            @pl.when((c >= 0) & (c < chunks))
            def _():
                stage(c)

        return carry

    lax.fori_loop(0, chunks + lags[-1], tick, 0)
    for copy in own + moves:
        copy.wait()


def sum_all(seqs, g, small, head, y, sg, tokens):
    width = g.shape[-1]
    flat = g.reshape(-1, width)
    chunks = flat.shape[0] // CHUNK
    count = lax.axis_size("seq")
    group = seqs * count
    moves = 2 * seqs * (count - 1)
    dma = pltpu.SemaphoreType.DMA
    anywhere = pl.BlockSpec(memory_space=pl.ANY)
    in_vmem = pl.BlockSpec(memory_space=pltpu.VMEM)
    block = jax.ShapeDtypeStruct((group, tokens, width), bf16)
    total, small, head, lay, grad = pl.pallas_call(
        functools.partial(sum_kernel, seqs, chunks, "xy", tuple(3 * i for i in range(11))),
        out_shape=(
            jax.ShapeDtypeStruct(flat.shape, bf16),
            jax.ShapeDtypeStruct(small.shape, f32),
            jax.ShapeDtypeStruct((32,) + head.shape, bf16),
            block,
            block,
        ),
        in_specs=[anywhere, in_vmem, in_vmem, anywhere, anywhere],
        out_specs=(anywhere, in_vmem, in_vmem, anywhere, anywhere),
        scratch_shapes=[
            pltpu.VMEM((chunks, CHUNK, HALF), bf16),
            pltpu.VMEM((chunks, CHUNK, HALF), bf16),
            pltpu.VMEM((chunks, CHUNK, HALF), bf16),
            pltpu.VMEM((chunks, CHUNK // 2, HALF), bf16),
            pltpu.VMEM((chunks, CHUNK // 4, HALF), bf16),
            pltpu.VMEM((chunks, CHUNK // 8, HALF), bf16),
            pltpu.VMEM((chunks, CHUNK // 16, HALF), bf16),
            pltpu.VMEM((5,) + small.shape, f32),
            dma((5, chunks)),
            dma((5, chunks)),
            dma((5, chunks)),
            dma((5, chunks)),
            dma((2, chunks)),
            dma((5,)),
            dma((5,)),
            dma((5,)),
            dma((5,)),
            dma((moves,)),
            dma((moves,)),
            dma((2 * seqs,)),
        ],
        compiler_params=pltpu.CompilerParams(
            collective_id=0, has_side_effects=True, vmem_limit_bytes=56 * 2**20
        ),
        name="sum_gradients",
    )(flat, small, head, y, sg)
    blocks = lax.axis_size("batch") // 8
    if blocks > 1:
        alike = [[i + 8 * j for j in range(blocks)] for i in range(8)]
        total = lax.psum(total, "batch", axis_index_groups=alike)
        small = lax.psum(small, "batch", axis_index_groups=alike)
        head = lax.all_gather(head, "batch", axis_index_groups=alike, axis=0, tiled=True)
    return total.reshape(g.shape), small, head, lay, grad


def finish_kernel(
    total, small_ref, cls_ref, label_ref, vec_ref, pool_ref, lay_in, grad_in,
    lay_out, loss_out, grad_out, gq, gk, gv, go, gqb, gvb, gob, gg1, gb1, gin, gib, gou, gub,
    gg2, gb2, gpool, gpb, gcp, gcb,
    low_s, full_s, pool_s, pass_s, in_sem, out_sem,
):
    units = low_s.shape[0]
    group = loss_out.shape[0]
    seqs = cls_ref.shape[0]
    loads = [pltpu.make_async_copy(total.at[u], low_s.at[u], in_sem.at[u]) for u in range(units)]
    for copy in loads:
        copy.start()
    places = (
        [gou.at[pl.ds(j * WIDTH, WIDTH)] for j in range(4)]
        + [gin.at[:, pl.ds(j * WIDTH, WIDTH)] for j in range(4)]
        + [go, gq, gk, gv]
    )
    stores = [
        pltpu.make_async_copy(full_s.at[u], places[u], out_sem.at[u]) for u in range(units)
    ]
    passed_in = [
        pltpu.make_async_copy(src, pass_s.at[i], in_sem.at[units + i])
        for i, src in enumerate((lay_in, grad_in))
    ]
    passed = [
        pltpu.make_async_copy(pass_s.at[i], dst, out_sem.at[units + i])
        for i, dst in enumerate((lay_out, grad_out))
    ]
    for copy in passed_in:
        copy.start()
    pool_store = pltpu.make_async_copy(pool_s, gpool, out_sem.at[units + 2])

    def widen(u):
        loads[u].wait()

        @pl.loop(0, WIDTH // 128)
        def _(i):
            r = tile(i, 128)
            full_s[u, r, :] = low_s[u, r, :].astype(f32)

        stores[u].start()

    for u in range(4):
        widen(u)
    for before, after in zip(passed_in, passed):
        before.wait()
        after.start()

    def exact(left, right, dims=NN):
        return lax.dot_general(left, right, dims, precision=highest, preferred_element_type=f32)

    pooled = jnp.tanh(dot(cls_ref[...], pool_ref[...]) + vec_ref[PB : PB + 1, :])
    row = lax.broadcasted_iota(jnp.int32, (8, 1), 0)
    class_rows = jnp.where(row < 3, vec_ref[CP : CP + 8, :], 0.0)
    picked = jnp.where(
        row == lax.broadcasted_iota(jnp.int32, (8, 128), 1), vec_ref[CB : CB + 1, 0:128], 0.0
    )
    logits = exact(class_rows, pooled, NT) + jnp.sum(picked, axis=-1, keepdims=True)
    logits = jnp.where(row < 3, logits, masked_fill)
    top = jnp.max(logits, axis=0, keepdims=True)
    raised = jnp.exp(logits - top)
    total_row = jnp.sum(raised, axis=0, keepdims=True)
    chosen = (row == label_ref[...]).astype(f32)
    losses = (top + jnp.log(total_row)) - jnp.sum(
        jnp.where(chosen > 0.0, logits, 0.0), axis=0, keepdims=True
    )
    logit_grad = raised / total_row - chosen
    first = lax.axis_index("batch") * group
    pickers = (
        lax.broadcasted_iota(jnp.int32, (seqs, 128), 0)
        == lax.broadcasted_iota(jnp.int32, (seqs, 128), 1) + first
    ).astype(f32)
    loss_out[...] = exact(losses, pickers)[0, 0:group]
    pre = exact(logit_grad, class_rows, TN) * (1.0 - pooled * pooled)
    ones = jnp.ones((1, seqs), f32)
    gcb[...] = exact(ones, logit_grad, NT)[0, 0:3]
    gpb[...] = jnp.sum(pre, axis=0)
    gcp[...] = exact(pooled, logit_grad, (((0,), (1,)), ((), ())))[:, 0:3]
    high = pre.astype(bf16)
    rest = pre - high.astype(f32)
    mid = rest.astype(bf16)
    low = (rest - mid.astype(f32)).astype(bf16)
    for j in range(3):
        cols = pl.ds(j * 256, 256)
        cls = cls_ref[:, cols]
        pool_s[cols, :] = dot(cls, high, TN) + dot(cls, mid, TN) + dot(cls, low, TN)
    pool_store.start()
    for i, ref in (
        (QB, gqb), (VB, gvb), (OB, gob), (G1, gg1), (B1, gb1), (UB, gub), (G2, gg2), (B2, gb2),
    ):
        ref[...] = small_ref[i, :]
    for j in range(4):
        gib[j * WIDTH : (j + 1) * WIDTH] = small_ref[IB + j, :]
    for u in range(4, units):
        widen(u)
    for copy in stores + passed + [pool_store]:
        copy.wait()


def finish(total, small, cls, labels, vecs, pool, lay, grad):
    group, tokens, width = lay.shape
    anywhere = pl.BlockSpec(memory_space=pl.ANY)
    in_vmem = pl.BlockSpec(memory_space=pltpu.VMEM)
    square = ((width, width), f32, anywhere)
    row = ((width,), f32, in_vmem)
    outs = (
        [(lay.shape, bf16, anywhere), ((group,), f32, in_vmem), (grad.shape, bf16, anywhere)]
        + [square] * 4
        + [row] * 5
        + [((width, 4 * width), f32, anywhere), ((4 * width,), f32, in_vmem)]
        + [((4 * width, width), f32, anywhere), row, row, row]
        + [square, row, ((width, 3), f32, in_vmem), ((3,), f32, in_vmem)]
    )
    units = total.shape[0]
    return pl.pallas_call(
        finish_kernel,
        out_shape=tuple(jax.ShapeDtypeStruct(s, t) for s, t, _ in outs),
        in_specs=[anywhere] + [in_vmem] * 5 + [anywhere, anywhere],
        out_specs=tuple(m for _, _, m in outs),
        scratch_shapes=[
            pltpu.VMEM((units, width, width), bf16), pltpu.VMEM((units, width, width), f32),
            pltpu.VMEM((width, width), f32), pltpu.VMEM((2,) + lay.shape, bf16),
            pltpu.SemaphoreType.DMA((units + 2,)), pltpu.SemaphoreType.DMA((units + 3,)),
        ],
        compiler_params=pltpu.CompilerParams(vmem_limit_bytes=60 * 2**20),
        name="finish",
    )(total, small, cls, labels, vecs, pool, lay, grad)


def local(
    states, lengths, labels, cotangent,
    query_proj, key_proj, value_proj, output_proj,
    query_bias, value_bias, output_bias, first_gain, first_bias,
    inner_proj, inner_bias, outer_proj, outer_bias, second_gain, second_bias,
    pool_proj, pool_bias, class_proj, class_bias,
):
    group, tokens, width = states.shape
    seqs = group // lax.axis_size("seq")
    (
        vecs, x, upstream, q, k, v, att, n1, low, hid, slope, n2, stat, y,
    ) = forward(
        lengths, states, cotangent,
        (query_proj, key_proj, value_proj, output_proj, inner_proj, outer_proj),
        (query_bias, value_bias, output_bias, first_gain, first_bias, inner_bias, outer_bias,
         second_gain, second_bias, pool_bias, class_proj, class_bias),
    )
    g, attn_grad, sums_ffn, head = ffn_back(
        seqs, labels, vecs, (upstream, n2, hid, slope, low, n1, stat, y),
        inner_proj, outer_proj, pool_proj,
    )
    g, states_rows, sums_attn = attn_back(
        seqs, lengths, attn_grad, g, (q, k, v, att, x, stat),
        (query_proj, key_proj, value_proj, output_proj),
    )
    small = jnp.concatenate([sums_attn[0:2], sums_ffn[2:12], jnp.zeros((4, width), f32)])
    total, small, head, lay, grad = sum_all(seqs, g, small, head, y, states_rows, tokens)
    cls = head[:, 0 : 6 * seqs].reshape(-1, width)
    label_row = head[:, 6 * seqs, 0:seqs].reshape(1, -1).astype(jnp.int32)
    return finish(total, small, cls, label_row, vecs, pool_proj, lay, grad)


def solution(mesh):
    split = P("batch", "seq", None)
    in_specs = (split, P("batch"), P("batch"), split) + (P(),) * 19
    out_specs = (split, P("batch"), split) + (P(),) * 19
    return jax.shard_map(local, mesh=mesh, in_specs=in_specs, out_specs=out_specs, check_vma=False)
```

time: 608 us -> 387 us (0.64); the launches traced: 597 us -> 384 us
  Pallas kernels: 141 us -> 375 us
  matrix products: 169 us -> 0 us
  local copies, waits for them, and re-layouts: 98.1 us -> 6.37 us
  blocking collectives: 69.6 us -> 0 us
  starting transfers between devices: 49.4 us -> 0 us
  waiting for transfers between devices: 43 us -> 0 us
  other arithmetic: 24.2 us -> 1.6 us
    pallas_call x1 -> x5, Pallas kernels: 141 us -> 375 us  [the longest x1 189 us: sum_all(): pl.pallas_call(functools.partial(sum_kernel, seqs, chunks, 'xy', tuple((3...]
    dot_general x32 -> x0, matrix products: 152 us -> none  [the longest x6 32.5 us: project_right(): return jnp.einsum('to,io->ti', left, right, preferred_element_type=f32)]
    all_gather x1 -> x0, blocking collectives: 60.9 us -> none  [local(): lax.all_gather(cls_own, ('batch', 'seq'), axis=0, tiled=True).astype(f32)]
    ppermute x12 -> x0, starting transfers between devices: 49.4 us -> none  [shifted(): return lax.ppermute(block, 'seq', route)]
    ppermute x12 -> x0, waiting for transfers between devices: 43 us -> none  [shifted(): return lax.ppermute(block, 'seq', route)]
    reshape x8 -> x1, local copies, waits for them, and re-layouts: 26 us -> 1.65 us  [local(): cls = head[:, 0:6 * seqs].reshape(-1, width)]
    slice x5 -> x2, local copies, waits for them, and re-layouts: 19 us -> 0.75 us  [the longest x1 0.74 us: local(): sums_attn[0:2]]
    sub x1 -> x0, matrix products: 17.1 us -> none  [local(): weights_exp = jnp.where(usable, jnp.exp(masked - row_top), 0.0)]
  transfers between devices with their start and end apart: 12 -> 0, of which waited for: 4 -> 0; matrix products, arithmetic and copies ran while one was open for 8% -> 0% of each run, Pallas kernels for 0% -> 0%
where the time goes in v2:
time: 387 us; the launch traced here: 384 us
  Pallas kernels  375 us (97%)
  local copies, waits for them, and re-layouts  6.37 us (2%)
    pallas_call x1, Pallas kernels, sum_all(): pl.pallas_call(functools.partial(sum_kernel, seqs, chunks, 'xy', tuple((3...  189 us
    pallas_call x1, Pallas kernels, forward(): pl.pallas_call(functools.partial(forward_kernel, seqs), out_shape=tuple((...  73.3 us
    pallas_call x1, Pallas kernels, attn_back(): pl.pallas_call(functools.partial(attn_back_kernel, seqs), out_shape=(jax....  45.9 us
    pallas_call x1, Pallas kernels, ffn_back(): pl.pallas_call(functools.partial(ffn_back_kernel, seqs), out_shape=(jax.S...  44.9 us
    pallas_call x1, Pallas kernels, finish(): pl.pallas_call(finish_kernel, out_shape=tuple((jax.ShapeDtypeStruct(s, t)...  21.3 us

profile of v2, /device:TPU:1, one launch (start us, length us, event | category | flops | bytes accessed | tf_op | source)
XLA Modules:
  0.0 383.8 jit_solution(1765056964467383421)
XLA Ops:
  0.7 0.1 pad.2.clone
  0.7 1.5 copy.48.class_proj
  2.3 73.3 %forward.1 = (f32[24,768]{1,0:T(8,128)}, bf16[1024,768]{1,0:T(8,128)(2,1)}, bf16[1024,768]{1,0:T(8,128)(2,1)}, bf16[1024,768]{1,0:T(8,128)(2,1)}, bf16[1024,768]...) custom-call(s32[8]{0:T(128)} %len_ref.3, ...), custom_call_target="tpu_custom_call" | custom-call | flops 16106127360 | bytes 52428800 | tf_op jit(solution)/shard_map/forward/pallas_call | solution.py:344
  75.6 44.9 %ffn_back.1 = (bf16[12,768,768]{2,1,0:T(8,128)(2,1)}, bf16[1024,768]{1,0:T(8,128)(2,1)}, f32[16,768]{1,0:T(8,128)}, bf16[16,128]{1,0:T(8,128)(2,1)}) custom-call(s32[8]{0:T(128)} %label_ref.1, f32[24,768]{1,0:T(8,128)} %get-tuple-element.48.vec_ref, bf16[1024,768]{1,0:T(8,128)(2,1)} %get-tuple-element.49.cot, bf16[1024,768]{1,0:T(8,128)(2,1)} %get-tuple-element.50.n2, ...), custom_call_target="tpu_custom_call" | custom-call | flops 19327352832 | bytes 47185920 | tf_op jit(solution)/shard_map/ffn_back/pallas_call | solution.py:522
  120.5 0.0 copy-start
  120.5 45.9 %attn_back.1 = (bf16[12,768,768]{2,1,0:T(8,128)(2,1)}, bf16[1024,768]{1,0:T(8,128)(2,1)}, f32[8,768]{1,0:T(8,128)}) custom-call(s32[8]{0:T(128)} %len_ref.3, bf16[1024,768]{1,0:T(8,128)(2,1)} %get-tuple-element.57.ag_ref, bf16[12,768,768]{2,1,0:T(8,128)(2,1)} %get-tuple-element.58.g_in, ...), custom_call_target="tpu_custom_call", output_to_operand_aliasing={{0}: (2, {})} | custom-call | flops 13690208256 | bytes 26214400 | tf_op jit(solution)/shard_map/attn_back/pallas_call | solution.py:679
  166.4 0.7 slice.12
  167.2 0.0 copy-done
  167.2 0.7 maximum_maximum_fusion.small_ref
  167.9 189.5 %sum_gradients.1 = (bf16[9216,768]{1,0:T(8,128)(2,1)}, f32[16,768]{1,0:T(8,128)}, bf16[32,16,128]{2,1,0:T(8,128)(2,1)}, bf16[8,128,768]{2,1,0:T(8,128)(2,1)}, bf16[8,128,768]{2,1,0:T(8,128)(2,1)}) custom-call(bf16[9216,768]{1,0:T(8,128)(2,1)} %bitcast.4, f32[16,768]{1,0:T(8,128)} %maximum_maximum_fusion.small_ref, ...), custom_call_target="tpu_custom_call" | custom-call | tf_op jit(solution)/shard_map/sum_gradients/pallas_call | solution.py:915
  357.3 0.9 convert_reduce_fusion
  358.2 0.6 reshape.70.label_ref
  358.9 1.6 reshape.69.cls_ref
  360.5 21.3 %finish.1 = (bf16[8,128,768]{2,1,0:T(8,128)(2,1)}, f32[8]{0:T(128)}, bf16[8,128,768]{2,1,0:T(8,128)(2,1)}, f32[768,768]{1,0:T(8,128)}, f32[768,768]{1,0:T(8,128)...) custom-call(bf16[12,768,768]{2,1,0:T(8,128)(2,1)} %bitcast.3, ...), custom_call_target="tpu_custom_call" | custom-call | tf_op jit(solution)/shard_map/finish/pallas_call | solution.py:1076
  381.8 1.7 copy.49
  (2 shorter events, 0.0 us)
Async XLA Ops:
  120.5 46.7 %copy-start = (f32[16,768]{1,0:T(8,128)S(1)}, f32[16,768]{1,0:T(8,128)}, u32[]{:S(2)}) copy-start(f32[16,768]{1,0:T(8,128)} %get-tuple-element.66) | copy-start | bytes 147460

commit v3 on v2

--- a/solution.py
+++ b/solution.py
@@ -385,166 +385,6 @@
     return dot(high, pool_s[...], NT) + dot(mid, pool_s[...], NT) + dot(low, pool_s[...], NT)
 
 
-def ffn_back_kernel(
-    seqs, label_ref, vec_ref, cot, n2, hid, slope, low, n1, stat, y, w1, w2, pool,
-    g_out, ag_out, sums_out, head_out,
-    cot_s, n2_s, hid_s, slope_s, low_s, n1_s, stat_s, cls_s, w1_s, w2_s, pool_s,
-    pg_s, fg_s, eg_s, gst, ag_s, row_s, in_sem, out_sem,
-):
-    rows = cot_s.shape[0]
-    one = rows // seqs
-    cls_in = [
-        pltpu.make_async_copy(
-            y.at[pl.ds(s * one, 16)], cls_s.at[pl.ds(s * 16, 16)], in_sem.at[10 + s]
-        )
-        for s in range(seqs)
-    ]
-    loads = copies(
-        [
-            (pool, pool_s), (cot, cot_s), (n2, n2_s), (stat, stat_s), (w2, w2_s), (hid, hid_s),
-            (slope, slope_s), (low, low_s), (w1, w1_s), (n1, n1_s),
-        ],
-        in_sem,
-    )
-    for copy in cls_in + loads:
-        copy.start()
-    for copy in cls_in:
-        copy.wait()
-    loads[0].wait()
-    z = lax.axis_index("seq")
-    place = lax.broadcasted_iota(jnp.int32, (16 * seqs, 1), 0)
-    labels = jnp.zeros((16 * seqs, 1), jnp.int32)
-    label_row = jnp.zeros((1, 128), f32)
-    lane = lax.broadcasted_iota(jnp.int32, (1, 128), 1)
-    for s in range(seqs):
-        label = label_ref[z * seqs + s]
-        labels = jnp.where(place == 16 * s, label, labels)
-        label_row = jnp.where(lane == s, label.astype(f32), label_row)
-    cls_grad = exit_back(cls_s[...], labels, vec_ref, pool_s)
-    row_s[...] = jnp.zeros_like(row_s)
-    for s in range(seqs):
-        first = cls_s[16 * s : 16 * (s + 1), :].astype(f32)
-        for j in range(6):
-            row_s[s * 6 + j : s * 6 + j + 1, :] = first[0:1, j * 128 : (j + 1) * 128]
-    row_s[12:13, :] = label_row
-    head_out[...] = row_s[...].astype(bf16)
-    for copy in loads[1:4]:
-        copy.wait()
-    sums_out[...] = jnp.zeros_like(sums_out)
-    ROW = 128
-
-    def add_sum(index, block):
-        sums_out[index : index + 1, :] += jnp.sum(block, axis=0, keepdims=True)
-
-    @pl.loop(0, rows // ROW)
-    def _(i):
-        r = tile(i, ROW)
-        upstream = cot_s[r, :].astype(f32)
-        place = lax.broadcasted_iota(jnp.int32, (ROW, 1), 0) + i * ROW
-        for s in range(seqs):
-            upstream = upstream + jnp.where(place == s * one, cls_grad[16 * s : 16 * s + 1, :], 0.0)
-        normed = n2_s[r, :].astype(f32)
-        add_sum(G2, upstream * normed)
-        add_sum(B2, upstream)
-        zg = norm_rows_back(upstream, normed, stat_s[r, 13:14], vec_ref[G2 : G2 + 1, :])
-        low = zg.astype(bf16)
-        pg_s[r, :] = low
-        add_sum(UB, low.astype(f32))
-        fg_s[r, :] = zg
-
-    for copy in loads[4:9]:
-        copy.wait()
-
-    def g_copy(slot, unit):
-        return pltpu.make_async_copy(gst.at[slot], g_out.at[unit], out_sem.at[slot])
-
-    for j in range(4):
-
-        @pl.loop(0, WIDTH // 256)
-        def _(t):
-            cols = tile(t, 256)
-            ff = pl.ds(pl.multiple_of(j * WIDTH + t * 256, 256), 256)
-            grad = dot(pg_s[...], w2_s[ff, :], NT) * slope_s[:, ff].astype(f32)
-            low = grad.astype(bf16)
-            eg_s[:, cols] = low
-            sums_out[IB + j : IB + j + 1, cols] = jnp.sum(low.astype(f32), axis=0, keepdims=True)
-
-        if j > 0:
-            g_copy(0, j - 1).wait()
-
-        @pl.loop(0, WIDTH // 256)
-        def _(t):
-            ff = pl.ds(pl.multiple_of(j * WIDTH + t * 256, 256), 256)
-            gst[0, tile(t, 256), :] = dot(hid_s[:, ff], pg_s[...], TN).astype(bf16)
-
-        g_copy(0, j).start()
-        if j > 0:
-            g_copy(1, 4 + j - 1).wait()
-
-        @pl.loop(0, WIDTH // 256)
-        def _(t):
-            gst[1, tile(t, 256), :] = dot(low_s[:, tile(t, 256)], eg_s[...], TN).astype(bf16)
-
-        g_copy(1, 4 + j).start()
-
-        @pl.loop(0, WIDTH // 256)
-        def _(t):
-            cols = tile(t, 256)
-            fg_s[:, cols] += dot(eg_s[...], w1_s[cols, j * WIDTH : (j + 1) * WIDTH], NT)
-
-    loads[9].wait()
-
-    @pl.loop(0, rows // ROW)
-    def _(i):
-        r = tile(i, ROW)
-        upstream = fg_s[r, :]
-        normed = n1_s[r, :].astype(f32)
-        add_sum(G1, upstream * normed)
-        add_sum(B1, upstream)
-        zg = norm_rows_back(upstream, normed, stat_s[r, 12:13], vec_ref[G1 : G1 + 1, :])
-        low = zg.astype(bf16)
-        ag_s[r, :] = low
-        add_sum(OB, low.astype(f32))
-
-    ag_copy = pltpu.make_async_copy(ag_s, ag_out, out_sem.at[2])
-    ag_copy.start()
-    g_copy(0, 3).wait()
-    g_copy(1, 7).wait()
-    ag_copy.wait()
-
-
-def ffn_back(seqs, labels, vecs, saved, w1, w2, pool):
-    rows, width = saved[0].shape
-    ff = 4 * width
-    anywhere = pl.BlockSpec(memory_space=pl.ANY)
-    in_vmem = pl.BlockSpec(memory_space=pltpu.VMEM)
-    wide = pltpu.VMEM((rows, width), bf16)
-    return pl.pallas_call(
-        functools.partial(ffn_back_kernel, seqs),
-        out_shape=(
-            jax.ShapeDtypeStruct((12, width, width), bf16),
-            jax.ShapeDtypeStruct((rows, width), bf16),
-            jax.ShapeDtypeStruct((16, width), f32),
-            jax.ShapeDtypeStruct((16, 128), bf16),
-        ),
-        in_specs=[pl.BlockSpec(memory_space=pltpu.SMEM), in_vmem] + [anywhere] * (len(saved) + 3),
-        out_specs=(anywhere, anywhere, in_vmem, in_vmem),
-        scratch_shapes=[
-            wide, wide, pltpu.VMEM((rows, ff), bf16), pltpu.VMEM((rows, ff), bf16), wide, wide,
-            pltpu.VMEM((rows, 128), f32), pltpu.VMEM((16 * seqs, width), bf16),
-            pltpu.VMEM(w1.shape, bf16), pltpu.VMEM(w2.shape, bf16), pltpu.VMEM(pool.shape, bf16),
-            wide, pltpu.VMEM((rows, width), f32), wide, pltpu.VMEM((2, width, width), bf16), wide,
-            pltpu.VMEM((16, 128), f32),
-            pltpu.SemaphoreType.DMA((10 + seqs,)), pltpu.SemaphoreType.DMA((3,)),
-        ],
-        compiler_params=pltpu.CompilerParams(vmem_limit_bytes=58 * 2**20),
-        cost_estimate=pl.CostEstimate(
-            flops=8 * rows * width * ff, bytes_accessed=45 * 2**20, transcendentals=0
-        ),
-        name="ffn_back",
-    )(labels, vecs, *saved, w1, w2, pool)
-
-
 def attend_back_pair(q2, k2, v2, d2, logs, delta, length, keys):
     k2 = k2[:keys]
     v2 = v2[:keys]
@@ -571,153 +411,30 @@
     return dq, dk, dv
 
 
-def attn_back_kernel(
-    seqs, len_ref, ag_ref, g_in, q, k, v, att, x, stat, wq, wk, wv, wo,
-    g_out, sg_out, sums_out,
-    q_s, k_s, v_s, att_s, x_s, stat_s, wq_s, wk_s, wv_s, wo_s,
-    dat_s, dq_s, dk_s, dv_s, rowt_s, gst, sg_s, in_sem, out_sem,
-):
-    rows = ag_ref.shape[0]
-    one = rows // seqs
-    z = lax.axis_index("seq")
-    loads = copies(
-        [
-            (wo, wo_s), (att, att_s), (q, q_s), (k, k_s), (v, v_s), (stat, stat_s),
-            (x, x_s), (wq, wq_s), (wk, wk_s), (wv, wv_s),
-        ],
-        in_sem,
-    )
-    for copy in loads:
-        copy.start()
-    loads[0].wait()
-
-    @pl.loop(0, WIDTH // 256)
-    def _(t):
-        cols = tile(t, 256)
-        dat_s[:, cols] = dot(ag_ref[...], wo_s[cols, :], NT).astype(bf16)
-
-    def g_copy(unit):
-        return pltpu.make_async_copy(gst.at[unit], g_out.at[8 + unit], out_sem.at[unit])
-
-    loads[1].wait()
-
-    @pl.loop(0, WIDTH // 256)
-    def _(t):
-        gst[0, tile(t, 256), :] = dot(att_s[:, tile(t, 256)], ag_ref[...], TN).astype(bf16)
-
-    g_copy(0).start()
-    for copy in loads[2:6]:
-        copy.wait()
-    head_of = lax.broadcasted_iota(jnp.int32, (16, WIDTH), 1) // HEAD_DIM
-    picker = (head_of == lax.broadcasted_iota(jnp.int32, (16, WIDTH), 0)).astype(bf16)
-    for s in range(seqs):
-        part = pl.ds(s * one, one)
-        product = dat_s[part, :].astype(f32) * att_s[part, :].astype(f32)
-        high = product.astype(bf16)
-        low = (product - high.astype(f32)).astype(bf16)
-        rowt_s[s, 128:144, :] = dot(picker, high, NT) + dot(picker, low, NT)
-        rowt_s[s, 0:128, :] = jnp.transpose(stat_s[part, :])
-        length = len_ref[z * seqs + s]
-        step = one // 4
-        for n in range(4):
-            keys = (n + 1) * step
-
-            @pl.when((length > n * step) & (length <= (n + 1) * step))
-            def _():
-                @pl.loop(0, HEADS // 2)
-                def _(p):
-                    cols = tile(p, 128)
-                    logs = [rowt_s[s, pl.ds(2 * p + w, 1), :] for w in (0, 1)]
-                    delta = [rowt_s[s, pl.ds(128 + 2 * p + w, 1), :] for w in (0, 1)]
-                    dq, dk, dv = attend_back_pair(
-                        q_s[part, cols], k_s[part, cols], v_s[part, cols], dat_s[part, cols],
-                        logs, delta, length, keys,
-                    )
-                    dq_s[part, cols] = dq.astype(bf16)
-                    dk_s[pl.ds(s * one, keys), cols] = dk.astype(bf16)
-                    dv_s[pl.ds(s * one, keys), cols] = dv.astype(bf16)
-                    if keys < one:
-                        rest = pl.ds(s * one + keys, one - keys)
-                        dk_s[rest, cols] = jnp.zeros((one - keys, 128), bf16)
-                        dv_s[rest, cols] = jnp.zeros((one - keys, 128), bf16)
-
-    for copy in loads[6:]:
-        copy.wait()
-
-    @pl.loop(0, WIDTH // 256)
-    def _(t):
-        cols = tile(t, 256)
-        total = ag_ref[:, cols].astype(f32)
-        for d, w in ((dq_s, wq_s), (dk_s, wk_s), (dv_s, wv_s)):
-            total = total + dot(d[...], w[cols, :], NT)
-        sg_s[:, cols] = total.astype(bf16)
-        sums_out[0:1, cols] = jnp.sum(dq_s[:, cols].astype(f32), axis=0, keepdims=True)
-        sums_out[1:2, cols] = jnp.sum(dv_s[:, cols].astype(f32), axis=0, keepdims=True)
-        sums_out[2:8, cols] = jnp.zeros((6, 256), f32)
-
-    sg_copy = pltpu.make_async_copy(sg_s, sg_out, out_sem.at[4])
-    sg_copy.start()
-    for i, d in enumerate((dq_s, dk_s, dv_s)):
-
-        @pl.loop(0, WIDTH // 256)
-        def _(t):
-            gst[1 + i, tile(t, 256), :] = dot(x_s[:, tile(t, 256)], d[...], TN).astype(bf16)
-
-        g_copy(1 + i).start()
-    for unit in range(4):
-        g_copy(unit).wait()
-    sg_copy.wait()
-
-
-def attn_back(seqs, lengths, ag, g, saved, weights):
-    rows, width = ag.shape
-    one = rows // seqs
-    anywhere = pl.BlockSpec(memory_space=pl.ANY)
-    in_vmem = pl.BlockSpec(memory_space=pltpu.VMEM)
-    wide = pltpu.VMEM((rows, width), bf16)
-    square = pltpu.VMEM((width, width), bf16)
-    return pl.pallas_call(
-        functools.partial(attn_back_kernel, seqs),
-        out_shape=(
-            jax.ShapeDtypeStruct(g.shape, bf16),
-            jax.ShapeDtypeStruct((rows, width), bf16),
-            jax.ShapeDtypeStruct((8, width), f32),
-        ),
-        in_specs=[pl.BlockSpec(memory_space=pltpu.SMEM), in_vmem] + [anywhere] * (len(saved) + 5),
-        out_specs=(anywhere, anywhere, in_vmem),
-        input_output_aliases={2: 0},
-        scratch_shapes=[wide] * 5
-        + [pltpu.VMEM((rows, 128), f32)]
-        + [square] * 4
-        + [wide] * 4
-        + [
-            pltpu.VMEM((seqs, 144, one), f32), pltpu.VMEM((4, width, width), bf16), wide,
-            pltpu.SemaphoreType.DMA((10,)), pltpu.SemaphoreType.DMA((5,)),
-        ],
-        compiler_params=pltpu.CompilerParams(vmem_limit_bytes=56 * 2**20),
-        cost_estimate=pl.CostEstimate(
-            flops=16 * rows * width * width + 10 * rows * one * width,
-            bytes_accessed=25 * 2**20, transcendentals=12 * rows * one,
-        ),
-        name="attn_back",
-    )(lengths, ag, g, *saved, *weights)
-
-
 def place_of_block():
     return (lax.axis_index("batch") % 8) * 4 + lax.axis_index("seq")
 
 
-def sum_kernel(
-    seqs, chunks, pattern, lags, g_ref, small_ref, head_ref, y_ref, sg_ref,
+def back_kernel(
+    seqs, chunks, pattern, lags, len_ref, label_ref, vec_ref,
+    cot, n2, hid, slope, low, n1, stat, y, q, k, v, att, x,
+    w1, w2, pool, wq, wk, wv, wo,
     out_ref, small_out, head_out, lay_out, grad_out,
-    acc, res, r0, r1, r2, r3, r4, sgot,
-    rs_send, rs_recv, ag_send, ag_recv, loc, sm_send, sm_recv, hd_send, hd_recv,
+    wide, fg_s, stat_s, w1_s, w2_s, pool_s, cls_s, row_s, rowt_s,
+    acc, staged, r0, r1, r2, r3, r4, sgot,
+    in_sem, hid_sem, rs_send, rs_recv, ag_send, ag_recv, loc, sm_send, sm_recv, hd_send, hd_recv,
     tok_send, tok_recv, tok_own,
 ):
+    rows = fg_s.shape[0]
+    one = rows // seqs
+    tokens = lay_out.shape[1]
+    count = lax.axis_size("seq")
     b = lax.axis_index("batch")
     z = lax.axis_index("seq")
     core = b % 2
+
     got = [r0, r1, r2, r3, r4]
+    res = r0
     near_b = [flipped(b, 2), flipped(b, 4), b, b]
     near_z = [z, z, flipped(z, 1), flipped(z, 2)]
     mine = [(b // 2) % 2, (b // 4) % 2, z % 2, (z // 2) % 2]
@@ -740,40 +457,22 @@
     greeted = [core_partner, (near_b[0], near_z[0]), (near_b[1], near_z[1])] + greet_line()
     for who in greeted:
         pl.semaphore_signal(barrier, inc=1, device_id=who, device_id_type=MESH)
-    pl.semaphore_wait(barrier, len(greeted))
-
-    tokens = lay_out.shape[1]
-    count = lax.axis_size("seq")
-    moves = []
-    own = []
-    for i, (src, dst) in enumerate(((y_ref, lay_out), (sg_ref, grad_out))):
-        for s in range(seqs):
-            base_sem = i * seqs * (count - 1)
-            moves += spread(src, dst, seqs, tokens, False, tok_send, tok_recv, base_sem, s)
-            own.append(own_part(src, dst, seqs, tokens, False, tok_own.at[i * seqs + s], s))
-    for copy in own:
-        copy.start()
-    half_moves = len(moves) // 2
-    move_ticks = [i for i in range(half_moves)] + [12 + 4 * i for i in range(half_moves)]
 
     def base(c, level):
-        rows = 0
+        first = 0
         size = CHUNK
         for l in range(level):
             size = size // 2
-            rows = rows + direction(c, l)[2] * size
-        return pl.multiple_of(rows, 16)
-
-    def g_rows(c):
-        return pl.ds(pl.multiple_of(c * CHUNK, CHUNK), CHUNK)
-
+            first = first + direction(c, l)[2] * size
+        return pl.multiple_of(first, 16)
+
+    slots = staged.shape[0]
     my_cols = pl.ds(pl.multiple_of(core * HALF, HALF), HALF)
-    other_cols = pl.ds(pl.multiple_of((1 - core) * HALF, HALF), HALF)
 
     def rs_copy(c, s):
         if s == 0:
             return pltpu.make_async_remote_copy(
-                g_ref.at[g_rows(c), other_cols], r0.at[c], rs_send.at[0, c], rs_recv.at[0, c],
+                staged.at[c % slots], r0.at[c], rs_send.at[0, c], rs_recv.at[0, c],
                 device_id=core_partner, device_id_type=MESH,
             )
         size = CHUNK >> s
@@ -784,10 +483,13 @@
             device_id=(nb, nz), device_id_type=MESH,
         )
 
+    def out_rows(c):
+        return out_ref.at[pl.ds(pl.multiple_of(c * CHUNK, CHUNK), CHUNK), my_cols]
+
     def ag_copy(c, s):
         if s == 0:
             return pltpu.make_async_remote_copy(
-                res.at[c], out_ref.at[g_rows(c), my_cols], ag_send.at[0, c], ag_recv.at[0, c],
+                res.at[c], out_rows(c), ag_send.at[0, c], ag_recv.at[0, c],
                 device_id=core_partner, device_id_type=MESH,
             )
         size = CHUNK >> s
@@ -798,34 +500,25 @@
             ag_send.at[s, c], ag_recv.at[s, c], device_id=(nb, nz), device_id_type=MESH,
         )
 
-    def loc_in(c):
-        return pltpu.make_async_copy(g_ref.at[g_rows(c), my_cols], acc.at[c], loc.at[0, c])
-
     def loc_out(c):
-        return pltpu.make_async_copy(res.at[c], out_ref.at[g_rows(c), my_cols], loc.at[1, c])
-
-    def stage_first(c):
-        rs_copy(c, 0).start()
-        loc_in(c).start()
+        return pltpu.make_async_copy(res.at[c], out_rows(c), loc.at[c])
 
     def stage_scatter(s, c):
         rs_copy(c, s - 1).wait_recv()
-        if s == 1:
-            loc_in(c).wait()
         half = CHUNK >> s
         start = base(c, s - 1)
         m = direction(c, s - 1)[2]
         for which in (0, 1):
             off = pl.multiple_of(((1 - m) if which == 0 else m) * half, 16)
-            rows = pl.ds(pl.multiple_of(start + off, 16), half)
-            acc[c, rows] = acc[c, rows] + got[s - 1][c, pl.ds(off, half)]
+            part = pl.ds(pl.multiple_of(start + off, 16), half)
+            acc[c, part] = acc[c, part] + got[s - 1][c, pl.ds(off, half)]
             if which == 0:
                 rs_copy(c, s).start()
 
     def stage_turn(c):
         rs_copy(c, 4).wait_recv()
-        rows = pl.ds(base(c, 4), 16)
-        res[c, rows] = acc[c, rows] + r4[c]
+        part = pl.ds(base(c, 4), 16)
+        res[c, part] = acc[c, part] + r4[c]
         ag_copy(c, 4).start()
 
     def stage_gather(s, c):
@@ -837,22 +530,283 @@
     def stage_last(c):
         ag_copy(c, 0).wait_recv()
         loc_out(c).wait()
+        for s in range(1, 5):
+            rs_copy(c, s).wait_send()
         for s in range(5):
-            rs_copy(c, s).wait_send()
             ag_copy(c, s).wait_send()
 
     stages = (
-        [stage_first]
-        + [functools.partial(stage_scatter, s) for s in (1, 2, 3, 4)]
+        [functools.partial(stage_scatter, s) for s in (1, 2, 3, 4)]
         + [stage_turn]
         + [functools.partial(stage_gather, s) for s in (3, 2, 1, 0)]
         + [stage_last]
     )
 
-    place = place_of_block()
+    def tick(t):
+        for stage, lag in reversed(list(zip(stages, lags))):
+            c = t - lag
+
+            @pl.when((c >= 0) & (c < chunks))
+            def _():
+                stage(c)
+
+    def give(c, left, right, fresh=False):
+        grad = dot(left, right, TN).astype(bf16)
+        first = grad[:, 0:HALF]
+        second = grad[:, HALF:]
+
+        @pl.when(c >= slots)
+        def _():
+            rs_copy(c - slots, 0).wait_send()
+
+        staged[c % slots] = jnp.where(core == 0, second, first)
+        acc[c] = jnp.where(core == 0, first, second)
+        rs_copy(c, 0).start()
+
+    (cot_s, n2_s, low_s, n1_s, pg_s, eg_s) = [wide.at[i] for i in range(6)]
+    ag_s = wide.at[10]
+
+    def chunk_load(j):
+        cols = pl.ds(pl.multiple_of(j * WIDTH, WIDTH), WIDTH)
+        return (
+            pltpu.make_async_copy(hid.at[:, cols], wide.at[6 + j % 2], hid_sem.at[0, j]),
+            pltpu.make_async_copy(slope.at[:, cols], wide.at[8 + j % 2], hid_sem.at[1, j]),
+        )
+
+    cls_in = [
+        pltpu.make_async_copy(
+            y.at[pl.ds(s * one, 16)], cls_s.at[pl.ds(s * 16, 16)], in_sem.at[20 + s]
+        )
+        for s in range(seqs)
+    ]
+    loads = copies(
+        [
+            (pool, pool_s), (cot, cot_s), (n2, n2_s), (stat, stat_s), (w2, w2_s),
+            (low, low_s), (w1, w1_s), (n1, n1_s),
+        ],
+        in_sem,
+    )
+    for copy in cls_in + loads[:5]:
+        copy.start()
+    for copy in chunk_load(0):
+        copy.start()
+    for copy in loads[5:]:
+        copy.start()
+    later = copies([(q, wide.at[0]), (k, wide.at[1])], in_sem.at[pl.ds(8, 2)])
+    middle = copies([(v, wide.at[6]), (att, wide.at[8])], in_sem.at[pl.ds(10, 2)])
+    (x_load,) = copies([(x, wide.at[7])], in_sem.at[pl.ds(12, 1)])
+    attn_weights = [
+        pltpu.make_async_copy(w, w2_s.at[pl.ds(i * WIDTH, WIDTH)], in_sem.at[13 + i])
+        for i, w in enumerate((wo, wq, wk, wv))
+    ]
+
+    pl.semaphore_wait(barrier, len(greeted))
+    y_moves = []
+    own = []
+    for s in range(seqs):
+        y_moves += spread(y, lay_out, seqs, tokens, False, tok_send, tok_recv, 0, s)
+        own.append(own_part(y, lay_out, seqs, tokens, False, tok_own.at[s], s))
+    for copy in own + y_moves:
+        copy.start()
+
+    for copy in cls_in:
+        copy.wait()
+    loads[0].wait()
+    place = lax.broadcasted_iota(jnp.int32, (16 * seqs, 1), 0)
+    labels = jnp.zeros((16 * seqs, 1), jnp.int32)
+    label_row = jnp.zeros((1, 128), f32)
+    lane = lax.broadcasted_iota(jnp.int32, (1, 128), 1)
+    for s in range(seqs):
+        label = label_ref[z * seqs + s]
+        labels = jnp.where(place == 16 * s, label, labels)
+        label_row = jnp.where(lane == s, label.astype(f32), label_row)
+    cls_grad = exit_back(cls_s[...], labels, vec_ref, pool_s)
+    row_s[...] = jnp.zeros_like(row_s)
+    for s in range(seqs):
+        first = cls_s[16 * s : 16 * (s + 1), :].astype(f32)
+        for j in range(6):
+            row_s[s * 6 + j : s * 6 + j + 1, :] = first[0:1, j * 128 : (j + 1) * 128]
+    row_s[12:13, :] = label_row
+    block = place_of_block()
+    head_out[block] = row_s[...].astype(bf16)
+    for copy in loads[1:4]:
+        copy.wait()
+    small_out[...] = jnp.zeros_like(small_out)
+    ROW = 128
+
+    def add_sum(index, values):
+        small_out[index : index + 1, :] += jnp.sum(values, axis=0, keepdims=True)
+
+    @pl.loop(0, rows // ROW)
+    def _(i):
+        r = tile(i, ROW)
+        upstream = cot_s[r, :].astype(f32)
+        place = lax.broadcasted_iota(jnp.int32, (ROW, 1), 0) + i * ROW
+        for s in range(seqs):
+            upstream = upstream + jnp.where(place == s * one, cls_grad[16 * s : 16 * s + 1, :], 0.0)
+        normed = n2_s[r, :].astype(f32)
+        add_sum(G2, upstream * normed)
+        add_sum(B2, upstream)
+        zg = norm_rows_back(upstream, normed, stat_s[r, 13:14], vec_ref[G2 : G2 + 1, :])
+        rounded = zg.astype(bf16)
+        pg_s[r, :] = rounded
+        add_sum(UB, rounded.astype(f32))
+        fg_s[r, :] = zg
+
+    for copy in later:
+        copy.start()
+    for copy in loads[4:7]:
+        copy.wait()
+
+    @pl.loop(0, 4)
+    def _(j):
+        for copy in chunk_load(j):
+            copy.wait()
+
+        @pl.when(j < 3)
+        def _():
+            for copy in chunk_load(j + 1):
+                copy.start()
+
+        @pl.when(j == 3)
+        def _():
+            for copy in middle:
+                copy.start()
+
+        @pl.loop(0, WIDTH // 256)
+        def _(t):
+            cols = tile(t, 256)
+            ff = pl.ds(pl.multiple_of(j * WIDTH + t * 256, 256), 256)
+            grad = dot(pg_s[...], w2_s[ff, :], NT) * wide[8 + j % 2, :, cols].astype(f32)
+            rounded = grad.astype(bf16)
+            eg_s[:, cols] = rounded
+            small_out[pl.ds(IB + j, 1), cols] = jnp.sum(
+                rounded.astype(f32), axis=0, keepdims=True
+            )
+
+        for i in range(4):
+
+            @pl.when(j == i)
+            def _():
+                attn_weights[i].start()
+
+        @pl.loop(0, 3)
+        def _(t):
+            give(6 * j + t, wide[6 + j % 2, :, tile(t, 256)], pg_s[...])
+
+        tick(3 * j)
+
+        @pl.loop(0, 3)
+        def _(t):
+            give(6 * j + 3 + t, low_s[:, tile(t, 256)], eg_s[...])
+
+        tick(3 * j + 1)
+        ff_cols = pl.ds(pl.multiple_of(j * WIDTH, WIDTH), WIDTH)
+
+        @pl.loop(0, WIDTH // 256)
+        def _(t):
+            cols = tile(t, 256)
+            fg_s[:, cols] += dot(eg_s[...], w1_s[cols, ff_cols], NT)
+
+        tick(3 * j + 2)
+
+    x_load.start()
+    loads[7].wait()
+
+    @pl.loop(0, rows // ROW)
+    def _(i):
+        r = tile(i, ROW)
+        upstream = fg_s[r, :]
+        normed = n1_s[r, :].astype(f32)
+        add_sum(G1, upstream * normed)
+        add_sum(B1, upstream)
+        zg = norm_rows_back(upstream, normed, stat_s[r, 12:13], vec_ref[G1 : G1 + 1, :])
+        rounded = zg.astype(bf16)
+        ag_s[r, :] = rounded
+        add_sum(OB, rounded.astype(f32))
+
+    tick(12)
+
+    (q_s, k_s, dv_s, sg_s, dq_s, dk_s, v_s, x_s, att_s, dat_s) = [wide.at[i] for i in range(10)]
+    wo_s, wq_s, wk_s, wv_s = [w2_s.at[pl.ds(i * WIDTH, WIDTH)] for i in range(4)]
+    attn_weights[0].wait()
+
+    @pl.loop(0, WIDTH // 256)
+    def _(t):
+        cols = tile(t, 256)
+        dat_s[:, cols] = dot(ag_s[...], wo_s[cols, :], NT).astype(bf16)
+
+    for copy in middle + later:
+        copy.wait()
+
+    @pl.loop(0, 3)
+    def _(t):
+        give(24 + t, att_s[:, tile(t, 256)], ag_s[...])
+
+    tick(13)
+    head_of = lax.broadcasted_iota(jnp.int32, (16, WIDTH), 1) // HEAD_DIM
+    picker = (head_of == lax.broadcasted_iota(jnp.int32, (16, WIDTH), 0)).astype(bf16)
+    for s in range(seqs):
+        part = pl.ds(s * one, one)
+        product = dat_s[part, :].astype(f32) * att_s[part, :].astype(f32)
+        high = product.astype(bf16)
+        rest = (product - high.astype(f32)).astype(bf16)
+        rowt_s[s, 128:144, :] = dot(picker, high, NT) + dot(picker, rest, NT)
+        rowt_s[s, 0:128, :] = jnp.transpose(stat_s[part, :])
+
+    @pl.loop(0, seqs * 3)
+    def _(i):
+        s = i // 3
+        part = pl.ds(pl.multiple_of(s * one, one), one)
+        length = len_ref[z * seqs + s]
+        for half in (0, 1):
+            p = 2 * (i % 3) + half
+            cols = tile(p, 128)
+            logs = [rowt_s[s, pl.ds(2 * p + w, 1), :] for w in (0, 1)]
+            delta = [rowt_s[s, pl.ds(128 + 2 * p + w, 1), :] for w in (0, 1)]
+            dq, dk, dv = attend_back_pair(
+                q_s[part, cols], k_s[part, cols], v_s[part, cols], dat_s[part, cols],
+                logs, delta, length, one,
+            )
+            dq_s[part, cols] = dq.astype(bf16)
+            dk_s[part, cols] = dk.astype(bf16)
+            dv_s[part, cols] = dv.astype(bf16)
+        tick(14 + i)
+
+    for copy in attn_weights[1:]:
+        copy.wait()
+    x_load.wait()
+
+    @pl.loop(0, WIDTH // 256)
+    def _(t):
+        cols = tile(t, 256)
+        total = ag_s[:, cols].astype(f32)
+        for d, w in ((dq_s, wq_s), (dk_s, wk_s), (dv_s, wv_s)):
+            total = total + dot(d[...], w[cols, :], NT)
+        sg_s[:, cols] = total.astype(bf16)
+        small_out[QB : QB + 1, cols] = jnp.sum(dq_s[:, cols].astype(f32), axis=0, keepdims=True)
+        small_out[VB : VB + 1, cols] = jnp.sum(dv_s[:, cols].astype(f32), axis=0, keepdims=True)
+
+    moves = []
+    for s in range(seqs):
+        moves += spread(
+            sg_s, grad_out, seqs, tokens, False, tok_send, tok_recv, seqs * (count - 1), s
+        )
+        own.append(own_part(sg_s, grad_out, seqs, tokens, False, tok_own.at[seqs + s], s))
+        own[-1].start()
+    done = 14 + 3 * seqs
+    for i, d in enumerate((dq_s, dk_s, dv_s)):
+
+        @pl.loop(0, 3)
+        def _(t):
+            give(27 + 3 * i + t, x_s[:, tile(t, 256)], d[...])
+
+        tick(done + i)
+    done += 3
+
 
     def small_copies(i):
-        first = place - place % (1 << i)
+        first = block - block % (1 << i)
         part = pl.ds(first, 1 << i)
         return (
             pltpu.make_async_remote_copy(
@@ -865,10 +819,9 @@
             ),
         )
 
-    small_out[...] = small_ref[...]
-    head_out[place] = head_ref[...]
-
-    def tick(t, carry):
+    move_ticks = [done + 2 * i for i in range(len(moves))]
+
+    def late_tick(t, carry):
         for when, copy in zip(move_ticks, moves):
 
             @pl.when(t == when)
@@ -877,7 +830,7 @@
 
         for i in range(len(partners) + 1):
 
-            @pl.when(t == 3 * i)
+            @pl.when(t == done + 3 * i)
             def _():
                 if i > 0:
                     for copy in small_copies(i - 1):
@@ -887,76 +840,76 @@
                     for copy in small_copies(i):
                         copy.start()
 
-        for stage, lag in reversed(list(zip(stages, lags))):
-            c = t - lag
-
-            @pl.when((c >= 0) & (c < chunks))
-            def _():
-                stage(c)
-
+        tick(t)
         return carry
 
-    lax.fori_loop(0, chunks + lags[-1], tick, 0)
-    for copy in own + moves:
+    lax.fori_loop(done, chunks + lags[-1], late_tick, 0)
+    for c in range(chunks - slots, chunks):
+        rs_copy(c, 0).wait_send()
+    for copy in own + y_moves + moves:
         copy.wait()
 
 
-def sum_all(seqs, g, small, head, y, sg, tokens):
-    width = g.shape[-1]
-    flat = g.reshape(-1, width)
-    chunks = flat.shape[0] // CHUNK
+def back(seqs, tokens, lengths, labels, vecs, saved, weights):
+    rows, width = saved[0].shape
+    ff = 4 * width
+    one = rows // seqs
     count = lax.axis_size("seq")
-    group = seqs * count
+    chunks = 12 * width // CHUNK
     moves = 2 * seqs * (count - 1)
     dma = pltpu.SemaphoreType.DMA
     anywhere = pl.BlockSpec(memory_space=pl.ANY)
     in_vmem = pl.BlockSpec(memory_space=pltpu.VMEM)
-    block = jax.ShapeDtypeStruct((group, tokens, width), bf16)
+    in_smem = pl.BlockSpec(memory_space=pltpu.SMEM)
+    block = jax.ShapeDtypeStruct((seqs * count, tokens, width), bf16)
+    small = (16, width)
+    half = functools.partial(pltpu.VMEM, dtype=bf16)
     total, small, head, lay, grad = pl.pallas_call(
-        functools.partial(sum_kernel, seqs, chunks, "xy", tuple(3 * i for i in range(11))),
+        functools.partial(back_kernel, seqs, chunks, "xy", tuple(3 * i for i in range(10))),
         out_shape=(
-            jax.ShapeDtypeStruct(flat.shape, bf16),
-            jax.ShapeDtypeStruct(small.shape, f32),
-            jax.ShapeDtypeStruct((32,) + head.shape, bf16),
+            jax.ShapeDtypeStruct((12 * width, width), bf16),
+            jax.ShapeDtypeStruct(small, f32),
+            jax.ShapeDtypeStruct((32, 16, 128), bf16),
             block,
             block,
         ),
-        in_specs=[anywhere, in_vmem, in_vmem, anywhere, anywhere],
+        in_specs=[in_smem, in_smem, in_vmem] + [anywhere] * (len(saved) + len(weights)),
         out_specs=(anywhere, in_vmem, in_vmem, anywhere, anywhere),
         scratch_shapes=[
+            pltpu.VMEM((11, rows, width), bf16), pltpu.VMEM((rows, width), f32),
+            pltpu.VMEM((rows, 128), f32), pltpu.VMEM((width, ff), bf16),
+            pltpu.VMEM((ff, width), bf16), pltpu.VMEM((width, width), bf16),
+            pltpu.VMEM((16 * seqs, width), bf16), pltpu.VMEM((16, 128), f32),
+            pltpu.VMEM((seqs, 144, one), f32),
             pltpu.VMEM((chunks, CHUNK, HALF), bf16),
-            pltpu.VMEM((chunks, CHUNK, HALF), bf16),
+            pltpu.VMEM((6, CHUNK, HALF), bf16),
             pltpu.VMEM((chunks, CHUNK, HALF), bf16),
             pltpu.VMEM((chunks, CHUNK // 2, HALF), bf16),
             pltpu.VMEM((chunks, CHUNK // 4, HALF), bf16),
             pltpu.VMEM((chunks, CHUNK // 8, HALF), bf16),
             pltpu.VMEM((chunks, CHUNK // 16, HALF), bf16),
-            pltpu.VMEM((5,) + small.shape, f32),
-            dma((5, chunks)),
-            dma((5, chunks)),
-            dma((5, chunks)),
-            dma((5, chunks)),
-            dma((2, chunks)),
-            dma((5,)),
-            dma((5,)),
-            dma((5,)),
-            dma((5,)),
-            dma((moves,)),
-            dma((moves,)),
-            dma((2 * seqs,)),
+            pltpu.VMEM((5,) + small, f32),
+            dma((20 + seqs,)), dma((2, 4)),
+            dma((5, chunks)), dma((5, chunks)), dma((5, chunks)), dma((5, chunks)),
+            dma((chunks,)), dma((5,)), dma((5,)), dma((5,)), dma((5,)),
+            dma((moves,)), dma((moves,)), dma((2 * seqs,)),
         ],
         compiler_params=pltpu.CompilerParams(
-            collective_id=0, has_side_effects=True, vmem_limit_bytes=56 * 2**20
+            collective_id=0, has_side_effects=True, vmem_limit_bytes=62 * 2**20
         ),
-        name="sum_gradients",
-    )(flat, small, head, y, sg)
+        cost_estimate=pl.CostEstimate(
+            flops=8 * rows * width * ff + 16 * rows * width * width + 10 * rows * one * width,
+            bytes_accessed=100 * 2**20, transcendentals=12 * rows * one,
+        ),
+        name="back",
+    )(lengths, labels, vecs, *saved, *weights)
     blocks = lax.axis_size("batch") // 8
     if blocks > 1:
         alike = [[i + 8 * j for j in range(blocks)] for i in range(8)]
         total = lax.psum(total, "batch", axis_index_groups=alike)
         small = lax.psum(small, "batch", axis_index_groups=alike)
         head = lax.all_gather(head, "batch", axis_index_groups=alike, axis=0, tiled=True)
-    return total.reshape(g.shape), small, head, lay, grad
+    return total.reshape(12, width, width), small, head, lay, grad
 
 
 def finish_kernel(
@@ -971,11 +924,11 @@
     loads = [pltpu.make_async_copy(total.at[u], low_s.at[u], in_sem.at[u]) for u in range(units)]
     for copy in loads:
         copy.start()
-    places = (
-        [gou.at[pl.ds(j * WIDTH, WIDTH)] for j in range(4)]
-        + [gin.at[:, pl.ds(j * WIDTH, WIDTH)] for j in range(4)]
-        + [go, gq, gk, gv]
-    )
+    places = []
+    for j in range(4):
+        part = pl.ds(j * WIDTH, WIDTH)
+        places += [gou.at[part], gin.at[:, part]]
+    places += [go, gq, gk, gv]
     stores = [
         pltpu.make_async_copy(full_s.at[u], places[u], out_sem.at[u]) for u in range(units)
     ]
@@ -1105,16 +1058,11 @@
         (query_bias, value_bias, output_bias, first_gain, first_bias, inner_bias, outer_bias,
          second_gain, second_bias, pool_bias, class_proj, class_bias),
     )
-    g, attn_grad, sums_ffn, head = ffn_back(
-        seqs, labels, vecs, (upstream, n2, hid, slope, low, n1, stat, y),
-        inner_proj, outer_proj, pool_proj,
+    total, small, head, lay, grad = back(
+        seqs, tokens, lengths, labels, vecs,
+        (upstream, n2, hid, slope, low, n1, stat, y, q, k, v, att, x),
+        (inner_proj, outer_proj, pool_proj, query_proj, key_proj, value_proj, output_proj),
     )
-    g, states_rows, sums_attn = attn_back(
-        seqs, lengths, attn_grad, g, (q, k, v, att, x, stat),
-        (query_proj, key_proj, value_proj, output_proj),
-    )
-    small = jnp.concatenate([sums_attn[0:2], sums_ffn[2:12], jnp.zeros((4, width), f32)])
-    total, small, head, lay, grad = sum_all(seqs, g, small, head, y, states_rows, tokens)
     cls = head[:, 0 : 6 * seqs].reshape(-1, width)
     label_row = head[:, 6 * seqs, 0:seqs].reshape(1, -1).astype(jnp.int32)
     return finish(total, small, cls, label_row, vecs, pool_proj, lay, grad)

time: 387 us -> 303 us (0.78)
  Pallas kernels: 375 us -> 296 us
    pallas_call x3 -> x1, Pallas kernels: 280 us -> 201 us  [back(): pl.pallas_call(functools.partial(back_kernel, seqs, chunks, 'xy', tuple((...]
where the time goes in v3:
time: 303 us
  Pallas kernels  296 us (98%)
  local copies, waits for them, and re-layouts  5.55 us (2%)
    pallas_call x1, Pallas kernels, back(): pl.pallas_call(functools.partial(back_kernel, seqs, chunks, 'xy', tuple((...  201 us
    pallas_call x1, Pallas kernels, forward(): pl.pallas_call(functools.partial(forward_kernel, seqs), out_shape=tuple((...  73.2 us
    pallas_call x1, Pallas kernels, finish(): pl.pallas_call(finish_kernel, out_shape=tuple((jax.ShapeDtypeStruct(s, t)...  21.3 us

profile of v3, /device:TPU:1, one launch (start us, length us, event | category | flops | bytes accessed | tf_op | source)
XLA Modules:
  0.0 303.1 jit_solution(12435456418532981824)
XLA Ops:
  0.7 1.5 copy.47.class_proj
  2.2 73.2 %forward.1 = (f32[24,768]{1,0:T(8,128)}, bf16[1024,768]{1,0:T(8,128)(2,1)}, bf16[1024,768]{1,0:T(8,128)(2,1)}, bf16[1024,768]{1,0:T(8,128)(2,1)}, bf16[1024,768]...) custom-call(s32[8]{0:T(128)} %len_ref.3, ...), custom_call_target="tpu_custom_call" | custom-call | flops 16106127360 | bytes 52428800 | tf_op jit(solution)/shard_map/forward/pallas_call | solution.py:344
  75.4 201.4 %back.1 = (bf16[9216,768]{1,0:T(8,128)(2,1)}, f32[16,768]{1,0:T(8,128)}, bf16[32,16,128]{2,1,0:T(8,128)(2,1)}, bf16[8,128,768]{2,1,0:T(8,128)(2,1)}, bf16[8,128,768]{2,1,0:T(8,128)(2,1)}) custom-call(s32[8]{0:T(128)} %len_ref.3, s32[8]{0:T(128)} %label_ref.1, f32[24,768]{1,0:T(8,128)} %get-tuple-element.41.vec_ref, bf16[1024,768]{1,0:T(8,128)(2,1)} %get-tuple-element.42.cot, ...), custom_call_target="tpu_custom_call" | custom-call | flops 33017561088 | bytes 104857600 | tf_op jit(solution)/shard_map/back/pallas_call | solution.py:867
  276.9 0.9 convert_reduce_fusion
  277.8 0.6 reshape.66.label_ref
  278.4 1.7 reshape.65.cls_ref
  280.0 21.3 %finish.1 = (bf16[8,128,768]{2,1,0:T(8,128)(2,1)}, f32[8]{0:T(128)}, bf16[8,128,768]{2,1,0:T(8,128)(2,1)}, f32[768,768]{1,0:T(8,128)}, f32[768,768]{1,0:T(8,128)...) custom-call(bf16[12,768,768]{2,1,0:T(8,128)(2,1)} %bitcast.2, ...), custom_call_target="tpu_custom_call" | custom-call | tf_op jit(solution)/shard_map/finish/pallas_call | solution.py:1029
  301.4 1.7 copy.48

commit v4 on v3

v4 whole, which is shorter than its diff:
```python
import functools

import jax
import jax.numpy as jnp
from jax import lax
from jax.experimental import pallas as pl
from jax.experimental.pallas import tpu as pltpu
from jax.sharding import PartitionSpec as P

HEADS = 12
HEAD_DIM = 64
WIDTH = 768
HALF = 384
CHUNK = 256
MESH = pl.DeviceIdType.MESH

bf16 = jnp.bfloat16
f32 = jnp.float32
highest = lax.Precision.HIGHEST
norm_eps = 1e-06
masked_fill = -1e30
inv_root_two = 0.7071067811865476
inv_root_tau = 0.3989422804014327


def pick(code, table):
    out = table[-1]
    for i in range(len(table) - 2, -1, -1):
        out = jnp.where(code == i, table[i], out)
    return out


def flipped(index, bit):
    return index + bit * (1 - 2 * ((index // bit) % 2))


NT = (((1,), (1,)), ((), ()))
NN = (((1,), (0,)), ((), ()))
TN = (((0,), (0,)), ((), ()))
VECS = 24
QB, VB, OB, G1, B1, IB, UB, G2, B2, PB, CP, CB = 0, 1, 2, 3, 4, 5, 9, 10, 11, 12, 13, 16


def dot(left, right, dims=NN):
    return lax.dot_general(left, right, dims, preferred_element_type=f32)


def gelu_parts(u):
    t = 1.0 / (1.0 + (0.3275911 * inv_root_two) * jnp.abs(u))
    bell = jnp.exp(-0.5 * u * u)
    poly = 1.061405429
    for coefficient in (-1.453152027, 1.421413741, -0.284496736, 0.254829592):
        poly = poly * t + coefficient
    tail = (0.5 * t) * poly * bell
    cumulative = jnp.where(u >= 0.0, 1.0 - tail, tail)
    return u * cumulative, cumulative + u * (bell * inv_root_tau)


def norm_rows(z):
    average = jnp.mean(z, axis=-1, keepdims=True)
    centered = z - average
    inv_root = lax.rsqrt(jnp.mean(centered * centered, axis=-1, keepdims=True) + norm_eps)
    return centered * inv_root, inv_root


def norm_rows_back(upstream, normed, inv_root, gain):
    scaled = upstream * gain
    return inv_root * (
        scaled
        - jnp.mean(scaled, axis=-1, keepdims=True)
        - normed * jnp.mean(scaled * normed, axis=-1, keepdims=True)
    )


def tile(i, size):
    return pl.ds(pl.multiple_of(i * size, size), size)


def copies(pairs, sems):
    out = []
    for i, (src, dst) in enumerate(pairs):
        out.append(pltpu.make_async_copy(src, dst, sems.at[i]))
    return out


def head_lanes(which):
    lane = lax.broadcasted_iota(jnp.int32, (1, 128), 1)
    return (lane >= 64) if which else (lane < 64)


def only(mask, block):
    return jnp.where(mask, block, jnp.zeros_like(block))


def attend_pair(q2, k2, v2, length, keys):
    k2 = k2[:keys]
    v2 = v2[:keys]
    place = lax.broadcasted_iota(jnp.int32, (1, keys), 1)
    out = None
    logs = []
    for which in (0, 1):
        lanes = head_lanes(which)
        scores = dot(only(lanes, q2) * bf16(0.125), k2, NT)
        scores = jnp.where(place < length, scores, masked_fill)
        top = jnp.max(scores, axis=-1, keepdims=True)
        weights = jnp.exp(scores - top)
        total = jnp.sum(weights, axis=-1, keepdims=True)
        part = dot(weights.astype(bf16), only(lanes, v2)) * (1.0 / total)
        out = part if out is None else out + part
        logs.append(top + jnp.log(total))
    return out, logs


def three_terms(values):
    high = values.astype(bf16).astype(f32)
    mid = (values - high).astype(bf16).astype(f32)
    return high, mid, values - high - mid


def attend_back_pair(q2, k2, v2, d2, a2, q_aux, key_aux, value_aux):
    lane = lax.broadcasted_iota(jnp.int32, (1, 128), 1)
    product = d2.astype(f32) * a2.astype(f32)
    d_aux = jnp.zeros_like(product)
    for which in (0, 1):
        delta = jnp.sum(only(head_lanes(which), product), axis=-1, keepdims=True)
        for i, piece in enumerate(three_terms(-delta)):
            d_aux = jnp.where(lane == 64 * (1 - which) + i, piece, d_aux)
    d_aux = d_aux.astype(bf16)
    q2 = q2 * bf16(0.125)
    heads = []
    for which in (0, 1):
        lanes = head_lanes(which)
        heads.append(
            [
                jnp.where(lanes, block, other)
                for block, other in ((q2, q_aux), (k2, key_aux), (v2, value_aux), (d2, d_aux))
            ]
        )
    scores = [dot(kh, qh, NT) for qh, kh, _, _ in heads]
    prob_grads = [dot(vh, dh, NT) for _, _, vh, dh in heads]
    probs = [jnp.exp(s) for s in scores]
    score_grads = [(p * g).astype(bf16) for p, g in zip(probs, prob_grads)]
    out = [
        (dot(g, kh, TN), dot(g, qh), dot(p.astype(bf16), dh))
        for g, p, (qh, kh, _, dh) in zip(score_grads, probs, heads)
    ]
    first = head_lanes(0)
    dq, dk, dv = [jnp.where(first, one, two) for one, two in zip(*out)]
    return dq * 0.125, dk, dv


def exit_back(cls_rows, labels, vec_ref, pool_s):
    pooled = jnp.tanh(dot(cls_rows, pool_s[...]) + vec_ref[PB : PB + 1, :])
    class_rows = vec_ref[CP : CP + 3, :]
    logits = [
        jnp.sum(pooled * class_rows[i : i + 1, :], axis=-1, keepdims=True)
        + vec_ref[CB : CB + 1, i : i + 1]
        for i in range(3)
    ]
    top = jnp.maximum(jnp.maximum(logits[0], logits[1]), logits[2])
    raised = [jnp.exp(l - top) for l in logits]
    total = raised[0] + raised[1] + raised[2]
    back = jnp.zeros_like(pooled)
    for i in range(3):
        back = back + (raised[i] / total - (labels == i).astype(f32)) * class_rows[i : i + 1, :]
    pre = back * (1.0 - pooled * pooled)
    high = pre.astype(bf16)
    rest = pre - high.astype(f32)
    mid = rest.astype(bf16)
    low = (rest - mid.astype(f32)).astype(bf16)
    return dot(high, pool_s[...], NT) + dot(mid, pool_s[...], NT) + dot(low, pool_s[...], NT)


def spread(src, dst, seqs, tokens, to_rows, sends, recvs, base, s, ordered=False):
    count = lax.axis_size("seq")
    b = lax.axis_index("batch")
    z = lax.axis_index("seq")
    out = []
    for d in range(1, count):
        if ordered and count == 4:
            d = jnp.where(z % 2 == 0, d % 3 + 1, d)
        other = lax.rem(z + d, count)
        if to_rows:
            source = src.at[other * seqs + s]
            target = dst.at[pl.ds(pl.multiple_of((s * count + z) * tokens, tokens), tokens)]
        else:
            source = src.at[pl.ds(pl.multiple_of((s * count + other) * tokens, tokens), tokens)]
            target = dst.at[z * seqs + s]
        i = base + s * (count - 1) + d - 1
        out.append(
            pltpu.make_async_remote_copy(
                source, target, sends.at[i], recvs.at[i],
                device_id=(b, other), device_id_type=MESH,
            )
        )
    return out


def own_part(src, dst, seqs, tokens, to_rows, sem, s):
    count = lax.axis_size("seq")
    z = lax.axis_index("seq")
    block = z * seqs + s
    rows = pl.ds(pl.multiple_of((s * count + z) * tokens, tokens), tokens)
    if to_rows:
        return pltpu.make_async_copy(src.at[block], dst.at[rows], sem)
    return pltpu.make_async_copy(src.at[rows], dst.at[block], sem)


def greet_line():
    count = lax.axis_size("seq")
    z = lax.axis_index("seq")
    return [(lax.axis_index("batch"), lax.rem(z + d, count)) for d in range(1, count)]


def forward_kernel(
    seqs, len_ref, label_ref, states, cot, wq, wk, wv, wo, w1, w2, pool,
    query_bias, value_bias, output_bias, first_gain, first_bias, inner_bias, outer_bias,
    second_gain, second_bias, pool_bias, class_proj, class_bias,
    vec_ref, small_out, head_out, x_out, q_out, k_out, v_out, att_out, n1_out, low_out, hid_out,
    slope_out, stat_out, y_out, aux_out, pg_out,
    x_s, wq_s, wk_s, wv_s, wo_s, w1_s, w2_s,
    q_s, k_s, v_s, att_s, n1_s, low_s, hid_s, slope_s, stat_s, y_s, aux_s, n2_s, z_s,
    cot_s, pool_s, row_s, in_sem, out_sem, own_sem, sends, recvs,
):
    rows = z_s.shape[0]
    tokens = states.shape[1]
    line = greet_line()
    barrier = pltpu.get_barrier_semaphore()
    for who in line:
        pl.semaphore_signal(barrier, inc=1, device_id=who, device_id_type=MESH)
    weights_in = copies(
        [(wq, wq_s), (wk, wk_s), (wv, wv_s), (wo, wo_s), (w1, w1_s), (w2, w2_s), (pool, pool_s)],
        in_sem,
    )
    z = lax.axis_index("seq")
    own = [own_part(states, x_s, seqs, tokens, True, own_sem.at[s], s) for s in range(seqs)]
    own_cot = [
        own_part(cot, cot_s, seqs, tokens, True, own_sem.at[seqs + s], s) for s in range(seqs)
    ]
    for copy in own + weights_in + own_cot:
        copy.start()
    pl.semaphore_wait(barrier, len(line))

    def move(first, s, ordered):
        src, dst, start = (states, x_s, 0) if first else (cot, cot_s, seqs * len(line))
        return spread(src, dst, seqs, tokens, True, sends, recvs, start, s, ordered)

    moves = [move(True, s, False) for s in range(seqs)]
    late = [move(False, s, False) for s in range(seqs)]
    for copy in move(True, 0, True):
        copy.start()
    vec_ref[...] = jnp.zeros_like(vec_ref)
    for i, ref in (
        (QB, query_bias), (VB, value_bias), (OB, output_bias), (G1, first_gain), (B1, first_bias),
        (UB, outer_bias), (G2, second_gain), (B2, second_bias), (PB, pool_bias),
    ):
        vec_ref[i : i + 1, :] = ref[...].astype(f32).reshape(1, WIDTH)
    for i in range(4):
        vec_ref[IB + i : IB + i + 1, :] = (
            inner_bias[i * WIDTH : (i + 1) * WIDTH].astype(f32).reshape(1, WIDTH)
        )
    vec_ref[CP : CP + 3, :] = class_proj[...].astype(f32)
    vec_ref[CB : CB + 1, 0:3] = class_bias[...].astype(f32).reshape(1, 3)

    waiting = []
    def send_late(s):
        for copy in move(False, s, True):
            copy.start()

    for s in range(seqs):
        for copy in moves[s]:
            copy.wait_recv()
        own[s].wait()
        if s == 0:
            for i in range(1, seqs):
                for copy in move(True, i, True):
                    copy.start()
        part = pl.ds(s * rows, rows)
        waiting += forward_rows(
            s, part, len_ref[z * seqs + s], rows, s == 0, vec_ref, weights_in,
            (lambda: send_late(0)) if s == 0 else None,
            (x_s, wq_s, wk_s, wv_s, wo_s, w1_s, w2_s, q_s, k_s, v_s, att_s, n1_s, low_s, hid_s,
             slope_s, stat_s, y_s, aux_s, n2_s, z_s),
            (x_out, q_out, k_out, v_out, att_out, n1_out, low_out, hid_out, slope_out,
             stat_out, y_out, aux_out),
            out_sem,
        )
        if s == 0:
            for i in range(1, seqs):
                send_late(i)

    place = lax.broadcasted_iota(jnp.int32, (16 * seqs, 1), 0)
    labels = jnp.zeros((16 * seqs, 1), jnp.int32)
    label_row = jnp.zeros((1, 128), f32)
    lane = lax.broadcasted_iota(jnp.int32, (1, 128), 1)
    for s in range(seqs):
        label = label_ref[z * seqs + s]
        labels = jnp.where(place == 16 * s, label, labels)
        label_row = jnp.where(lane == s, label.astype(f32), label_row)
    cls_rows = jnp.concatenate([y_s[s * rows : s * rows + 16, :] for s in range(seqs)])
    weights_in[6].wait()
    cls_grad = exit_back(cls_rows, labels, vec_ref, pool_s)
    row_s[...] = jnp.zeros_like(row_s)
    for s in range(seqs):
        first = y_s[s * rows : s * rows + 16, :].astype(f32)
        for j in range(6):
            row_s[s * 6 + j : s * 6 + j + 1, :] = first[0:1, j * 128 : (j + 1) * 128]
    row_s[6 * seqs : 6 * seqs + 1, :] = label_row
    head_out[...] = row_s[...].astype(bf16)
    small_out[...] = jnp.zeros_like(small_out)

    def add_sum(index, values):
        small_out[index : index + 1, :] += jnp.sum(values, axis=0, keepdims=True)

    for s in range(seqs):
        for copy in late[s]:
            copy.wait_recv()
        own_cot[s].wait()

        @pl.loop(0, rows // 128)
        def _(i):
            r = pl.ds(pl.multiple_of(s * rows + i * 128, 128), 128)
            place = lax.broadcasted_iota(jnp.int32, (128, 1), 0) + i * 128
            upstream = cot_s[r, :].astype(f32) + jnp.where(
                place == 0, cls_grad[16 * s : 16 * s + 1, :], 0.0
            )
            normed = n2_s[r, :].astype(f32)
            add_sum(G2, upstream * normed)
            add_sum(B2, upstream)
            grad = norm_rows_back(upstream, normed, stat_s[r, 13:14], vec_ref[G2 : G2 + 1, :])
            rounded = grad.astype(bf16)
            n2_s[r, :] = rounded
            add_sum(UB, rounded.astype(f32))

        part = pl.ds(s * rows, rows)
        waiting.append(pltpu.make_async_copy(n2_s.at[part], pg_out.at[part], out_sem.at[s, 12]))
        waiting[-1].start()
    for group in moves + late:
        for copy in group:
            copy.wait_send()
    for copy in waiting:
        copy.wait()


def forward_rows(
    s, part, length, rows, first_time, vec_ref, weights_in, halfway, scratch, outs, out_sem
):
    (x_s, wq_s, wk_s, wv_s, wo_s, w1_s, w2_s, q_s, k_s, v_s, att_s, n1_s, low_s, hid_s,
     slope_s, stat_s, y_s, aux_s, n2_s, z_s) = scratch
    start = s * rows
    out = [
        pltpu.make_async_copy(src.at[part], dst.at[part], out_sem.at[s, i])
        for i, (src, dst) in enumerate(
            zip(
                (x_s, q_s, k_s, v_s, att_s, n1_s, low_s, hid_s, slope_s, stat_s, y_s, aux_s), outs
            )
        )
    ]
    out[0].start()
    for i, (w, dst, bias) in enumerate(((wq_s, q_s, QB), (wk_s, k_s, None), (wv_s, v_s, VB))):
        if first_time:
            weights_in[i].wait()

        @pl.loop(0, WIDTH // 256)
        def _(j):
            cols = tile(j, 256)
            grid = dot(x_s[part, :], w[:, cols])
            if bias is not None:
                grid = grid + vec_ref[bias : bias + 1, cols]
            dst[part, cols] = grid.astype(bf16)

        out[1 + i].start()

    stat_s[part, :] = jnp.zeros((rows, 128), f32)
    lane = lax.broadcasted_iota(jnp.int32, (1, 128), 1)

    @pl.loop(0, HEADS // 2)
    def _(p):
        cols = tile(p, 128)
        mix, logs = attend_pair(q_s[part, cols], k_s[part, cols], v_s[part, cols], length, rows)
        att_s[part, cols] = mix.astype(bf16)
        aux = jnp.where((lane == 3) | (lane == 67), 1.0, jnp.zeros((rows, 128), f32))
        for which in (0, 1):
            for i, piece in enumerate(three_terms(-logs[which])):
                aux = jnp.where(lane == 64 * (1 - which) + i, piece, aux)
        aux_s[part, cols] = aux.astype(bf16)

    out[4].start()
    out[11].start()
    if halfway is not None:
        halfway()
    if first_time:
        weights_in[3].wait()

    @pl.loop(0, WIDTH // 256)
    def _(j):
        cols = tile(j, 256)
        z_s[:, cols] = (
            x_s[part, cols].astype(f32)
            + dot(att_s[part, :], wo_s[:, cols])
            + vec_ref[OB : OB + 1, cols]
        )

    @pl.loop(0, rows // 128)
    def _(i):
        r = tile(i, 128)
        q = pl.ds(pl.multiple_of(start + i * 128, 128), 128)
        normed, inv_root = norm_rows(z_s[r, :])
        n1_s[q, :] = normed.astype(bf16)
        first = normed * vec_ref[G1 : G1 + 1, :] + vec_ref[B1 : B1 + 1, :]
        low_s[q, :] = first.astype(bf16)
        z_s[r, :] = first + vec_ref[UB : UB + 1, :]
        stat_s[q, :] = jnp.where(lane == 12, inv_root, stat_s[q, :])

    out[5].start()
    out[6].start()
    if first_time:
        weights_in[4].wait()
        weights_in[5].wait()
    ft = 256

    @pl.loop(0, 4 * WIDTH // ft)
    def _(j):
        cols = tile(j, ft)
        u = dot(low_s[part, :], w1_s[:, cols]) + vec_ref[pl.ds(IB + j // 3, 1), tile(j % 3, ft)]
        h, slope = gelu_parts(u)
        hid_s[part, cols] = h.astype(bf16)
        slope_s[part, cols] = slope.astype(bf16)

    out[7].start()
    out[8].start()

    @pl.loop(0, WIDTH // 256)
    def _(j):
        cols = tile(j, 256)
        z_s[:, cols] += dot(hid_s[part, :], w2_s[:, cols])

    @pl.loop(0, rows // 128)
    def _(i):
        r = tile(i, 128)
        q = pl.ds(pl.multiple_of(start + i * 128, 128), 128)
        normed, inv_root = norm_rows(z_s[r, :])
        n2_s[q, :] = normed.astype(bf16)
        y_s[q, :] = (normed * vec_ref[G2 : G2 + 1, :] + vec_ref[B2 : B2 + 1, :]).astype(bf16)
        stat_s[q, :] = jnp.where(lane == 13, inv_root, stat_s[q, :])

    for i in (9, 10):
        out[i].start()
    return out


def forward(lengths, labels, states, cotangent, weights, small):
    count = lax.axis_size("seq")
    group, tokens, width = states.shape
    seqs = group // count
    one = count * tokens
    rows = seqs * one
    ff = 4 * width
    anywhere = pl.BlockSpec(memory_space=pl.ANY)
    in_vmem = pl.BlockSpec(memory_space=pltpu.VMEM)
    wide = ((rows, width), bf16)
    saved = [wide] * 6 + [((rows, ff), bf16)] * 2 + [((rows, 128), f32), wide, wide, wide]
    outs = [((VECS, width), f32), ((16, width), f32), ((16, 128), bf16), wide] + saved
    moves = 2 * seqs * (count - 1)
    flops = 2 * rows * width * (4 * width + 2 * ff) + 4 * rows * one * width
    dma = pltpu.SemaphoreType.DMA
    return pl.pallas_call(
        functools.partial(forward_kernel, seqs),
        out_shape=tuple(jax.ShapeDtypeStruct(s, t) for s, t in outs),
        in_specs=[pl.BlockSpec(memory_space=pltpu.SMEM)] * 2
        + [anywhere] * 9
        + [in_vmem] * len(small),
        out_specs=(in_vmem,) * 3 + (anywhere,) * (len(outs) - 3),
        scratch_shapes=[pltpu.VMEM((rows, width), bf16)]
        + [pltpu.VMEM(w.shape, bf16) for w in weights[:6]]
        + [pltpu.VMEM(s, t) for s, t in saved]
        + [
            pltpu.VMEM((one, width), f32), pltpu.VMEM((rows, width), bf16),
            pltpu.VMEM((width, width), bf16), pltpu.VMEM((16, 128), f32),
            dma((7,)), dma((seqs, 13)), dma((2 * seqs,)),
            dma((moves,)), dma((moves,)),
        ],
        compiler_params=pltpu.CompilerParams(
            collective_id=1, has_side_effects=True, vmem_limit_bytes=60 * 2**20
        ),
        cost_estimate=pl.CostEstimate(
            flops=flops, bytes_accessed=50 * 2**20, transcendentals=rows * (ff + 12 * one)
        ),
        name="forward",
    )(lengths, labels, states, cotangent, *weights, *small)


def place_of_block():
    return (lax.axis_index("batch") % 8) * 4 + lax.axis_index("seq")


def back_kernel(
    seqs, chunks, pattern, lags, len_ref, vec_ref, small_ref, head_ref,
    pg, hid, slope, low, n1, stat, y, q, k, v, att, x, aux,
    w1, w2, wq, wk, wv, wo,
    out_ref, small_out, head_out, lay_out, grad_out,
    wide, fg_s, stat_s, w1_s, w2_s,
    acc, staged, r0, r1, r2, r3, r4, sgot, own_s,
    in_sem, hid_sem, rs_send, rs_recv, ag_send, ag_recv, loc, sm_send, sm_recv, hd_send, hd_recv,
    tok_send, tok_recv, tok_own,
):
    rows = fg_s.shape[0]
    one = rows // seqs
    tokens = lay_out.shape[1]
    count = lax.axis_size("seq")
    b = lax.axis_index("batch")
    z = lax.axis_index("seq")
    core = b % 2

    got = [r0, r1, r2, r3, r4]
    res = r0
    near_b = [flipped(b, 2), flipped(b, 4), b, b]
    near_z = [z, z, flipped(z, 1), flipped(z, 2)]
    mine = [(b // 2) % 2, (b // 4) % 2, z % 2, (z // 2) % 2]
    orders = {"x": (0, 1, 2, 3), "y": (1, 0, 2, 3)}
    period = len(pattern)

    def direction(c, level):
        code = c % period
        dirs = [orders[p][level] for p in pattern]
        return (
            pick(code, [near_b[d] for d in dirs]),
            pick(code, [near_z[d] for d in dirs]),
            pick(code, [mine[d] for d in dirs]),
        )

    core_partner = (flipped(b, 1), z)
    barrier = pltpu.get_barrier_semaphore()
    partners = [(near_b[2], near_z[2]), (near_b[3], near_z[3]), core_partner]
    partners += [(near_b[0], near_z[0]), (near_b[1], near_z[1])]
    greeted = [core_partner, (near_b[0], near_z[0]), (near_b[1], near_z[1])] + greet_line()
    for who in greeted:
        pl.semaphore_signal(barrier, inc=1, device_id=who, device_id_type=MESH)

    def base(c, level):
        first = 0
        size = CHUNK
        for l in range(level):
            size = size // 2
            first = first + direction(c, l)[2] * size
        return pl.multiple_of(first, 16)

    slots = staged.shape[0]
    my_cols = pl.ds(pl.multiple_of(core * HALF, HALF), HALF)

    def rs_copy(c, s):
        if s == 0:
            return pltpu.make_async_remote_copy(
                staged.at[c % slots], r0.at[c], rs_send.at[0, c], rs_recv.at[0, c],
                device_id=core_partner, device_id_type=MESH,
            )
        size = CHUNK >> s
        nb, nz, m = direction(c, s - 1)
        start = pl.multiple_of(base(c, s - 1) + (1 - m) * size, 16)
        return pltpu.make_async_remote_copy(
            acc.at[c, pl.ds(start, size)], got[s].at[c], rs_send.at[s, c], rs_recv.at[s, c],
            device_id=(nb, nz), device_id_type=MESH,
        )

    def out_rows(c):
        return out_ref.at[pl.ds(pl.multiple_of(c * CHUNK, CHUNK), CHUNK), my_cols]

    def ag_copy(c, s):
        if s == 0:
            return pltpu.make_async_remote_copy(
                res.at[c], out_rows(c), ag_send.at[0, c], ag_recv.at[0, c],
                device_id=core_partner, device_id_type=MESH,
            )
        size = CHUNK >> s
        nb, nz, _ = direction(c, s - 1)
        start = base(c, s)
        return pltpu.make_async_remote_copy(
            res.at[c, pl.ds(start, size)], res.at[c, pl.ds(start, size)],
            ag_send.at[s, c], ag_recv.at[s, c], device_id=(nb, nz), device_id_type=MESH,
        )

    def loc_out(c):
        return pltpu.make_async_copy(res.at[c], out_rows(c), loc.at[c])

    def stage_scatter(s, c):
        rs_copy(c, s - 1).wait_recv()
        half = CHUNK >> s
        start = base(c, s - 1)
        m = direction(c, s - 1)[2]
        for which in (0, 1):
            off = pl.multiple_of(((1 - m) if which == 0 else m) * half, 16)
            part = pl.ds(pl.multiple_of(start + off, 16), half)
            acc[c, part] = acc[c, part] + got[s - 1][c, pl.ds(off, half)]
            if which == 0:
                rs_copy(c, s).start()

    def stage_turn(c):
        rs_copy(c, 4).wait_recv()
        part = pl.ds(base(c, 4), 16)
        res[c, part] = acc[c, part] + r4[c]
        ag_copy(c, 4).start()

    def stage_gather(s, c):
        ag_copy(c, s + 1).wait_recv()
        ag_copy(c, s).start()
        if s == 0:
            loc_out(c).start()

    def stage_last(c):
        ag_copy(c, 0).wait_recv()
        loc_out(c).wait()
        for s in range(1, 5):
            rs_copy(c, s).wait_send()
        for s in range(5):
            ag_copy(c, s).wait_send()

    stages = (
        [functools.partial(stage_scatter, s) for s in (1, 2, 3, 4)]
        + [stage_turn]
        + [functools.partial(stage_gather, s) for s in (3, 2, 1, 0)]
        + [stage_last]
    )

    piece = tokens // 4
    per_seq = 4 * (count - 1)

    def send_piece(src, dst, first_sem, number):
        s = number // per_seq
        part = (number // (count - 1)) % 4
        d = number % (count - 1)
        other = (z + d + 1) % count
        i = first_sem + s * (count - 1) + d
        start = pl.multiple_of((s * count + other) * tokens + part * piece, piece)
        pltpu.make_async_remote_copy(
            src.at[pl.ds(start, piece)],
            dst.at[z * seqs + s, pl.ds(pl.multiple_of(part * piece, piece), piece)],
            tok_send.at[i], tok_recv.at[i], device_id=(b, other), device_id_type=MESH,
        ).start()

    def tick(t):
        @pl.when(t < seqs * per_seq)
        def _():
            send_piece(y, lay_out, 0, t)

        @pl.when((t >= 22) & (t < 22 + seqs * per_seq))
        def _():
            send_piece(wide.at[3], grad_out, seqs * (count - 1), t - 22)

        for stage, lag in reversed(list(zip(stages, lags))):
            c = t - lag

            @pl.when((c >= 0) & (c < chunks))
            def _():
                stage(c)

    def give(c, left, right, fresh=False):
        grad = dot(left, right, TN).astype(bf16)
        first = grad[:, 0:HALF]
        second = grad[:, HALF:]

        @pl.when(c >= slots)
        def _():
            rs_copy(c - slots, 0).wait_send()

        staged[c % slots] = jnp.where(core == 0, second, first)
        acc[c] = jnp.where(core == 0, first, second)
        rs_copy(c, 0).start()

    (low_s, n1_s, pg_s, eg_s) = [wide.at[i] for i in range(2, 6)]
    ag_s = wide.at[10]

    def chunk_load(j):
        cols = pl.ds(pl.multiple_of(j * WIDTH, WIDTH), WIDTH)
        return (
            pltpu.make_async_copy(hid.at[:, cols], wide.at[6 + j % 2], hid_sem.at[0, j]),
            pltpu.make_async_copy(slope.at[:, cols], wide.at[8 + j % 2], hid_sem.at[1, j]),
        )

    pg_load, low_load, n1_load, stat_load = copies(
        [(pg, pg_s), (low, low_s), (n1, n1_s), (stat, stat_s)], in_sem
    )

    def weight_load(j):
        part = pl.ds(pl.multiple_of(j * WIDTH, WIDTH), WIDTH)
        return (
            pltpu.make_async_copy(w2.at[part], w2_s.at[part], hid_sem.at[2, j]),
            pltpu.make_async_copy(w1.at[:, part], w1_s.at[:, part], hid_sem.at[3, j]),
        )

    pg_load.start()
    for copy in chunk_load(0) + weight_load(0)[:1] + (low_load,) + weight_load(0)[1:]:
        copy.start()
    own_in = [
        pltpu.make_async_copy(
            y.at[pl.ds(pl.multiple_of(s * one + z * tokens, tokens), tokens)],
            own_s.at[s], tok_own.at[s],
        )
        for s in range(seqs)
    ]
    own_y = [
        pltpu.make_async_copy(own_s.at[s], lay_out.at[z * seqs + s], tok_own.at[2 * seqs + s])
        for s in range(seqs)
    ]
    for copy in own_in:
        copy.start()
    later = copies(
        [(q, wide.at[0]), (k, wide.at[1]), (aux, wide.at[11])], in_sem.at[pl.ds(7, 3)]
    )
    middle = copies([(v, wide.at[6]), (att, wide.at[8])], in_sem.at[pl.ds(10, 2)])
    (x_load,) = copies([(x, wide.at[7])], in_sem.at[pl.ds(12, 1)])
    attn_weights = [
        pltpu.make_async_copy(w, w2_s.at[pl.ds(i * WIDTH, WIDTH)], in_sem.at[13 + i])
        for i, w in enumerate((wo, wq, wk, wv))
    ]
    block = place_of_block()
    head_out[block] = head_ref[...]
    small_out[...] = small_ref[...]
    y_moves = []
    for s in range(seqs):
        y_moves += spread(y, lay_out, seqs, tokens, False, tok_send, tok_recv, 0, s)
    pl.semaphore_wait(barrier, len(greeted))
    ROW = 128

    def add_sum(index, values):
        small_out[index : index + 1, :] += jnp.sum(values, axis=0, keepdims=True)

    pg_load.wait()

    @pl.loop(0, 4)
    def _(j):
        chunk_load(j)[0].wait()

        @pl.loop(0, 3)
        def _(t):
            give(6 * j + t, wide[6 + j % 2, :, tile(t, 256)], pg_s[...])

            @pl.when(j < 2)
            def _():
                tick(6 * j + t)

        chunk_load(j)[1].wait()
        weight_load(j)[0].wait()

        @pl.when(j < 3)
        def _():
            for copy in chunk_load(j + 1) + weight_load(j + 1):
                copy.start()

        @pl.when(j == 0)
        def _():
            for before, after in zip(own_in, own_y):
                before.wait()
                after.start()
            fg_s[...] = pg_s[...].astype(f32)

        @pl.when(j == 1)
        def _():
            for copy in (n1_load, stat_load):
                copy.start()

        @pl.when(j == 2)
        def _():
            for copy in later:
                copy.start()

        @pl.when(j == 3)
        def _():
            for copy in middle:
                copy.start()

        @pl.loop(0, WIDTH // 256)
        def _(t):
            cols = tile(t, 256)
            ff = pl.ds(pl.multiple_of(j * WIDTH + t * 256, 256), 256)
            grad = dot(pg_s[...], w2_s[ff, :], NT) * wide[8 + j % 2, :, cols].astype(f32)
            rounded = grad.astype(bf16)
            eg_s[:, cols] = rounded
            small_out[pl.ds(IB + j, 1), cols] = jnp.sum(
                rounded.astype(f32), axis=0, keepdims=True
            )

        for i in range(4):

            @pl.when(j == i)
            def _():
                attn_weights[i].start()

        @pl.when(j == 0)
        def _():
            low_load.wait()

        @pl.loop(0, 3)
        def _(t):
            give(6 * j + 3 + t, low_s[:, tile(t, 256)], eg_s[...])

            @pl.when(j < 2)
            def _():
                tick(6 * j + 3 + t)

        @pl.when(j >= 2)
        def _():
            tick(8 + 2 * j)

        weight_load(j)[1].wait()
        ff_cols = pl.ds(pl.multiple_of(j * WIDTH, WIDTH), WIDTH)

        @pl.loop(0, WIDTH // 256)
        def _(t):
            cols = tile(t, 256)
            fg_s[:, cols] += dot(eg_s[...], w1_s[cols, ff_cols], NT)

        @pl.when(j >= 2)
        def _():
            tick(9 + 2 * j)

    x_load.start()
    n1_load.wait()
    stat_load.wait()

    @pl.loop(0, rows // ROW)
    def _(i):
        r = tile(i, ROW)
        upstream = fg_s[r, :]
        normed = n1_s[r, :].astype(f32)
        add_sum(G1, upstream * normed)
        add_sum(B1, upstream)
        zg = norm_rows_back(upstream, normed, stat_s[r, 12:13], vec_ref[G1 : G1 + 1, :])
        rounded = zg.astype(bf16)
        ag_s[r, :] = rounded
        add_sum(OB, rounded.astype(f32))

    tick(16)

    (q_s, k_s, dv_s, sg_s, dq_s, dk_s, v_s, x_s, att_s, dat_s) = [wide.at[i] for i in range(10)]
    wo_s, wq_s, wk_s, wv_s = [w2_s.at[pl.ds(i * WIDTH, WIDTH)] for i in range(4)]
    attn_weights[0].wait()

    @pl.loop(0, WIDTH // 256)
    def _(t):
        cols = tile(t, 256)
        dat_s[:, cols] = dot(ag_s[...], wo_s[cols, :], NT).astype(bf16)

    for copy in middle + later:
        copy.wait()

    @pl.loop(0, 3)
    def _(t):
        give(24 + t, att_s[:, tile(t, 256)], ag_s[...])

    tick(17)
    aux_s = wide.at[11]
    for copy in attn_weights[1:]:
        copy.wait()
    x_load.wait()
    lane = lax.broadcasted_iota(jnp.int32, (1, 128), 1)

    def move(s, ordered):
        return spread(
            sg_s, grad_out, seqs, tokens, False, tok_send, tok_recv, seqs * (count - 1), s, ordered
        )

    own_sg = [
        own_part(sg_s, grad_out, seqs, tokens, False, tok_own.at[seqs + s], s) for s in range(seqs)
    ]

    @pl.loop(0, seqs)
    def _(s):
        part = pl.ds(pl.multiple_of(s * one, one), one)
        hidden = lax.broadcasted_iota(jnp.int32, (one, 1), 0) >= len_ref[z * seqs + s]
        ones = jnp.where((lane % 64) < 3, 1.0, jnp.zeros((one, 128), f32))
        key_aux = jnp.where((lane % 64 == 3) & hidden, masked_fill, ones).astype(bf16)
        value_aux = ones.astype(bf16)

        @pl.loop(0, 2)
        def _(i):
            for turn in range(3):
                cols = tile(3 * i + turn, 128)
                dq, dk, dv = attend_back_pair(
                    q_s[part, cols], k_s[part, cols], v_s[part, cols], dat_s[part, cols],
                    att_s[part, cols], aux_s[part, cols], key_aux, value_aux,
                )
                dq_s[part, cols] = dq.astype(bf16)
                dk_s[part, cols] = dk.astype(bf16)
                dv_s[part, cols] = dv.astype(bf16)
            tick(18 + 5 * s + 2 * i)
            tick(19 + 5 * s + 2 * i)

        @pl.loop(0, WIDTH // 256)
        def _(t):
            cols = tile(t, 256)
            total = ag_s[part, cols].astype(f32)
            for d, w in ((dq_s, wq_s), (dk_s, wk_s), (dv_s, wv_s)):
                total = total + dot(d[part, :], w[cols, :], NT)
            sg_s[part, cols] = total.astype(bf16)
            for index, d in ((QB, dq_s), (VB, dv_s)):
                small_out[index : index + 1, cols] += jnp.sum(
                    d[part, cols].astype(f32), axis=0, keepdims=True
                )

        for i in range(seqs):

            @pl.when(s == i)
            def _():
                own_sg[i].start()

        tick(22 + 5 * s)

    moves = []
    for s in range(seqs):
        moves += move(s, False)
    done = 18 + 5 * seqs
    for i, d in enumerate((dq_s, dk_s, dv_s)):

        @pl.loop(0, 3)
        def _(t):
            give(27 + 3 * i + t, x_s[:, tile(t, 256)], d[...])
            tick(done + 3 * i + t)

    done += 9


    def small_copies(i):
        first = block - block % (1 << i)
        part = pl.ds(first, 1 << i)
        return (
            pltpu.make_async_remote_copy(
                small_out, sgot.at[i], sm_send.at[i], sm_recv.at[i],
                device_id=partners[i], device_id_type=MESH,
            ),
            pltpu.make_async_remote_copy(
                head_out.at[part], head_out.at[part], hd_send.at[i], hd_recv.at[i],
                device_id=partners[i], device_id_type=MESH,
            ),
        )


    def late_tick(t, carry):
        for i in range(len(partners) + 1):

            @pl.when(t == done + 3 * i)
            def _():
                if i > 0:
                    for copy in small_copies(i - 1):
                        copy.wait()
                    small_out[...] = small_out[...] + sgot[i - 1]
                if i < len(partners):
                    for copy in small_copies(i):
                        copy.start()

        tick(t)
        return carry

    lax.fori_loop(done, chunks + lags[-1], late_tick, 0)
    for c in range(chunks - slots, chunks):
        rs_copy(c, 0).wait_send()
    for copy in own_sg + own_y + y_moves + moves:
        copy.wait()


def back(seqs, tokens, lengths, vecs, small, head, saved, weights):
    rows, width = saved[0].shape
    ff = 4 * width
    one = rows // seqs
    count = lax.axis_size("seq")
    chunks = 12 * width // CHUNK
    moves = 2 * seqs * (count - 1)
    dma = pltpu.SemaphoreType.DMA
    anywhere = pl.BlockSpec(memory_space=pl.ANY)
    in_vmem = pl.BlockSpec(memory_space=pltpu.VMEM)
    in_smem = pl.BlockSpec(memory_space=pltpu.SMEM)
    block = jax.ShapeDtypeStruct((seqs * count, tokens, width), bf16)
    half = functools.partial(pltpu.VMEM, dtype=bf16)
    total, small, head, lay, grad = pl.pallas_call(
        functools.partial(back_kernel, seqs, chunks, "xy", tuple(1 + 3 * i for i in range(10))),
        out_shape=(
            jax.ShapeDtypeStruct((12 * width, width), bf16),
            jax.ShapeDtypeStruct(small.shape, f32),
            jax.ShapeDtypeStruct((32,) + head.shape, bf16),
            block,
            block,
        ),
        in_specs=[in_smem, in_vmem, in_vmem, in_vmem] + [anywhere] * (len(saved) + len(weights)),
        out_specs=(anywhere, in_vmem, in_vmem, anywhere, anywhere),
        scratch_shapes=[
            pltpu.VMEM((12, rows, width), bf16), pltpu.VMEM((rows, width), f32),
            pltpu.VMEM((rows, 128), f32), pltpu.VMEM((width, ff), bf16),
            pltpu.VMEM((ff, width), bf16),
            pltpu.VMEM((chunks, CHUNK, HALF), bf16),
            pltpu.VMEM((6, CHUNK, HALF), bf16),
            pltpu.VMEM((chunks, CHUNK, HALF), bf16),
            pltpu.VMEM((chunks, CHUNK // 2, HALF), bf16),
            pltpu.VMEM((chunks, CHUNK // 4, HALF), bf16),
            pltpu.VMEM((chunks, CHUNK // 8, HALF), bf16),
            pltpu.VMEM((chunks, CHUNK // 16, HALF), bf16),
            pltpu.VMEM((5,) + small.shape, f32), pltpu.VMEM((seqs, tokens, width), bf16),
            dma((17,)), dma((4, 4)),
            dma((5, chunks)), dma((5, chunks)), dma((5, chunks)), dma((5, chunks)),
            dma((chunks,)), dma((5,)), dma((5,)), dma((5,)), dma((5,)),
            dma((moves,)), dma((moves,)), dma((3 * seqs,)),
        ],
        compiler_params=pltpu.CompilerParams(
            collective_id=0, has_side_effects=True, vmem_limit_bytes=62 * 2**20
        ),
        cost_estimate=pl.CostEstimate(
            flops=8 * rows * width * ff + 16 * rows * width * width + 10 * rows * one * width,
            bytes_accessed=100 * 2**20, transcendentals=12 * rows * one,
        ),
        name="back",
    )(lengths, vecs, small, head, *saved, *weights)
    blocks = lax.axis_size("batch") // 8
    if blocks > 1:
        alike = [[i + 8 * j for j in range(blocks)] for i in range(8)]
        total = lax.psum(total, "batch", axis_index_groups=alike)
        small = lax.psum(small, "batch", axis_index_groups=alike)
        head = lax.all_gather(head, "batch", axis_index_groups=alike, axis=0, tiled=True)
    return total.reshape(12, width, width), small, head, lay, grad


def finish_kernel(
    total, small_ref, cls_ref, label_ref, vec_ref, pool_ref, lay_in, grad_in,
    lay_out, loss_out, grad_out, gq, gk, gv, go, gqb, gvb, gob, gg1, gb1, gin, gib, gou, gub,
    gg2, gb2, gpool, gpb, gcp, gcb,
    low_s, full_s, pool_s, pass_s, in_sem, out_sem,
):
    units = low_s.shape[0]
    group = loss_out.shape[0]
    seqs = cls_ref.shape[0]
    loads = [pltpu.make_async_copy(total.at[u], low_s.at[u], in_sem.at[u]) for u in range(units)]
    for copy in loads:
        copy.start()
    places = []
    for j in range(4):
        part = pl.ds(j * WIDTH, WIDTH)
        places += [gou.at[part], gin.at[:, part]]
    places += [go, gq, gk, gv]
    stores = [
        pltpu.make_async_copy(full_s.at[u], places[u], out_sem.at[u]) for u in range(units)
    ]
    passed_in = [
        pltpu.make_async_copy(src, pass_s.at[i], in_sem.at[units + i])
        for i, src in enumerate((lay_in, grad_in))
    ]
    passed = [
        pltpu.make_async_copy(pass_s.at[i], dst, out_sem.at[units + i])
        for i, dst in enumerate((lay_out, grad_out))
    ]
    for copy in passed_in:
        copy.start()
    pool_store = pltpu.make_async_copy(pool_s, gpool, out_sem.at[units + 2])

    def widen(u):
        loads[u].wait()

        @pl.loop(0, WIDTH // 128)
        def _(i):
            r = tile(i, 128)
            full_s[u, r, :] = low_s[u, r, :].astype(f32)

        stores[u].start()

    for u in range(4):
        widen(u)
    for before, after in zip(passed_in, passed):
        before.wait()
        after.start()

    def exact(left, right, dims=NN):
        return lax.dot_general(left, right, dims, precision=highest, preferred_element_type=f32)

    pooled = jnp.tanh(dot(cls_ref[...], pool_ref[...]) + vec_ref[PB : PB + 1, :])
    row = lax.broadcasted_iota(jnp.int32, (8, 1), 0)
    class_rows = jnp.where(row < 3, vec_ref[CP : CP + 8, :], 0.0)
    picked = jnp.where(
        row == lax.broadcasted_iota(jnp.int32, (8, 128), 1), vec_ref[CB : CB + 1, 0:128], 0.0
    )
    logits = exact(class_rows, pooled, NT) + jnp.sum(picked, axis=-1, keepdims=True)
    logits = jnp.where(row < 3, logits, masked_fill)
    top = jnp.max(logits, axis=0, keepdims=True)
    raised = jnp.exp(logits - top)
    total_row = jnp.sum(raised, axis=0, keepdims=True)
    chosen = (row == label_ref[...]).astype(f32)
    losses = (top + jnp.log(total_row)) - jnp.sum(
        jnp.where(chosen > 0.0, logits, 0.0), axis=0, keepdims=True
    )
    logit_grad = raised / total_row - chosen
    first = lax.axis_index("batch") * group
    pickers = (
        lax.broadcasted_iota(jnp.int32, (seqs, 128), 0)
        == lax.broadcasted_iota(jnp.int32, (seqs, 128), 1) + first
    ).astype(f32)
    loss_out[...] = exact(losses, pickers)[0, 0:group]
    pre = exact(logit_grad, class_rows, TN) * (1.0 - pooled * pooled)
    ones = jnp.ones((1, seqs), f32)
    gcb[...] = exact(ones, logit_grad, NT)[0, 0:3]
    gpb[...] = jnp.sum(pre, axis=0)
    gcp[...] = exact(logit_grad, pooled)[0:3, :]
    high = pre.astype(bf16)
    rest = pre - high.astype(f32)
    mid = rest.astype(bf16)
    low = (rest - mid.astype(f32)).astype(bf16)
    for j in range(3):
        cols = pl.ds(j * 256, 256)
        cls = cls_ref[:, cols]
        pool_s[cols, :] = dot(cls, high, TN) + dot(cls, mid, TN) + dot(cls, low, TN)
    pool_store.start()
    for i, ref in (
        (QB, gqb), (VB, gvb), (OB, gob), (G1, gg1), (B1, gb1), (UB, gub), (G2, gg2), (B2, gb2),
    ):
        ref[...] = small_ref[i, :]
    for j in range(4):
        gib[j * WIDTH : (j + 1) * WIDTH] = small_ref[IB + j, :]
    for u in range(4, units):
        widen(u)
    for copy in stores + passed + [pool_store]:
        copy.wait()


def finish(total, small, cls, labels, vecs, pool, lay, grad):
    group, tokens, width = lay.shape
    anywhere = pl.BlockSpec(memory_space=pl.ANY)
    in_vmem = pl.BlockSpec(memory_space=pltpu.VMEM)
    square = ((width, width), f32, anywhere)
    row = ((width,), f32, in_vmem)
    outs = (
        [(lay.shape, bf16, anywhere), ((group,), f32, in_vmem), (grad.shape, bf16, anywhere)]
        + [square] * 4
        + [row] * 5
        + [((width, 4 * width), f32, anywhere), ((4 * width,), f32, in_vmem)]
        + [((4 * width, width), f32, anywhere), row, row, row]
        + [square, row, ((3, width), f32, in_vmem), ((3,), f32, in_vmem)]
    )
    units = total.shape[0]
    return pl.pallas_call(
        finish_kernel,
        out_shape=tuple(jax.ShapeDtypeStruct(s, t) for s, t, _ in outs),
        in_specs=[anywhere] + [in_vmem] * 5 + [anywhere, anywhere],
        out_specs=tuple(m for _, _, m in outs),
        scratch_shapes=[
            pltpu.VMEM((units, width, width), bf16), pltpu.VMEM((units, width, width), f32),
            pltpu.VMEM((width, width), f32), pltpu.VMEM((2,) + lay.shape, bf16),
            pltpu.SemaphoreType.DMA((units + 2,)), pltpu.SemaphoreType.DMA((units + 3,)),
        ],
        compiler_params=pltpu.CompilerParams(vmem_limit_bytes=60 * 2**20),
        name="finish",
    )(total, small, cls, labels, vecs, pool, lay, grad)


def local(
    states, lengths, labels, cotangent,
    query_proj, key_proj, value_proj, output_proj,
    query_bias, value_bias, output_bias, first_gain, first_bias,
    inner_proj, inner_bias, outer_proj, outer_bias, second_gain, second_bias,
    pool_proj, pool_bias, class_proj, class_bias,
):
    group, tokens, width = states.shape
    seqs = group // lax.axis_size("seq")
    vecs, small, head, x, q, k, v, att, n1, low, hid, slope, stat, y, aux, pg = forward(
        lengths, labels, states, cotangent,
        (query_proj, key_proj, value_proj, output_proj, inner_proj, outer_proj, pool_proj),
        (query_bias, value_bias, output_bias, first_gain, first_bias, inner_bias, outer_bias,
         second_gain, second_bias, pool_bias, class_proj.T, class_bias),
    )
    total, small, head, lay, grad = back(
        seqs, tokens, lengths, vecs, small, head,
        (pg, hid, slope, low, n1, stat, y, q, k, v, att, x, aux),
        (inner_proj, outer_proj, query_proj, key_proj, value_proj, output_proj),
    )
    cls = head[:, 0 : 6 * seqs].reshape(-1, width)
    label_row = head[:, 6 * seqs, 0:seqs].reshape(1, -1).astype(jnp.int32)
    out = finish(total, small, cls, label_row, vecs, pool_proj, lay, grad)
    return out[:20] + (out[20].T,) + out[21:]


def solution(mesh):
    split = P("batch", "seq", None)
    in_specs = (split, P("batch"), P("batch"), split) + (P(),) * 19
    out_specs = (split, P("batch"), split) + (P(),) * 19
    return jax.shard_map(local, mesh=mesh, in_specs=in_specs, out_specs=out_specs, check_vma=False)
```

time: 303 us -> 279 us (0.921)
  Pallas kernels: 296 us -> 275 us
  local copies, waits for them, and re-layouts: 5.55 us -> 2.34 us
    pallas_call x1, Pallas kernels: 201 us -> 176 us  [back(): pl.pallas_call(functools.partial(back_kernel, seqs, chunks, 'xy', tuple((...]
    pallas_call x1, Pallas kernels: 73.2 us -> 77.3 us  [forward(): pl.pallas_call(functools.partial(forward_kernel, seqs), out_shape=tuple((...]
where the time goes in v4:
time: 279 us
  Pallas kernels  275 us (99%)
    pallas_call x1, Pallas kernels, back(): pl.pallas_call(functools.partial(back_kernel, seqs, chunks, 'xy', tuple((...  176 us
    pallas_call x1, Pallas kernels, forward(): pl.pallas_call(functools.partial(forward_kernel, seqs), out_shape=tuple((...  77.3 us
    pallas_call x1, Pallas kernels, finish(): pl.pallas_call(finish_kernel, out_shape=tuple((jax.ShapeDtypeStruct(s, t)...  21 us

profile of v4, /device:TPU:1, one launch (start us, length us, event | category | flops | bytes accessed | tf_op | source)
XLA Modules:
  0.0 278.6 jit_solution(11950561759475919507)
XLA Ops:
  0.7 77.3 %forward.1 = (f32[24,768]{1,0:T(8,128)}, f32[16,768]{1,0:T(8,128)}, bf16[16,128]{1,0:T(8,128)(2,1)}, bf16[1024,768]{1,0:T(8,128)(2,1)}, bf16[1024,768]{1,0:T(8,1...) custom-call(s32[8]{0:T(128)} %len_ref.3, ...), custom_call_target="tpu_custom_call" | custom-call | flops 16106127360 | bytes 52428800 | tf_op jit(solution)/shard_map/forward/pallas_call | solution.py:467
  78.0 176.2 %back.1 = (bf16[9216,768]{1,0:T(8,128)(2,1)}, f32[16,768]{1,0:T(8,128)}, bf16[32,16,128]{2,1,0:T(8,128)(2,1)}, bf16[8,128,768]{2,1,0:T(8,128)(2,1)}, bf16[8,128,768]{2,1,0:T(8,128)(2,1)}) custom-call(s32[8]{0:T(128)} %len_ref.3, f32[24,768]{1,0:T(8,128)} %get-tuple-element.65.vec_ref, f32[16,768]{1,0:T(8,128)} %get-tuple-element.66.small_ref, ...), custom_call_target="tpu_custom_call" | custom-call | flops 33017561088 | bytes 104857600 | tf_op jit(solution)/shard_map/back/pallas_call | solution.py:973
  254.2 0.9 convert_reduce_fusion
  255.1 0.7 reshape.66.label_ref
  255.8 1.7 reshape.65.cls_ref
  257.5 21.0 %finish.1 = (bf16[8,128,768]{2,1,0:T(8,128)(2,1)}, f32[8]{0:T(128)}, bf16[8,128,768]{2,1,0:T(8,128)(2,1)}, f32[768,768]{1,0:T(8,128)}, f32[768,768]{1,0:T(8,128)...) custom-call(bf16[12,768,768]{2,1,0:T(8,128)(2,1)} %bitcast.4, ...), custom_call_target="tpu_custom_call" | custom-call | tf_op jit(solution)/shard_map/finish/pallas_call | solution.py:1133

commit v5 on v4

--- a/solution.py
+++ b/solution.py
@@ -247,7 +247,7 @@
 
     moves = [move(True, s, False) for s in range(seqs)]
     late = [move(False, s, False) for s in range(seqs)]
-    for copy in move(True, 0, True):
+    for copy in move(True, 0, False):
         copy.start()
     vec_ref[...] = jnp.zeros_like(vec_ref)
     for i, ref in (
@@ -264,7 +264,7 @@
 
     waiting = []
     def send_late(s):
-        for copy in move(False, s, True):
+        for copy in move(False, s, False):
             copy.start()
 
     for s in range(seqs):
@@ -273,7 +273,7 @@
         own[s].wait()
         if s == 0:
             for i in range(1, seqs):
-                for copy in move(True, i, True):
+                for copy in move(True, i, False):
                     copy.start()
         part = pl.ds(s * rows, rows)
         waiting += forward_rows(
@@ -642,9 +642,9 @@
         def _():
             send_piece(y, lay_out, 0, t)
 
-        @pl.when((t >= 22) & (t < 22 + seqs * per_seq))
+        @pl.when((t >= 23) & (t < 23 + seqs * per_seq))
         def _():
-            send_piece(wide.at[3], grad_out, seqs * (count - 1), t - 22)
+            send_piece(wide.at[3], grad_out, seqs * (count - 1), t - 23)
 
         for stage, lag in reversed(list(zip(stages, lags))):
             c = t - lag
@@ -799,7 +799,7 @@
 
         @pl.when(j >= 2)
         def _():
-            tick(8 + 2 * j)
+            tick(6 + 3 * j)
 
         weight_load(j)[1].wait()
         ff_cols = pl.ds(pl.multiple_of(j * WIDTH, WIDTH), WIDTH)
@@ -811,7 +811,8 @@
 
         @pl.when(j >= 2)
         def _():
-            tick(9 + 2 * j)
+            tick(7 + 3 * j)
+            tick(8 + 3 * j)
 
     x_load.start()
     n1_load.wait()
@@ -829,7 +830,7 @@
         ag_s[r, :] = rounded
         add_sum(OB, rounded.astype(f32))
 
-    tick(16)
+    tick(18)
 
     (q_s, k_s, dv_s, sg_s, dq_s, dk_s, v_s, x_s, att_s, dat_s) = [wide.at[i] for i in range(10)]
     wo_s, wq_s, wk_s, wv_s = [w2_s.at[pl.ds(i * WIDTH, WIDTH)] for i in range(4)]
@@ -847,7 +848,7 @@
     def _(t):
         give(24 + t, att_s[:, tile(t, 256)], ag_s[...])
 
-    tick(17)
+    tick(19)
     aux_s = wide.at[11]
     for copy in attn_weights[1:]:
         copy.wait()
@@ -882,8 +883,11 @@
                 dq_s[part, cols] = dq.astype(bf16)
                 dk_s[part, cols] = dk.astype(bf16)
                 dv_s[part, cols] = dv.astype(bf16)
-            tick(18 + 5 * s + 2 * i)
-            tick(19 + 5 * s + 2 * i)
+            tick(20 + 4 * s + 2 * i)
+
+            @pl.when(i == 0)
+            def _():
+                tick(21 + 4 * s)
 
         @pl.loop(0, WIDTH // 256)
         def _(t):
@@ -903,7 +907,7 @@
             def _():
                 own_sg[i].start()
 
-        tick(22 + 5 * s)
+        tick(23 + 4 * s)
 
     moves = []
     for s in range(seqs):
@@ -1017,24 +1021,25 @@
 
 
 def finish_kernel(
-    total, small_ref, cls_ref, label_ref, vec_ref, pool_ref, lay_in, grad_in,
+    seqs, total, small_ref, head_ref, vec_ref, pool_ref, lay_in, grad_in,
     lay_out, loss_out, grad_out, gq, gk, gv, go, gqb, gvb, gob, gg1, gb1, gin, gib, gou, gub,
     gg2, gb2, gpool, gpb, gcp, gcb,
-    low_s, full_s, pool_s, pass_s, in_sem, out_sem,
+    low_s, full_s, pool_s, pass_s, head_s, cls_s, in_sem, out_sem,
 ):
     units = low_s.shape[0]
     group = loss_out.shape[0]
-    seqs = cls_ref.shape[0]
+    places = head_ref.shape[0]
+    every = seqs * places
     loads = [pltpu.make_async_copy(total.at[u], low_s.at[u], in_sem.at[u]) for u in range(units)]
     for copy in loads:
         copy.start()
-    places = []
+    targets = []
     for j in range(4):
         part = pl.ds(j * WIDTH, WIDTH)
-        places += [gou.at[part], gin.at[:, part]]
-    places += [go, gq, gk, gv]
+        targets += [gou.at[part], gin.at[:, part]]
+    targets += [go, gq, gk, gv]
     stores = [
-        pltpu.make_async_copy(full_s.at[u], places[u], out_sem.at[u]) for u in range(units)
+        pltpu.make_async_copy(full_s.at[u], targets[u], out_sem.at[u]) for u in range(units)
     ]
     passed_in = [
         pltpu.make_async_copy(src, pass_s.at[i], in_sem.at[units + i])
@@ -1058,7 +1063,7 @@
 
         stores[u].start()
 
-    for u in range(4):
+    for u in range(units):
         widen(u)
     for before, after in zip(passed_in, passed):
         before.wait()
@@ -1067,7 +1072,18 @@
     def exact(left, right, dims=NN):
         return lax.dot_general(left, right, dims, precision=highest, preferred_element_type=f32)
 
-    pooled = jnp.tanh(dot(cls_ref[...], pool_ref[...]) + vec_ref[PB : PB + 1, :])
+    head_s[...] = head_ref[...].astype(f32)
+    eye = lax.broadcasted_iota(jnp.int32, (places, places), 0) == lax.broadcasted_iota(
+        jnp.int32, (places, places), 1
+    )
+    label_rows = []
+    for s in range(seqs):
+        for j in range(6):
+            cls_s[s * places : (s + 1) * places, j * 128 : (j + 1) * 128] = head_s[:, s * 6 + j, :]
+        column = head_s[:, 6 * seqs, s : s + 1]
+        label_rows.append(jnp.sum(jnp.where(eye, column, 0.0), axis=0, keepdims=True))
+    cls = cls_s[...].astype(bf16)
+    pooled = jnp.tanh(dot(cls, pool_ref[...]) + vec_ref[PB : PB + 1, :])
     row = lax.broadcasted_iota(jnp.int32, (8, 1), 0)
     class_rows = jnp.where(row < 3, vec_ref[CP : CP + 8, :], 0.0)
     picked = jnp.where(
@@ -1078,19 +1094,22 @@
     top = jnp.max(logits, axis=0, keepdims=True)
     raised = jnp.exp(logits - top)
     total_row = jnp.sum(raised, axis=0, keepdims=True)
-    chosen = (row == label_ref[...]).astype(f32)
+    chosen = jnp.concatenate(
+        [(row.astype(f32) == labels).astype(f32) for labels in label_rows], axis=-1
+    )
     losses = (top + jnp.log(total_row)) - jnp.sum(
         jnp.where(chosen > 0.0, logits, 0.0), axis=0, keepdims=True
     )
     logit_grad = raised / total_row - chosen
-    first = lax.axis_index("batch") * group
+    first = lax.axis_index("batch") * (group // seqs)
+    own = lax.broadcasted_iota(jnp.int32, (every, 128), 1)
     pickers = (
-        lax.broadcasted_iota(jnp.int32, (seqs, 128), 0)
-        == lax.broadcasted_iota(jnp.int32, (seqs, 128), 1) + first
+        lax.broadcasted_iota(jnp.int32, (every, 128), 0)
+        == (own % seqs) * places + first + own // seqs
     ).astype(f32)
     loss_out[...] = exact(losses, pickers)[0, 0:group]
     pre = exact(logit_grad, class_rows, TN) * (1.0 - pooled * pooled)
-    ones = jnp.ones((1, seqs), f32)
+    ones = jnp.ones((1, every), f32)
     gcb[...] = exact(ones, logit_grad, NT)[0, 0:3]
     gpb[...] = jnp.sum(pre, axis=0)
     gcp[...] = exact(logit_grad, pooled)[0:3, :]
@@ -1100,8 +1119,8 @@
     low = (rest - mid.astype(f32)).astype(bf16)
     for j in range(3):
         cols = pl.ds(j * 256, 256)
-        cls = cls_ref[:, cols]
-        pool_s[cols, :] = dot(cls, high, TN) + dot(cls, mid, TN) + dot(cls, low, TN)
+        part = cls_s[:, cols].astype(bf16)
+        pool_s[cols, :] = dot(part, high, TN) + dot(part, mid, TN) + dot(part, low, TN)
     pool_store.start()
     for i, ref in (
         (QB, gqb), (VB, gvb), (OB, gob), (G1, gg1), (B1, gb1), (UB, gub), (G2, gg2), (B2, gb2),
@@ -1109,13 +1128,11 @@
         ref[...] = small_ref[i, :]
     for j in range(4):
         gib[j * WIDTH : (j + 1) * WIDTH] = small_ref[IB + j, :]
-    for u in range(4, units):
-        widen(u)
     for copy in stores + passed + [pool_store]:
         copy.wait()
 
 
-def finish(total, small, cls, labels, vecs, pool, lay, grad):
+def finish(seqs, total, small, head, vecs, pool, lay, grad):
     group, tokens, width = lay.shape
     anywhere = pl.BlockSpec(memory_space=pl.ANY)
     in_vmem = pl.BlockSpec(memory_space=pltpu.VMEM)
@@ -1131,18 +1148,19 @@
     )
     units = total.shape[0]
     return pl.pallas_call(
-        finish_kernel,
+        functools.partial(finish_kernel, seqs),
         out_shape=tuple(jax.ShapeDtypeStruct(s, t) for s, t, _ in outs),
-        in_specs=[anywhere] + [in_vmem] * 5 + [anywhere, anywhere],
+        in_specs=[anywhere] + [in_vmem] * 4 + [anywhere, anywhere],
         out_specs=tuple(m for _, _, m in outs),
         scratch_shapes=[
             pltpu.VMEM((units, width, width), bf16), pltpu.VMEM((units, width, width), f32),
             pltpu.VMEM((width, width), f32), pltpu.VMEM((2,) + lay.shape, bf16),
+            pltpu.VMEM(head.shape, f32), pltpu.VMEM((seqs * head.shape[0], width), f32),
             pltpu.SemaphoreType.DMA((units + 2,)), pltpu.SemaphoreType.DMA((units + 3,)),
         ],
         compiler_params=pltpu.CompilerParams(vmem_limit_bytes=60 * 2**20),
         name="finish",
-    )(total, small, cls, labels, vecs, pool, lay, grad)
+    )(total, small, head, vecs, pool, lay, grad)
 
 
 def local(
@@ -1165,9 +1183,7 @@
         (pg, hid, slope, low, n1, stat, y, q, k, v, att, x, aux),
         (inner_proj, outer_proj, query_proj, key_proj, value_proj, output_proj),
     )
-    cls = head[:, 0 : 6 * seqs].reshape(-1, width)
-    label_row = head[:, 6 * seqs, 0:seqs].reshape(1, -1).astype(jnp.int32)
-    out = finish(total, small, cls, label_row, vecs, pool_proj, lay, grad)
+    out = finish(seqs, total, small, head, vecs, pool_proj, lay, grad)
     return out[:20] + (out[20].T,) + out[21:]
 
 

time: 279 us -> 266 us (0.953)
  Pallas kernels: 275 us -> 265 us
    pallas_call x1, Pallas kernels: 176 us -> 168 us  [back(): pl.pallas_call(functools.partial(back_kernel, seqs, chunks, 'xy', tuple((...]
where the time goes in v5:
time: 266 us
  Pallas kernels  265 us (100%)
    pallas_call x1, Pallas kernels, back(): pl.pallas_call(functools.partial(back_kernel, seqs, chunks, 'xy', tuple((...  168 us
    pallas_call x1, Pallas kernels, forward(): pl.pallas_call(functools.partial(forward_kernel, seqs), out_shape=tuple((...  77.4 us
    pallas_call x1, Pallas kernels, finish(): pl.pallas_call(functools.partial(finish_kernel, seqs), out_shape=tuple((j...  20.3 us

profile of v5, /device:TPU:1, one launch (start us, length us, event | category | flops | bytes accessed | tf_op | source)
XLA Modules:
  0.0 266.1 jit_solution(16094751249321346392)
XLA Ops:
  0.7 77.4 %forward.1 = (f32[24,768]{1,0:T(8,128)}, f32[16,768]{1,0:T(8,128)}, bf16[16,128]{1,0:T(8,128)(2,1)}, bf16[1024,768]{1,0:T(8,128)(2,1)}, bf16[1024,768]{1,0:T(8,1...) custom-call(s32[8]{0:T(128)} %len_ref.3, ...), custom_call_target="tpu_custom_call" | custom-call | flops 16106127360 | bytes 52428800 | tf_op jit(solution)/shard_map/forward/pallas_call | solution.py:467
  78.0 167.5 %back.1 = (bf16[9216,768]{1,0:T(8,128)(2,1)}, f32[16,768]{1,0:T(8,128)}, bf16[32,16,128]{2,1,0:T(8,128)(2,1)}, bf16[8,128,768]{2,1,0:T(8,128)(2,1)}, bf16[8,128,768]{2,1,0:T(8,128)(2,1)}) custom-call(s32[8]{0:T(128)} %len_ref.3, f32[24,768]{1,0:T(8,128)} %get-tuple-element.65.vec_ref, f32[16,768]{1,0:T(8,128)} %get-tuple-element.66.small_ref, ...), custom_call_target="tpu_custom_call" | custom-call | flops 33017561088 | bytes 104857600 | tf_op jit(solution)/shard_map/back/pallas_call | solution.py:977
  245.6 20.3 %finish.1 = (bf16[8,128,768]{2,1,0:T(8,128)(2,1)}, f32[8]{0:T(128)}, bf16[8,128,768]{2,1,0:T(8,128)(2,1)}, f32[768,768]{1,0:T(8,128)}, f32[768,768]{1,0:T(8,128)...) custom-call(bf16[12,768,768]{2,1,0:T(8,128)(2,1)} %bitcast.3, ...), custom_call_target="tpu_custom_call" | custom-call | tf_op jit(solution)/shard_map/finish/pallas_call | solution.py:1150

commit v6 on v5

--- a/solution.py
+++ b/solution.py
@@ -864,6 +864,23 @@
         own_part(sg_s, grad_out, seqs, tokens, False, tok_own.at[seqs + s], s) for s in range(seqs)
     ]
 
+    def states_rows(s):
+        part = pl.ds(pl.multiple_of(s * one, one), one)
+
+        @pl.loop(0, WIDTH // 256)
+        def _(t):
+            cols = tile(t, 256)
+            total = ag_s[part, cols].astype(f32)
+            for d, w in ((dq_s, wq_s), (dk_s, wk_s), (dv_s, wv_s)):
+                total = total + dot(d[part, :], w[cols, :], NT)
+            sg_s[part, cols] = total.astype(bf16)
+            for index, d in ((QB, dq_s), (VB, dv_s)):
+                small_out[index : index + 1, cols] += jnp.sum(
+                    d[part, cols].astype(f32), axis=0, keepdims=True
+                )
+
+        own_sg[s].start()
+
     @pl.loop(0, seqs)
     def _(s):
         part = pl.ds(pl.multiple_of(s * one, one), one)
@@ -889,23 +906,9 @@
             def _():
                 tick(21 + 4 * s)
 
-        @pl.loop(0, WIDTH // 256)
-        def _(t):
-            cols = tile(t, 256)
-            total = ag_s[part, cols].astype(f32)
-            for d, w in ((dq_s, wq_s), (dk_s, wk_s), (dv_s, wv_s)):
-                total = total + dot(d[part, :], w[cols, :], NT)
-            sg_s[part, cols] = total.astype(bf16)
-            for index, d in ((QB, dq_s), (VB, dv_s)):
-                small_out[index : index + 1, cols] += jnp.sum(
-                    d[part, cols].astype(f32), axis=0, keepdims=True
-                )
-
-        for i in range(seqs):
-
-            @pl.when(s == i)
-            def _():
-                own_sg[i].start()
+        @pl.when(s == 0)
+        def _():
+            states_rows(0)
 
         tick(23 + 4 * s)
 
@@ -919,6 +922,10 @@
         def _(t):
             give(27 + 3 * i + t, x_s[:, tile(t, 256)], d[...])
             tick(done + 3 * i + t)
+
+        if i == 1:
+            for s in range(1, seqs):
+                states_rows(s)
 
     done += 9
 

time: 266 us -> 266 us (level)
  no operation moved by 1% of the time
where the time goes in v6:
time: 266 us
  Pallas kernels  265 us (100%)
    pallas_call x1, Pallas kernels, back(): pl.pallas_call(functools.partial(back_kernel, seqs, chunks, 'xy', tuple((...  167 us
    pallas_call x1, Pallas kernels, forward(): pl.pallas_call(functools.partial(forward_kernel, seqs), out_shape=tuple((...  77.4 us
    pallas_call x1, Pallas kernels, finish(): pl.pallas_call(functools.partial(finish_kernel, seqs), out_shape=tuple((j...  20.3 us

profile of v6, /device:TPU:1, one launch (start us, length us, event | category | flops | bytes accessed | tf_op | source)
XLA Modules:
  0.0 266.0 jit_solution(12473496562413807238)
XLA Ops:
  0.7 77.4 %forward.1 = (f32[24,768]{1,0:T(8,128)}, f32[16,768]{1,0:T(8,128)}, bf16[16,128]{1,0:T(8,128)(2,1)}, bf16[1024,768]{1,0:T(8,128)(2,1)}, bf16[1024,768]{1,0:T(8,1...) custom-call(s32[8]{0:T(128)} %len_ref.3, ...), custom_call_target="tpu_custom_call" | custom-call | flops 16106127360 | bytes 52428800 | tf_op jit(solution)/shard_map/forward/pallas_call | solution.py:467
  78.0 167.5 %back.1 = (bf16[9216,768]{1,0:T(8,128)(2,1)}, f32[16,768]{1,0:T(8,128)}, bf16[32,16,128]{2,1,0:T(8,128)(2,1)}, bf16[8,128,768]{2,1,0:T(8,128)(2,1)}, bf16[8,128,768]{2,1,0:T(8,128)(2,1)}) custom-call(s32[8]{0:T(128)} %len_ref.3, f32[24,768]{1,0:T(8,128)} %get-tuple-element.65.vec_ref, f32[16,768]{1,0:T(8,128)} %get-tuple-element.66.small_ref, ...), custom_call_target="tpu_custom_call" | custom-call | flops 33017561088 | bytes 104857600 | tf_op jit(solution)/shard_map/back/pallas_call | solution.py:984
  245.5 20.3 %finish.1 = (bf16[8,128,768]{2,1,0:T(8,128)(2,1)}, f32[8]{0:T(128)}, bf16[8,128,768]{2,1,0:T(8,128)(2,1)}, f32[768,768]{1,0:T(8,128)}, f32[768,768]{1,0:T(8,128)...) custom-call(bf16[12,768,768]{2,1,0:T(8,128)(2,1)} %bitcast.3, ...), custom_call_target="tpu_custom_call" | custom-call | tf_op jit(solution)/shard_map/finish/pallas_call | solution.py:1157
